TPU v7x, 128 devices: a whole 4x4x4 slice. The times are simulated.
128 devices in a mesh: rep: 4 (over y_hi, core), exp: 32 (over x, y_lo, z).
Axes of the slice: x: 4, y: 4 (y_hi: 2, y_lo: 2; y = y_hi * 2 + y_lo), z: 4, core: 2. Of those that a mesh axis runs over, the one named last changes fastest.
Arguments:
- patches: bfloat16 [2, 32, 576, 768], P(None, 'exp', 'rep'), may hold values from -6 to 6
- expert_ids: int32 [2, 32, 576, 2], P(None, 'exp', 'rep'), may hold values from 0 to 31, all different within a row; in each aligned block of 144 rows (0 to 143, 144 to 287, ..., all dimensions but the last counted through in order) at most 10 rows name the same one
- labels: int32 [2, 32, 64], replicated, may hold values from -1 to 21887, as said below
- label_count: int32 [2, 32], replicated, may hold values from 0 to 64, as said below
- square_weights: float32 [5, 768, 768], P(None, ('rep', 'exp')), may hold values from -0.72168784 to 0.72168784
- router_weight: float32 [768, 32], P(('rep', 'exp')), may hold values from -0.15625 to 0.15625
- position_table: float32 [576, 768], P(None, ('rep', 'exp')), may hold values from -3 to 3
- head_weight: float32 [768, 21888], P(None, ('rep', 'exp')), may hold values from -0.7577722 to 0.7577722
- expert_weights: float32 [32, 2, 768, 3072], P('exp', None, None, 'rep'), may hold values from -1.4433757 to 1.4433757
- vector_params: float32 [10, 768], P(None, ('rep', 'exp')), may hold values from -1.6 to 1.6
- square_rows: float32 [5, 768], P(None, ('rep', 'exp')), may hold values from 1.4128508e-09 to 5.6514033e-09
- square_cols: float32 [5, 768], replicated, may hold values from 1.4128508e-09 to 5.6514033e-09
- router_rows: float32 [768], P(('rep', 'exp')), may hold values from 1.0624638e-07 to 4.2950666e-07
- router_cols: float32 [32], replicated, may hold values from 1.0624638e-07 to 4.2950666e-07
- position_rows: float32 [576], replicated, may hold values from 2.452866e-12 to 9.811464e-12
- position_cols: float32 [768], P(('rep', 'exp')), may hold values from 2.452866e-12 to 9.811464e-12
- head_rows: float32 [768], replicated, may hold values from 9.2801994e-10 to 3.7180286e-09
- head_cols: float32 [21888], P(('rep', 'exp')), may hold values from 9.2801994e-10 to 3.7180286e-09
- expert_rows: float32 [32, 2, 768], P('exp'), may hold values from 3.1044086e-14 to 5.5189486e-12
- expert_cols: float32 [32, 2, 3072], P('exp', None, 'rep'), may hold values from 3.1044086e-14 to 5.5189486e-12
- vector_moment: float32 [10, 768], P(None, ('rep', 'exp')), may hold values from 1.4128508e-09 to 5.6514033e-09
Outputs:
- loss_sum: float32 [], replicated
- image_count: float32 [], replicated
- grad_norm: float32 [], replicated
- square_clipped: float32 [5, 768, 768], P(None, ('rep', 'exp'))
- square_rows_next: float32 [5, 768], P(None, ('rep', 'exp'))
- square_cols_next: float32 [5, 768], replicated
- square_weights_next: float32 [5, 768, 768], P(None, ('rep', 'exp'))
- router_clipped: float32 [768, 32], P(('rep', 'exp'))
- router_rows_next: float32 [768], P(('rep', 'exp'))
- router_cols_next: float32 [32], replicated
- router_weight_next: float32 [768, 32], P(('rep', 'exp'))
- position_clipped: float32 [576, 768], P(None, ('rep', 'exp'))
- position_rows_next: float32 [576], replicated
- position_cols_next: float32 [768], P(('rep', 'exp'))
- position_table_next: float32 [576, 768], P(None, ('rep', 'exp'))
- head_clipped: float32 [768, 21888], P(None, ('rep', 'exp'))
- head_rows_next: float32 [768], replicated
- head_cols_next: float32 [21888], P(('rep', 'exp'))
- head_weight_next: float32 [768, 21888], P(None, ('rep', 'exp'))
- expert_clipped: float32 [32, 2, 768, 3072], P('exp', None, None, 'rep')
- expert_rows_next: float32 [32, 2, 768], P('exp')
- expert_cols_next: float32 [32, 2, 3072], P('exp', None, 'rep')
- expert_weights_next: float32 [32, 2, 768, 3072], P('exp', None, None, 'rep')
- vector_clipped: float32 [10, 768], P(None, ('rep', 'exp'))
- vector_moment_next: float32 [10, 768], P(None, ('rep', 'exp'))
- vector_params_next: float32 [10, 768], P(None, ('rep', 'exp'))
Inputs may be any that keep to these rules, and one draw needn't show every extreme that they name: `expert_ids`: each row names 2 different experts; within each device's aligned block of 144 rows no expert is named more than 10 times, a bound that some block reaches. `labels`: the first label_count entries of an image are distinct classes; the rest are -1. `label_count`: an image with 0 labels is padding: it adds nothing to the loss or to image_count.
All inputs are finite; a program needn't handle non-finite values.
Results may differ from a plain program's by a relative error of at most 0.003.
The roundings to bfloat16 on the way count: a program that leaves them out, or rounds other values in their place, can miss the bound.
Values may be sent and summed in bfloat16 or wider, within the bound.
A program may use at most 192 MiB of HBM per device.

v0:
```python
import math

import jax
import jax.numpy as jnp
from jax import lax
from jax.sharding import PartitionSpec as P

D = 768
HEAD = 64
FF = 3072
PATCHES = 576


DECAY = 0.8
EPS_SQ = 1e-30
CLIP_NORM = 0.25


def layer_norm(value, gain, shift):
    centred = value - jnp.mean(value, axis=-1, keepdims=True)
    spread = jnp.mean(centred * centred, axis=-1, keepdims=True)
    return centred * lax.rsqrt(spread + 1e-06) * gain + shift


def plain_dot(left, right):
    return jnp.dot(left, right, preferred_element_type=jnp.float32)


def over_rows(left, right):
    return lax.dot_general(
        left, right, (((0,), (0,)), ((), ())), preferred_element_type=jnp.float32
    )


def over_last(left, right):
    return lax.dot_general(
        left, right, (((1,), (1,)), ((), ())), preferred_element_type=jnp.float32
    )


def factored_step(weight, clipped, rows_next, cols_next, rows_mean, rate):
    estimate = rows_next[..., :, None] * cols_next[..., None, :] / rows_mean
    return weight - rate * clipped * lax.rsqrt(estimate)


def reduce_experts(value):
    return lax.psum_scatter(value, "rep", scatter_dimension=2, tiled=True)


def shards(
    patches,
    expert_ids,
    labels,
    label_count,
    square_weights,
    router_weight,
    position_table,
    head_weight,
    expert_weights,
    vector_params,
    square_rows,
    square_cols,
    router_rows,
    router_cols,
    position_rows,
    position_cols,
    head_rows,
    head_cols,
    expert_rows,
    expert_cols,
    vector_moment,
):
    bfloat = jnp.bfloat16
    num_rep = lax.axis_size("rep")
    num_exp = lax.axis_size("exp")
    rep_index = lax.axis_index("rep")
    my_image = lax.axis_index("exp")
    device_index = lax.axis_index(("rep", "exp"))
    squares, router = (
        lax.all_gather(square_weights.astype(bfloat), ("rep", "exp"), axis=1, tiled=True),
        lax.all_gather(router_weight.astype(bfloat), ("rep", "exp"), axis=0, tiled=True),
    )
    table, vectors = (
        lax.all_gather(position_table, ("rep", "exp"), axis=1, tiled=True),
        lax.all_gather(vector_params, ("rep", "exp"), axis=1, tiled=True),
    )
    experts = lax.all_gather(expert_weights.astype(bfloat), "rep", axis=3, tiled=True)[0]
    w_in = experts[0]
    w_out = experts[1]
    micro_total, _, rows, width = patches.shape
    num_top = expert_ids.shape[3]
    num_expert = router.shape[1]
    vocab_dev = head_weight.shape[1]
    ff_dev = expert_weights.shape[3]
    capacity = max(2, (21 * rows * num_top + 20 * num_expert - 1) // (20 * num_expert))
    heads = width // HEAD
    scale = HEAD ** (-0.5)
    table_rows = lax.dynamic_slice_in_dim(table, rep_index * rows, rows, 0)
    head_low = head_weight.astype(bfloat)
    valid = (label_count > 0).astype(jnp.float32)
    image_count = jnp.sum(valid)
    columns = device_index * vocab_dev + jnp.arange(vocab_dev, dtype=jnp.int32)
    slot_range = jnp.arange(num_expert * capacity, dtype=jnp.int32)
    expert_range = jnp.arange(num_expert, dtype=jnp.int32)
    label_range = jnp.arange(labels.shape[2], dtype=jnp.int32)

    def expert_forward(received):
        shaped = received.shape
        flat = received.reshape(-1, width)
        pre_act = plain_dot(flat, w_in)
        act = jax.nn.gelu(pre_act).astype(bfloat)
        result = over_last(act, w_out).astype(bfloat).reshape(shaped)
        back = lax.all_to_all(result, "exp", split_axis=0, concat_axis=0, tiled=True)
        return (
            back,
            received,
            pre_act.reshape(shaped[0], shaped[1], -1),
            act.reshape(shaped[0], shaped[1], -1),
        )

    def micro_pass(micro):
        patch_rows = lax.dynamic_index_in_dim(patches, micro, 0, keepdims=False)[0]
        ids = lax.dynamic_index_in_dim(expert_ids, micro, 0, keepdims=False)[0]
        embed = plain_dot(patch_rows, squares[0]) + vectors[0] + table_rows
        norm_one, pull_one = jax.vjp(layer_norm, embed, vectors[1], vectors[2])
        hidden_one = norm_one.astype(bfloat)
        projected = jnp.einsum(
            "rd,kde->rke", hidden_one, squares[1:4], preferred_element_type=jnp.float32
        )
        query = (projected[:, 0] + vectors[3]).astype(bfloat)
        key_rows = projected[:, 1].astype(bfloat)
        value_rows = (projected[:, 2] + vectors[4]).astype(bfloat)
        key_all, value_all = (
            lax.all_gather(key_rows, "rep", axis=0, tiled=True),
            lax.all_gather(value_rows, "rep", axis=0, tiled=True),
        )
        query_h = query.reshape(rows, heads, HEAD)
        key_h = key_all.reshape(-1, heads, HEAD)
        value_h = value_all.reshape(-1, heads, HEAD)
        scores = (
            jnp.einsum("qhd,khd->hqk", query_h, key_h, preferred_element_type=jnp.float32) * scale
        )
        probs = jax.nn.softmax(scores, axis=-1)
        probs_low = probs.astype(bfloat)
        mixed = jnp.einsum("hqk,khd->qhd", probs_low, value_h, preferred_element_type=jnp.float32)
        mixed = mixed.reshape(rows, width).astype(bfloat)
        after_attn = embed + plain_dot(mixed, squares[4]) + vectors[5]
        norm_two, pull_two = jax.vjp(layer_norm, after_attn, vectors[6], vectors[7])
        hidden_two = norm_two.astype(bfloat)
        gate_probs = jax.nn.softmax(plain_dot(hidden_two, router), axis=-1)
        chosen = ids[:, :, None] == expert_range[None, None, :]
        chosen_float = chosen.astype(jnp.float32)
        gates = jnp.sum(gate_probs[:, None, :] * chosen_float, axis=-1)
        flat_hit = chosen.reshape(rows * num_top, num_expert).astype(jnp.int32)
        before = jnp.cumsum(flat_hit, axis=0) - flat_hit
        slot = jnp.sum(before * flat_hit, axis=1)
        target = ids.reshape(-1) * capacity + slot
        placing = (target[:, None] == slot_range[None, :]).astype(bfloat)
        copies = jnp.repeat(hidden_two, num_top, axis=0)
        outgoing = over_rows(placing, copies).astype(bfloat).reshape(num_expert, capacity, width)
        returned, received, pre_act, act = expert_forward(
            lax.all_to_all(outgoing, "exp", split_axis=0, concat_axis=0, tiled=True)
        )
        gathered = plain_dot(placing, returned.reshape(-1, width)).reshape(rows, num_top, width)
        after_moe = after_attn + jnp.sum(gates[:, :, None] * gathered, axis=1)
        norm_final, pull_final = jax.vjp(layer_norm, after_moe, vectors[8], vectors[9])
        partial_pool = jnp.sum(norm_final, axis=0) / PATCHES
        all_parts = lax.all_gather(partial_pool[None, :], ("rep", "exp"), axis=0, tiled=True)
        pooled = jnp.sum(all_parts.reshape(num_rep, num_exp, width), axis=0).astype(bfloat)
        logits = plain_dot(pooled, head_low)
        label_rows = lax.dynamic_index_in_dim(labels, micro, 0, keepdims=False)
        count_rows = lax.dynamic_index_in_dim(label_count, micro, 0, keepdims=False)
        live = label_range[None, :] < count_rows[:, None]
        targets = jnp.any(
            (label_rows[:, :, None] == columns[None, None, :]) & live[:, :, None], axis=1
        ).astype(jnp.float32)
        valid_rows = lax.dynamic_index_in_dim(valid, micro, 0, keepdims=False)
        loss_part = jnp.sum(valid_rows[:, None] * (jax.nn.softplus(logits) - targets * logits))
        dlogits = (valid_rows[:, None] * (jax.nn.sigmoid(logits) - targets) / image_count).astype(
            bfloat
        )
        head_grad = over_rows(pooled, dlogits)
        pool_grad = lax.psum(over_last(dlogits, head_low), ("rep", "exp"))
        my_grad = lax.dynamic_index_in_dim(pool_grad, my_image, 0, keepdims=False) / PATCHES
        dmoe_in, dgain_final, dshift_final = pull_final(jnp.broadcast_to(my_grad, (rows, width)))
        dout_rows = (
            (gates[:, :, None] * dmoe_in[:, None, :]).astype(bfloat).reshape(rows * num_top, width)
        )
        dgates = jnp.sum(dmoe_in[:, None, :] * gathered, axis=-1)
        dsend = over_rows(placing, dout_rows).astype(bfloat).reshape(num_expert, capacity, width)
        dreceived = lax.all_to_all(dsend, "exp", split_axis=0, concat_axis=0, tiled=True)
        dreceived = dreceived.reshape(-1, width)
        pre_flat = pre_act.reshape(-1, pre_act.shape[2])
        act_flat = act.reshape(-1, act.shape[2])
        dact = plain_dot(dreceived, w_out)
        gelu_pull = jax.vjp(jax.nn.gelu, pre_flat)[1]
        dpre = gelu_pull(dact)[0].astype(bfloat)
        dw_in = over_rows(received.reshape(-1, width), dpre)
        dw_out = over_rows(dreceived, act_flat)
        dback_part = over_last(dpre, w_in)
        dback = dback_part.astype(bfloat).reshape(num_expert, capacity, width)
        dreturn = lax.all_to_all(dback, "exp", split_axis=0, concat_axis=0, tiled=True)
        dcopies = plain_dot(placing, dreturn.reshape(-1, width)).reshape(rows, num_top, width)
        dprobs = jnp.sum(dgates[:, :, None] * chosen_float, axis=1)
        dgate_logits = (
            gate_probs * (dprobs - jnp.sum(gate_probs * dprobs, axis=-1, keepdims=True))
        ).astype(bfloat)
        router_grad = over_rows(hidden_two, dgate_logits)
        dhidden_two = over_last(dgate_logits, router) + jnp.sum(dcopies, axis=1)
        dnorm_two, dgain_two, dshift_two = pull_two(dhidden_two)
        dafter = dmoe_in + dnorm_two
        dafter_low = dafter.astype(bfloat)
        wo_grad = over_rows(mixed, dafter_low)
        dmixed = over_last(dafter_low, squares[4]).astype(bfloat).reshape(rows, heads, HEAD)
        dprob = jnp.einsum("qhd,khd->hqk", dmixed, value_h, preferred_element_type=jnp.float32)
        row_shift = jnp.sum(probs * dprob, axis=-1, keepdims=True)
        dscores = (probs * (dprob - row_shift)).astype(bfloat)
        dquery = (
            jnp.einsum("hqk,khd->qhd", dscores, key_h, preferred_element_type=jnp.float32) * scale
        )
        dkey = (
            jnp.einsum("hqk,qhd->khd", dscores, query_h, preferred_element_type=jnp.float32) * scale
        )
        dvalue = jnp.einsum("hqk,qhd->khd", probs_low, dmixed, preferred_element_type=jnp.float32)
        dkey_own, dvalue_own = (
            lax.psum_scatter(dkey.reshape(-1, width), "rep", scatter_dimension=0, tiled=True),
            lax.psum_scatter(dvalue.reshape(-1, width), "rep", scatter_dimension=0, tiled=True),
        )
        dproj = jnp.stack([dquery.reshape(rows, width), dkey_own, dvalue_own], axis=1).astype(
            bfloat
        )
        qkv_grad = jnp.einsum("rd,rke->kde", hidden_one, dproj, preferred_element_type=jnp.float32)
        dhidden_one = jnp.einsum(
            "rke,kde->rd", dproj, squares[1:4], preferred_element_type=jnp.float32
        )
        bias_query = jnp.sum(dproj[:, 0].astype(jnp.float32), axis=0)
        bias_value = jnp.sum(dproj[:, 2].astype(jnp.float32), axis=0)
        dnorm_one, dgain_one, dshift_one = pull_one(dhidden_one)
        dembed = dafter + dnorm_one
        embed_grad = over_rows(patch_rows, dembed.astype(bfloat))
        vector_grad = jnp.stack(
            [
                jnp.sum(dembed, axis=0),
                dgain_one,
                dshift_one,
                bias_query,
                bias_value,
                jnp.sum(dafter, axis=0),
                dgain_two,
                dshift_two,
                dgain_final,
                dshift_final,
            ]
        )
        square_grad = jnp.concatenate([embed_grad[None], qkv_grad, wo_grad[None]], axis=0)
        return (
            loss_part,
            (square_grad, router_grad, dembed, vector_grad, head_grad, jnp.stack([dw_in, dw_out])),
        )

    def accumulate(micro, carry):
        loss_part, grads = micro_pass(micro)
        expert_term = reduce_experts(grads[5])
        return (
            carry[0] + loss_part,
            carry[1] + grads[0],
            carry[2] + grads[1],
            carry[3] + grads[2],
            carry[4] + grads[3],
            carry[5] + grads[4],
            carry[6] + expert_term,
        )

    expert_zero = jnp.zeros((2, width, ff_dev), jnp.float32)
    start = (
        jnp.zeros((), jnp.float32),
        jnp.zeros((5, width, width), jnp.float32),
        jnp.zeros((width, num_expert), jnp.float32),
        jnp.zeros((rows, width), jnp.float32),
        jnp.zeros((10, width), jnp.float32),
        jnp.zeros((width, vocab_dev), jnp.float32),
        expert_zero,
    )
    result = lax.fori_loop(0, micro_total, accumulate, start)
    expert_sum = result[6]
    table_full = lax.dynamic_update_slice_in_dim(
        jnp.zeros((PATCHES, width), jnp.float32), result[3], rep_index * rows, 0
    )
    square_g, router_g, table_g, vector_g = (
        lax.psum_scatter(result[1], ("rep", "exp"), scatter_dimension=1, tiled=True),
        lax.psum_scatter(result[2], ("rep", "exp"), scatter_dimension=0, tiled=True),
        lax.psum_scatter(table_full, ("rep", "exp"), scatter_dimension=1, tiled=True),
        lax.psum_scatter(result[4], ("rep", "exp"), scatter_dimension=1, tiled=True),
    )
    head_g = result[5]
    expert_g = expert_sum[None]
    norm_part = (
        jnp.sum(square_g * square_g)
        + jnp.sum(router_g * router_g)
        + jnp.sum(table_g * table_g)
        + jnp.sum(vector_g * vector_g)
        + jnp.sum(head_g * head_g)
        + jnp.sum(expert_g * expert_g)
    )
    square_rowmean = jnp.mean(square_g * square_g, axis=2)
    router_rowmean = jnp.mean(router_g * router_g, axis=1)
    expert_rowsq = jnp.sum(expert_g * expert_g, axis=-1)
    zero_index = my_image * 0
    expert_spread = lax.dynamic_update_slice(
        jnp.zeros((num_exp, 2, width), jnp.float32),
        expert_rowsq,
        (my_image, zero_index, zero_index),
    )
    totals = lax.psum(
        (
            result[0],
            norm_part,
            jnp.sum(square_g * square_g, axis=1),
            jnp.sum(square_rows, axis=1),
            jnp.sum(square_rowmean, axis=1),
            jnp.sum(router_g * router_g, axis=0),
            jnp.sum(router_rows),
            jnp.sum(router_rowmean),
            jnp.sum(table_g * table_g, axis=1),
            jnp.sum(head_g * head_g, axis=1),
            expert_spread,
        ),
        ("rep", "exp"),
    )
    (
        loss_total,
        norm_total,
        square_colsq,
        square_rows_sum,
        square_mean_sum,
        router_colsq,
        router_rows_sum,
        router_mean_sum,
        table_rowsq,
        head_rowsq,
        expert_rowsq_all,
    ) = totals
    grad_norm = jnp.sqrt(norm_total)
    clip = jnp.minimum(1.0, CLIP_NORM / grad_norm)
    clip_sq = clip * clip
    keep = 1.0 - DECAY
    square_clip = clip * square_g
    square_rows_next = DECAY * square_rows + keep * (clip_sq * square_rowmean + EPS_SQ)
    square_cols_next = DECAY * square_cols + keep * (clip_sq * square_colsq / width + EPS_SQ)
    square_mean = (
        DECAY * square_rows_sum + keep * (clip_sq * square_mean_sum + width * EPS_SQ)
    ) / width
    square_rate = jnp.array([1.0, 1.0, 1.0, 1.0, 4.0], jnp.float32)[:, None, None] * (
        0.3 / math.sqrt(D)
    )
    square_next = factored_step(
        square_weights,
        square_clip,
        square_rows_next,
        square_cols_next,
        square_mean[:, None, None],
        square_rate,
    )
    router_clip = clip * router_g
    router_rows_next = DECAY * router_rows + keep * (clip_sq * router_rowmean + EPS_SQ)
    router_cols_next = DECAY * router_cols + keep * (clip_sq * router_colsq / width + EPS_SQ)
    router_mean = (
        DECAY * router_rows_sum + keep * (clip_sq * router_mean_sum + width * EPS_SQ)
    ) / width
    router_next = factored_step(
        router_weight,
        router_clip,
        router_rows_next,
        router_cols_next,
        router_mean,
        0.2 / math.sqrt(D),
    )
    table_clip = clip * table_g
    table_rows_next = DECAY * position_rows + keep * (clip_sq * table_rowsq / width + EPS_SQ)
    table_cols_next = DECAY * position_cols + keep * (
        clip_sq * jnp.mean(table_g * table_g, axis=0) + EPS_SQ
    )
    table_next = factored_step(
        position_table,
        table_clip,
        table_rows_next,
        table_cols_next,
        jnp.mean(table_rows_next),
        0.15,
    )
    head_clip = clip * head_g
    head_rows_next = DECAY * head_rows + keep * (
        clip_sq * head_rowsq / (vocab_dev * num_rep * num_exp) + EPS_SQ
    )
    head_cols_next = DECAY * head_cols + keep * (
        clip_sq * jnp.mean(head_g * head_g, axis=0) + EPS_SQ
    )
    head_next = factored_step(
        head_weight,
        head_clip,
        head_rows_next,
        head_cols_next,
        jnp.mean(head_rows_next),
        0.5 / math.sqrt(D),
    )
    expert_clip = clip * expert_g
    expert_mine = lax.dynamic_index_in_dim(expert_rowsq_all, my_image, 0, keepdims=True)
    expert_rows_next = DECAY * expert_rows + keep * (
        clip_sq * expert_mine / (ff_dev * num_rep) + EPS_SQ
    )
    expert_cols_next = DECAY * expert_cols + keep * (
        clip_sq * jnp.mean(expert_g * expert_g, axis=2) + EPS_SQ
    )
    expert_rate = jnp.array([0.3 / math.sqrt(D), 4.8 / math.sqrt(FF)], jnp.float32)[
        None, :, None, None
    ]
    expert_next = factored_step(
        expert_weights,
        expert_clip,
        expert_rows_next,
        expert_cols_next,
        jnp.mean(expert_rows_next, axis=-1)[..., None, None],
        expert_rate,
    )
    vector_clip = clip * vector_g
    moment_next = DECAY * vector_moment + keep * (vector_clip * vector_clip + EPS_SQ)
    vector_next = vector_params - 0.3 * vector_clip * lax.rsqrt(moment_next)
    return (
        loss_total,
        image_count,
        grad_norm,
        square_clip,
        square_rows_next,
        square_cols_next,
        square_next,
        router_clip,
        router_rows_next,
        router_cols_next,
        router_next,
        table_clip,
        table_rows_next,
        table_cols_next,
        table_next,
        head_clip,
        head_rows_next,
        head_cols_next,
        head_next,
        expert_clip,
        expert_rows_next,
        expert_cols_next,
        expert_next,
        vector_clip,
        moment_next,
        vector_next,
    )


def solution(mesh):
    in_specs = (
        P(None, "exp", "rep", None),
        P(None, "exp", "rep", None),
        P(),
        P(),
        P(None, ("rep", "exp"), None),
        P(("rep", "exp"), None),
        P(None, ("rep", "exp")),
        P(None, ("rep", "exp")),
        P("exp", None, None, "rep"),
        P(None, ("rep", "exp")),
        P(None, ("rep", "exp")),
        P(),
        P(("rep", "exp")),
        P(),
        P(),
        P(("rep", "exp")),
        P(),
        P(("rep", "exp")),
        P("exp", None, None),
        P("exp", None, "rep"),
        P(None, ("rep", "exp")),
    )
    out_specs = (
        P(),
        P(),
        P(),
        P(None, ("rep", "exp"), None),
        P(None, ("rep", "exp")),
        P(),
        P(None, ("rep", "exp"), None),
        P(("rep", "exp"), None),
        P(("rep", "exp")),
        P(),
        P(("rep", "exp"), None),
        P(None, ("rep", "exp")),
        P(),
        P(("rep", "exp")),
        P(None, ("rep", "exp")),
        P(None, ("rep", "exp")),
        P(),
        P(("rep", "exp")),
        P(None, ("rep", "exp")),
        P("exp", None, None, "rep"),
        P("exp", None, None),
        P("exp", None, "rep"),
        P("exp", None, None, "rep"),
        P(None, ("rep", "exp")),
        P(None, ("rep", "exp")),
        P(None, ("rep", "exp")),
    )
    return jax.shard_map(shards, mesh=mesh, in_specs=in_specs, out_specs=out_specs, check_vma=False)
```

profile of v0, /device:TPU:1, one launch (start us, length us, event | category | flops | bytes accessed | tf_op | source)
XLA Modules:
  0.0 2729.3 jit_solution(18268395873258033231)
XLA Ops:
  13.7 284.0 %all-gather.3 = f32[128,6,10]{2,1,0:T(8,128)S(1)} all-gather(f32[1,6,10]{2,1,0:T(8,128)S(1)} %bitcast.305), channel_id=1, replica_groups=mesh['rep'=4,'exp'=32] {'rep','exp'}, dimensions={0}, use_global_device_ids=true | all-gather | bytes 30960 | tf_op jit(solution)/shard_map/all_gather | solution.py:85
  297.9 286.9 %all-gather.5 = bf16[128,6,32]{2,1,0:T(8,128)(2,1)S(1)} all-gather(bf16[1,6,32]{2,1,0:T(8,128)(2,1)S(1)} %convert_bitcast_fusion.3), channel_id=1, replica_groups=mesh['rep'=4,'exp'=32] {'rep','exp'}, dimensions={0}, use_global_device_ids=true | all-gather | bytes 49536 | tf_op jit(solution)/shard_map/all_gather | solution.py:81
  588.7 48.0 %all-gather.16.cloned.1.call-done = bf16[5,768,768]{2,0,1:T(8,128)(2,1)} async-done(((bf16[5,6,768]{2,0,1:T(8,128)(2,1)}), bf16[5,768,768]{2,0,1:T(8,128)(2,1)}) %all-gather.16.cloned.1.call-update) | async-done | bytes 5898256 | tf_op jit(solution)/shard_map/all_gather | solution.py:80
  636.6 7.5 copy.166
  644.1 63.2 %all-gather.18.cloned.1.call-done = bf16[1,2,768,3072]{3,2,1,0:T(8,128)(2,1)} async-done(((bf16[1,2,768,768]{3,2,1,0:T(8,128)(2,1)}), bf16[1,2,768,3072]{3,2,1,0:T(8,128)(2,1)}) %all-gather.18.cloned.1.call-update) | async-done | bytes 9437200 | tf_op jit(solution)/shard_map/all_gather | solution.py:87
  707.3 8.3 slice_bitcast_fusion.1
  715.6 1707.7 %while.29 = (s32[]{:T(128)}, f32[]{:T(128)}, f32[5,768,768]{1,2,0:T(8,128)}, f32[768,32]{0,1:T(8,128)}, f32[144,768]{1,0:T(8,128)}, /*index=5*/f32[10,768]{1,0:T...) while((s32[]{:T(128)}, f32[]{:T(128)}, ...), condition=%wide.region_45.46_spmd.clone.clone, body=%wide.region_1.45_spmd.clone.clone.sunk | while | flops 12906099712 | bytes 454016832 | solution.py:284
  722.5 10.9 all_gather.55
  734.8 11.0 all-gather.10
  759.9 7.5 all-to-all-start
  769.0 11.1 all-to-all-done
  792.3 5.2 all-to-all-start.1
  799.5 10.2 all-to-all-done.1
  812.3 279.4 %all-gather.11 = f32[128,1,768]{2,1,0:T(1,128)S(1)} all-gather(f32[1,1,768]{2,1,0:T(1,128)S(1)} %reshape.762), channel_id=3, replica_groups=mesh['rep'=4,'exp'=32] {'rep','exp'}, dimensions={0}, use_global_device_ids=true | all-gather | bytes 396288 | tf_op jit(solution)/shard_map/while/body/eval_jaxpr/all_gather | solution.py:168
  1097.0 167.3 %all-reduce.12.cloned.1.call-done = f32[32,768]{1,0:T(8,128)} async-done(((f32[32,768]{1,0:T(8,128)}), f32[32,768]{1,0:T(8,128)}) %all-reduce.12.cloned.1.call-update) | async-done | bytes 98320 | tf_op jit(solution)/shard_map/while/body/eval_jaxpr/psum | solution.py:183
  1274.3 16.2 all_to_all.60
  1291.8 7.2 fusion.278
  1307.3 5.9 all-to-all-start.3
  1313.6 11.5 all-to-all-done.3
  1355.9 7.0 pad_maximum_fusion.7
  1374.3 37.4 %reduce-scatter.7.cloned.1.call-done = f32[144,768]{1,0:T(8,128)} async-done(((f32[576,768]{1,0:T(8,128)}), f32[144,768]{1,0:T(8,128)}) %reduce-scatter.7.cloned.1.call-update) | async-done | bytes 442384 | tf_op jit(solution)/shard_map/while/body/eval_jaxpr/reduce_scatter | solution.py:226
  1419.5 6.3 maximum_add_fusion.2
  1425.7 134.5 %reduce-scatter.9.cloned.1.call-done = f32[2,768,768]{2,1,0:T(8,128)} async-done(((f32[2,768,3072]{2,1,0:T(8,128)}), f32[2,768,768]{2,1,0:T(8,128)}) %reduce-scatter.9.cloned.1.call-update) | async-done | bytes 4718608 | tf_op jit(solution)/shard_map/while/body/eval_jaxpr/reduce_scatter | solution.py:47
  1560.3 5.2 select_add_fusion.8
  1572.9 10.9 all_gather.55
  1585.1 11.0 all-gather.10
  1610.2 7.2 all-to-all-start
  1619.0 11.1 all-to-all-done
  1642.4 5.2 all-to-all-start.1
  1649.5 10.2 all-to-all-done.1
  1662.3 279.4 %all-gather.11 = f32[128,1,768]{2,1,0:T(1,128)S(1)} all-gather(f32[1,1,768]{2,1,0:T(1,128)S(1)} %reshape.762), channel_id=3, replica_groups=mesh['rep'=4,'exp'=32] {'rep','exp'}, dimensions={0}, use_global_device_ids=true | all-gather | bytes 396288 | tf_op jit(solution)/shard_map/while/body/eval_jaxpr/all_gather | solution.py:168
  1947.0 167.3 %all-reduce.12.cloned.1.call-done = f32[32,768]{1,0:T(8,128)} async-done(((f32[32,768]{1,0:T(8,128)}), f32[32,768]{1,0:T(8,128)}) %all-reduce.12.cloned.1.call-update) | async-done | bytes 98320 | tf_op jit(solution)/shard_map/while/body/eval_jaxpr/psum | solution.py:183
  2124.3 16.2 all_to_all.60
  2141.8 7.2 fusion.278
  2157.4 5.9 all-to-all-start.3
  2163.6 11.5 all-to-all-done.3
  2206.1 7.0 pad_maximum_fusion.7
  2225.1 36.7 %reduce-scatter.7.cloned.1.call-done = f32[144,768]{1,0:T(8,128)} async-done(((f32[576,768]{1,0:T(8,128)}), f32[144,768]{1,0:T(8,128)}) %reduce-scatter.7.cloned.1.call-update) | async-done | bytes 442384 | tf_op jit(solution)/shard_map/while/body/eval_jaxpr/reduce_scatter | solution.py:226
  2269.6 11.7 maximum_add_fusion.2
  2281.2 129.1 %reduce-scatter.9.cloned.1.call-done = f32[2,768,768]{2,1,0:T(8,128)} async-done(((f32[2,768,3072]{2,1,0:T(8,128)}), f32[2,768,768]{2,1,0:T(8,128)}) %reduce-scatter.9.cloned.1.call-update) | async-done | bytes 4718608 | tf_op jit(solution)/shard_map/while/body/eval_jaxpr/reduce_scatter | solution.py:47
  2410.4 6.6 select_add_fusion.8
  2423.4 13.8 copy.169
  2443.0 7.0 dynamic_update_slice.6
  2452.2 68.2 %all-reduce.4 = f32[10,768]{0,1:T(8,128)S(1)} all-reduce(f32[10,768]{0,1:T(8,128)S(1)} %copy.172), channel_id=10, replica_groups=mesh['rep'=4,'exp'=32] {'rep','exp'}, use_global_device_ids=true, to_apply=%region_53.54.clone | all-reduce | flops 7680 | bytes 61440
  2521.8 101.6 %all-reduce.10.cloned.1.call-done = (f32[5,768,768]{2,1,0:T(8,128)}, f32[768,32]{1,0:T(8,128)}, f32[576,768]{0,1:T(8,128)}, f32[32,2,768]{2,1,0:T(2,128)}) async-done(((f32[5,768,768]{2,1,0:T(8,128)}, f32[768,32]{1,0:T(8,128)}, f32[576,768]{0,1:T(8,128)}, f32[32,2,768]{2,1,0:T(2,128)}), (f32[5,768,768]{2,1,0:T(8,128)}, f32[768,32]{1,0:T(8,128)}, f32[576,768]{0,1:T(8,128)}, ...) | async-done | bytes 13860880
  2632.5 65.7 %all-reduce.5 = (f32[]{:T(128)}, f32[]{:T(128)}, f32[5,768]{1,0:T(8,128)S(1)}, f32[5]{0:T(128)S(1)}, f32[5]{0:T(128)S(1)}, /*index=5*/f32[32]{0:T(128)S(1)}, f32...) all-reduce(f32[]{:T(128)} %get-tuple-element.1414, ...), channel_id=1, replica_groups=mesh['rep'=4,'exp'=32] {'rep','exp'}, use_global_device_ids=true, to_apply=%region_46.47 | all-reduce | flops 5230 | bytes 41840 | tf_op jit(solution)/shard_map/psum | solution.py:314
  2699.1 4.9 multiply_bitcast_fusion
  2715.2 5.8 bitcast_subtract_fusion
  (721 shorter events, 262.4 us)
Async XLA Ops:
  7.2 578.5 %all-gather.20.cloned.1.call-start = ((), (), s32[]{:S(2)}) async-start(), calls=%async_computation.9 | async-start | bytes 2641920 | tf_op jit(solution)/shard_map/all_gather | solution.py:84
  7.9 628.7 %all-gather.16.cloned.1.call-start = ((), (), s32[]{:S(2)}) async-start(), calls=%async_computation.7 | async-start | bytes 9510912 | tf_op jit(solution)/shard_map/all_gather | solution.py:80
  9.6 288.3 %copy-start.93 = (f32[6,32]{1,0:T(8,128)S(1)}, f32[6,32]{1,0:T(8,128)}, u32[]{:S(2)}) copy-start(f32[6,32]{1,0:T(8,128)} %param.30) | copy-start | bytes 2308
  9.6 697.7 %all-gather.18.cloned.1.call-start = ((), (), s32[]{:S(2)}) async-start(), calls=%async_computation.8 | async-start | bytes 11796480 | tf_op jit(solution)/shard_map/all_gather | solution.py:87
  13.6 571.3 %copy-start.33 = (f32[768,171]{0,1:T(8,128)S(1)}, f32[768,171]{0,1:T(8,128)}, u32[]{:S(2)}) copy-start(f32[768,171]{0,1:T(8,128)} %param.32) | copy-start | bytes 1575940
  13.6 571.5 %copy-start.106 = (s32[2,32]{1,0:T(2,128)S(1)}, s32[2,32]{1,0:T(2,128)}, u32[]{:S(2)}) copy-start(s32[2,32]{1,0:T(2,128)} %param.28) | copy-start | bytes 772
  644.1 71.5 %copy-start.77 = (s32[2,1,144,2]{2,3,1,0:T(2,128)S(1)}, s32[2,1,144,2]{2,3,1,0:T(2,128)}, u32[]{:S(2)}) copy-start(s32[2,1,144,2]{2,3,1,0:T(2,128)} %param.26) | copy-start | bytes 6916
  715.6 51.8 %copy-start.17 = (bf16[768,32]{1,0:T(8,128)(2,1)}, bf16[768,32]{1,0:T(8,128)(2,1)S(1)}, u32[]{:S(2)}) copy-start(bf16[768,32]{1,0:T(8,128)(2,1)S(1)} %get-tuple-element.1326) | copy-start | bytes 147460 | tf_op jit(solution)/shard_map/while
  715.6 82.0 %copy-start.108 = (f32[2,32]{1,0:T(2,128)}, f32[2,32]{1,0:T(2,128)S(1)}, u32[]{:S(2)}) copy-start(f32[2,32]{1,0:T(2,128)S(1)} %get-tuple-element.1320) | copy-start | bytes 772 | tf_op jit(solution)/shard_map/while
  715.6 377.6 %copy-start.12 = (bf16[768,171]{1,0:T(8,128)(2,1)}, bf16[768,171]{1,0:T(8,128)(2,1)S(1)}, u32[]{:S(2)}) copy-start(bf16[768,171]{1,0:T(8,128)(2,1)S(1)} %get-tuple-element.1329) | copy-start | bytes 787972 | tf_op jit(solution)/shard_map/while
  722.5 23.8 slice-start
  756.2 24.0 copy-start.6
  759.9 20.2 all-to-all-start
  792.3 17.3 all-to-all-start.1
  797.6 466.8 %all-reduce.12.cloned.1.call-start = ((), (), s32[]{:S(2)}) async-start(), calls=%async_computation.11 | async-start | bytes 196608 | tf_op jit(solution)/shard_map/while/body/eval_jaxpr/psum | solution.py:183
  811.2 456.4 %copy-start.42 = (f32[144]{0:T(256)}, f32[144]{0:T(256)S(1)}, u32[]{:S(2)}) copy-start(f32[144]{0:T(256)S(1)} %broadcast_multiply_fusion.15) | copy-start | bytes 1732 | tf_op jit(solution)/shard_map/while
  811.4 456.2 %copy-start.52 = (f32[144]{0:T(256)}, f32[144]{0:T(256)S(1)}, u32[]{:S(2)}) copy-start(f32[144]{0:T(256)S(1)} %fusion.274) | copy-start | bytes 1732 | tf_op jit(solution)/shard_map/while
  1091.7 175.9 %copy-start.27 = (bf16[32,768]{1,0:T(8,128)(2,1)}, bf16[32,768]{1,0:T(8,128)(2,1)S(1)}, u32[]{:S(2)}) copy-start(bf16[32,768]{1,0:T(8,128)(2,1)S(1)} %reduce_sum.1055) | copy-start | bytes 147460 | tf_op jit(solution)/shard_map/while
  1093.3 174.3 %copy-start.30 = (f32[32,171]{1,0:T(8,128)}, f32[32,171]{1,0:T(8,128)S(1)}, u32[]{:S(2)}) copy-start(f32[32,171]{1,0:T(8,128)S(1)} %get-tuple-element.1234) | copy-start | bytes 65668 | tf_op jit(solution)/shard_map/while
  1307.3 17.8 all-to-all-start.3
  1313.2 60.0 %reduce-scatter.5.cloned.1.call-start = ((), (), s32[]{:S(2)}) async-start(), calls=%async_computation.12 | async-start | bytes 2211840 | tf_op jit(solution)/shard_map/while/body/eval_jaxpr/reduce_scatter | solution.py:227
  1336.9 74.8 %reduce-scatter.7.cloned.1.call-start = ((), (), s32[]{:S(2)}) async-start(), calls=%async_computation.13 | async-start | bytes 2211840 | tf_op jit(solution)/shard_map/while/body/eval_jaxpr/reduce_scatter | solution.py:226
  1348.3 212.0 %reduce-scatter.9.cloned.1.call-start = ((), (), s32[]{:S(2)}) async-start(), calls=%async_computation.14 | async-start | bytes 23592960 | tf_op jit(solution)/shard_map/while/body/eval_jaxpr/reduce_scatter | solution.py:47
  1366.3 46.5 %copy-start.45 = (f32[768]{0:T(1024)S(1)}, f32[768]{0:T(1024)}, u32[]{:S(2)}) copy-start(f32[768]{0:T(1024)} %copy-done.44) | copy-start | bytes 9220 | tf_op jit(solution)/shard_map/while
  1366.3 46.5 %copy-start.69 = (f32[144]{0:T(256)S(1)}, f32[144]{0:T(256)}, u32[]{:S(2)}) copy-start(f32[144]{0:T(256)} %copy-done.68) | copy-start | bytes 1732 | tf_op jit(solution)/shard_map/while
  1366.3 46.5 %copy-start.80 = (f32[144]{0:T(256)S(1)}, f32[144]{0:T(256)}, u32[]{:S(2)}) copy-start(f32[144]{0:T(256)} %copy-done.79) | copy-start | bytes 1732 | tf_op jit(solution)/shard_map/while
  1566.0 51.5 %copy-start.17 = (bf16[768,32]{1,0:T(8,128)(2,1)}, bf16[768,32]{1,0:T(8,128)(2,1)S(1)}, u32[]{:S(2)}) copy-start(bf16[768,32]{1,0:T(8,128)(2,1)S(1)} %get-tuple-element.1326) | copy-start | bytes 147460 | tf_op jit(solution)/shard_map/while
  1566.0 81.7 %copy-start.108 = (f32[2,32]{1,0:T(2,128)}, f32[2,32]{1,0:T(2,128)S(1)}, u32[]{:S(2)}) copy-start(f32[2,32]{1,0:T(2,128)S(1)} %get-tuple-element.1320) | copy-start | bytes 772 | tf_op jit(solution)/shard_map/while
  1566.0 377.3 %copy-start.12 = (bf16[768,171]{1,0:T(8,128)(2,1)}, bf16[768,171]{1,0:T(8,128)(2,1)S(1)}, u32[]{:S(2)}) copy-start(bf16[768,171]{1,0:T(8,128)(2,1)S(1)} %get-tuple-element.1329) | copy-start | bytes 787972 | tf_op jit(solution)/shard_map/while
  1572.9 23.8 slice-start
  1606.6 23.7 copy-start.6
  1610.2 19.8 all-to-all-start
  1642.4 17.3 all-to-all-start.1
  1647.6 466.7 %all-reduce.12.cloned.1.call-start = ((), (), s32[]{:S(2)}) async-start(), calls=%async_computation.11 | async-start | bytes 196608 | tf_op jit(solution)/shard_map/while/body/eval_jaxpr/psum | solution.py:183
  1661.2 456.4 %copy-start.42 = (f32[144]{0:T(256)}, f32[144]{0:T(256)S(1)}, u32[]{:S(2)}) copy-start(f32[144]{0:T(256)S(1)} %broadcast_multiply_fusion.15) | copy-start | bytes 1732 | tf_op jit(solution)/shard_map/while
  1661.4 456.2 %copy-start.52 = (f32[144]{0:T(256)}, f32[144]{0:T(256)S(1)}, u32[]{:S(2)}) copy-start(f32[144]{0:T(256)S(1)} %fusion.274) | copy-start | bytes 1732 | tf_op jit(solution)/shard_map/while
  1941.7 175.9 %copy-start.27 = (bf16[32,768]{1,0:T(8,128)(2,1)}, bf16[32,768]{1,0:T(8,128)(2,1)S(1)}, u32[]{:S(2)}) copy-start(bf16[32,768]{1,0:T(8,128)(2,1)S(1)} %reduce_sum.1055) | copy-start | bytes 147460 | tf_op jit(solution)/shard_map/while
  1943.3 174.3 %copy-start.30 = (f32[32,171]{1,0:T(8,128)}, f32[32,171]{1,0:T(8,128)S(1)}, u32[]{:S(2)}) copy-start(f32[32,171]{1,0:T(8,128)S(1)} %get-tuple-element.1234) | copy-start | bytes 65668 | tf_op jit(solution)/shard_map/while
  2157.4 22.1 copy-start.63
  2157.4 17.8 all-to-all-start.3
  2163.3 60.7 %reduce-scatter.5.cloned.1.call-start = ((), (), s32[]{:S(2)}) async-start(), calls=%async_computation.12 | async-start | bytes 2211840 | tf_op jit(solution)/shard_map/while/body/eval_jaxpr/reduce_scatter | solution.py:227
  2186.9 74.9 %reduce-scatter.7.cloned.1.call-start = ((), (), s32[]{:S(2)}) async-start(), calls=%async_computation.13 | async-start | bytes 2211840 | tf_op jit(solution)/shard_map/while/body/eval_jaxpr/reduce_scatter | solution.py:226
  2198.3 212.0 %reduce-scatter.9.cloned.1.call-start = ((), (), s32[]{:S(2)}) async-start(), calls=%async_computation.14 | async-start | bytes 23592960 | tf_op jit(solution)/shard_map/while/body/eval_jaxpr/reduce_scatter | solution.py:47
  2218.5 44.4 %copy-start.45 = (f32[768]{0:T(1024)S(1)}, f32[768]{0:T(1024)}, u32[]{:S(2)}) copy-start(f32[768]{0:T(1024)} %copy-done.44) | copy-start | bytes 9220 | tf_op jit(solution)/shard_map/while
  2218.5 44.4 %copy-start.69 = (f32[144]{0:T(256)S(1)}, f32[144]{0:T(256)}, u32[]{:S(2)}) copy-start(f32[144]{0:T(256)} %copy-done.68) | copy-start | bytes 1732 | tf_op jit(solution)/shard_map/while
  2218.5 44.4 %copy-start.80 = (f32[144]{0:T(256)S(1)}, f32[144]{0:T(256)}, u32[]{:S(2)}) copy-start(f32[144]{0:T(256)} %copy-done.79) | copy-start | bytes 1732 | tf_op jit(solution)/shard_map/while
  2423.4 200.0 %all-reduce.10.cloned.1.call-start = ((), (), s32[]{:S(2)}) async-start(), calls=%async_computation.10 | async-start | bytes 28704768
  2450.1 71.0 %copy-start.16 = (f32[768,171]{0,1:T(8,128)S(1)}, f32[768,171]{0,1:T(8,128)}, u32[]{:S(2)}) copy-start(f32[768,171]{0,1:T(8,128)} %get-tuple-element.1419) | copy-start | bytes 1575940
  (163 other events, 1196.4 us)
Sparse Core Ops, SparseCore 0:
  9.7 307.1 all-gather.19
  319.2 317.3 all-gather.15
  638.9 68.3 all-gather.17
  1095.6 168.6 all-reduce.11
  1337.0 36.1 reduce-scatter.4
  1376.0 35.6 reduce-scatter.6
  1414.4 145.7 reduce-scatter.8
  1945.6 168.6 all-reduce.11
  2187.1 36.2 reduce-scatter.4
  2226.1 35.6 reduce-scatter.6
  2264.5 145.7 reduce-scatter.8
  2451.4 171.8 all-reduce.9
where the time goes:
time: 2740 us; the launch traced here: 2730 us
  blocking collectives  1340 us (49%)
  waiting for transfers between devices  953 us (35%)
  matrix products  154 us (6%)
  other arithmetic  112 us (4%)
  local copies, waits for them, and re-layouts  98.5 us (4%)
  starting transfers between devices  38.1 us (1%)
    all_gather x2, blocking collectives, micro_pass(): lax.all_gather(partial_pool[None, :], ('rep', 'exp'), axis=0, tiled=True)  559 us
    psum x2, waiting for transfers between devices, micro_pass(): pool_grad = lax.psum(over_last(dlogits, head_low), ('rep', 'exp'))  335 us
    all_gather x1, blocking collectives, shards(): lax.all_gather(router_weight.astype(bfloat), ('rep', 'exp'), axis=0, tile...  287 us
    all_gather x1, blocking collectives, shards(): lax.all_gather(vector_params, ('rep', 'exp'), axis=1, tiled=True)  284 us
    reduce_scatter x2, waiting for transfers between devices, reduce_experts(): return lax.psum_scatter(value, 'rep', scatter_dimension=2, tiled=True)  264 us
    unnamed x5, waiting for transfers between devices  102 us
    reduce_scatter x2, waiting for transfers between devices, micro_pass(): lax.psum_scatter(dkey.reshape(-1, width), 'rep', scatter_dimension=0, til...  74.1 us
    unnamed x1, blocking collectives  68.2 us
  transfers between devices with their start and end apart: 18, of which 16 were waited for; matrix products, arithmetic and copies ran while one was open for 5% of the time, Pallas kernels for 0%

commit v1 on v0

v1 whole, which is shorter than its diff:
```python
import functools
import math

import jax
import jax.numpy as jnp
from jax import lax
from jax.experimental import pallas as pl
from jax.experimental.pallas import tpu as pltpu
from jax.sharding import PartitionSpec as P

D = 768
HEAD = 64
FF = 3072
PATCHES = 576
CAP = 10
PAD = 8
LANES = 128


DECAY = 0.8
EPS_SQ = 1e-30
CLIP_NORM = 0.25
HIGHEST = lax.Precision.HIGHEST
MESH = pl.DeviceIdType.MESH

Y_SWAP = ((0, 2), (1, 3), (2, 0), (3, 1))
CORE_SWAP = ((0, 1), (1, 0), (2, 3), (3, 2))


def layer_norm(value, gain, shift):
    centred = value - jnp.mean(value, axis=-1, keepdims=True)
    spread = jnp.mean(centred * centred, axis=-1, keepdims=True)
    return centred * lax.rsqrt(spread + 1e-06) * gain + shift


def plain_dot(left, right):
    return jnp.dot(left, right, preferred_element_type=jnp.float32)


def over_rows(left, right):
    return lax.dot_general(
        left, right, (((0,), (0,)), ((), ())), preferred_element_type=jnp.float32
    )


def over_last(left, right):
    return lax.dot_general(
        left, right, (((1,), (1,)), ((), ())), preferred_element_type=jnp.float32
    )


def factored_step(weight, clipped, rows_next, cols_next, rows_mean, rate):
    estimate = rows_next[..., :, None] * cols_next[..., None, :] / rows_mean
    return weight - rate * clipped * lax.rsqrt(estimate)


def place():
    rep = lax.axis_index("rep")
    line = lax.axis_index("exp")
    y = lax.div(rep, 2) * 2 + lax.rem(lax.div(line, 4), 2)
    return {"y": y, "core": lax.rem(rep, 2), "x": lax.div(line, 8), "z": lax.rem(line, 4)}


def device(at):
    return {
        "rep": lax.div(at["y"], 2) * 2 + at["core"],
        "exp": at["x"] * 8 + lax.rem(at["y"], 2) * 4 + at["z"],
    }


def moved(at, axis, by):
    return {**at, axis: lax.rem(at[axis] + by, 2 if axis == "core" else 4)}


def box(ref, at, free, core=False):
    whole = slice(None)
    hi = whole if "y" in free else lax.div(at["y"], 2)
    low = whole if "y" in free else lax.rem(at["y"], 2)
    x = whole if "x" in free else at["x"]
    z = whole if "z" in free else at["z"]
    if core:
        return ref.at[hi, at["core"], x, low, z]
    return ref.at[hi, x, low, z]


def greet(at):
    barrier = pltpu.get_barrier_semaphore()
    peers = [moved(at, axis, by) for axis in ("x", "y", "z") for by in (1, 2, 3)]
    peers.append(moved(at, "core", 1))
    for peer in peers:
        pl.semaphore_signal(barrier, inc=1, device_id=device(peer), device_id_type=MESH)
    pl.semaphore_wait(barrier, len(peers))


def remote(src, dst, sems, index, peer):
    return pltpu.make_async_remote_copy(
        src_ref=src,
        dst_ref=dst,
        send_sem=sems[0].at[index],
        recv_sem=sems[1].at[index],
        device_id=device(peer),
        device_id_type=MESH,
    )


ORDERS = (("x", "y", "z"), ("y", "z", "x"), ("z", "x", "y"))


def gather_kernel(x_ref, *refs):
    outs, (send, recv, local) = refs[:3], refs[3:]
    at = place()
    sems = (send, recv)
    own = []
    for part in range(3):
        own.append(
            pltpu.make_async_copy(
                x_ref.at[part], box(outs[part], at, (), True), local.at[part]
            )
        )
        own[part].start()
    greet(at)
    flights = {}

    def launch(part, stage):
        axes = ORDERS[part]
        view = box(outs[part], at, axes[:stage], True)
        source = x_ref.at[part] if stage == 0 else view
        for by in (1, 2, 3):
            copy = remote(source, view, sems, part * 13 + stage * 3 + by - 1, moved(at, axes[stage], by))
            copy.start()
            flights[part, stage, by] = copy

    def forward(part, by):
        axes = ORDERS[part]
        view = box(outs[part], moved(at, axes[2], 4 - by), axes[:2], True)
        copy = remote(view, view, sems, part * 13 + 9 + by, moved(at, "core", 1))
        copy.start()
        flights[part, 3, by] = copy

    for part in range(3):
        launch(part, 0)
    for stage in (1, 2):
        for part in range(3):
            if stage == 1:
                own[part].wait()
            for by in (1, 2, 3):
                flights[part, stage - 1, by].wait_recv()
            launch(part, stage)
            if stage == 2:
                forward(part, 0)
    for part in range(3):
        for by in (1, 2, 3):
            flights[part, 2, by].wait_recv()
            forward(part, by)
    for key, copy in flights.items():
        copy.wait_send()
        if key[1] == 3:
            copy.wait_recv()


def gather_all(payload):
    shape = (2, 2, 4, 2, 4, 16, D)
    return pl.pallas_call(
        gather_kernel,
        out_shape=[jax.ShapeDtypeStruct(shape, payload.dtype)] * 3,
        in_specs=[pl.BlockSpec(memory_space=pl.ANY)],
        out_specs=[pl.BlockSpec(memory_space=pl.ANY)] * 3,
        scratch_shapes=[
            pltpu.SemaphoreType.DMA((39,)),
            pltpu.SemaphoreType.DMA((39,)),
            pltpu.SemaphoreType.DMA((3,)),
        ],
        compiler_params=pltpu.CompilerParams(collective_id=0, has_side_effects=True),
        name="gather_weights",
    )(payload)


def scatter_kernel(*refs):
    grads, outs = refs[:6], refs[6:12]
    first, total_one, second, total_two, third = (refs[12 + 6 * i : 18 + 6 * i] for i in range(5))
    sems = refs[42:44]
    at = place()
    greet(at)
    stages = []

    def launch(which, stage):
        axes = ORDERS[which // 2]
        axis = axes[2 - stage]
        source = (grads, total_one, total_two)[stage][which]
        landing = (first, second, third)[stage][which]
        copies = []
        for by in (1, 2, 3):
            view = part_of(source, moved(at, axis, by), axes, stage)
            copy = remote(view, landing.at[by - 1], sems, which * 9 + stage * 3 + by - 1, moved(at, axis, by))
            copy.start()
            copies.append(copy)
        return copies

    def part_of(source, where, axes, stage):
        if stage == 0:
            return box(source, where, axes[:2])
        if stage == 1:
            left = [axis for axis in ("h", "x", "l", "z") if axis not in names(axes[2])]
            return source.at[tuple(pick(axis, where, axes[1]) for axis in left)]
        left = [axis for axis in ("h", "x", "l", "z") if axis in names(axes[0])]
        return source.at[tuple(pick(axis, where, axes[0]) for axis in left)]

    def names(axis):
        return ("h", "l") if axis == "y" else (axis,)

    def pick(letter, where, axis):
        if letter not in names(axis):
            return slice(None)
        if letter == "h":
            return lax.div(where["y"], 2)
        if letter == "l":
            return lax.rem(where["y"], 2)
        return where[axis]

    waiting = {}
    for which in range(6):
        waiting[which, 0] = launch(which, 0)
    for stage in range(3):
        for which in range(6):
            axes = ORDERS[which // 2]
            for copy in waiting[which, stage]:
                copy.wait_recv()
            source = (grads, total_one, total_two)[stage][which]
            landing = (first, second, third)[stage][which]
            target = (total_one, total_two, outs)[stage][which]
            mine = part_of(source, at, axes, stage)
            target[...] = (mine[...] + landing[0]) + (landing[1] + landing[2])
            if stage < 2:
                waiting[which, stage + 1] = launch(which, stage + 1)
    for copies in waiting.values():
        for copy in copies:
            copy.wait_send()


def scatter_all(grads):
    block = (PAD, D)

    def shapes(which):
        axes = ORDERS[which // 2]
        dims = {"x": (4,), "z": (4,)}
        one = {"x": (2, 2, 4), "y": (4, 4), "z": (2, 4, 2)}[axes[2]]
        two = (2, 2) if axes[0] == "y" else (4,)
        return one, two

    scratch = []
    ones = [shapes(which)[0] for which in range(6)]
    twos = [shapes(which)[1] for which in range(6)]
    scratch += [pltpu.VMEM((3,) + one + block, jnp.float32) for one in ones]
    scratch += [pltpu.VMEM(one + block, jnp.float32) for one in ones]
    scratch += [pltpu.VMEM((3,) + two + block, jnp.float32) for two in twos]
    scratch += [pltpu.VMEM(two + block, jnp.float32) for two in twos]
    scratch += [pltpu.VMEM((3,) + block, jnp.float32)] * 6
    scratch += [pltpu.SemaphoreType.DMA((54,)), pltpu.SemaphoreType.DMA((54,))]
    return pl.pallas_call(
        scatter_kernel,
        out_shape=[jax.ShapeDtypeStruct(block, jnp.float32)] * 6,
        in_specs=[pl.BlockSpec(memory_space=pltpu.VMEM)] * 6,
        out_specs=[pl.BlockSpec(memory_space=pltpu.VMEM)] * 6,
        scratch_shapes=scratch,
        compiler_params=pltpu.CompilerParams(
            collective_id=1, has_side_effects=True, vmem_limit_bytes=40 * 2**20
        ),
        name="scatter_grads",
    )(*grads)


SMALL = ("z", "x", "y")


def pool_kernel(x_ref, o_ref, other, send, recv):
    at = place()
    sems = (send, recv)
    greet(at)
    swap = remote(x_ref, other, sems, 0, moved(at, "core", 1))
    swap.start()
    swap.wait()
    view = box(o_ref, at, ())
    view[...] = (x_ref[...] + other[...]).astype(jnp.bfloat16).astype(jnp.float32)
    for stage in range(3):
        copies = []
        for by in (1, 2, 3):
            view = box(o_ref, at, SMALL[:stage])
            copy = remote(view, view, sems, 1 + stage * 3 + by - 1, moved(at, SMALL[stage], by))
            copy.start()
            copies.append(copy)
        for copy in copies:
            copy.wait()


def gather_pooled(row):
    return pl.pallas_call(
        pool_kernel,
        out_shape=jax.ShapeDtypeStruct((2, 4, 2, 4) + row.shape, row.dtype),
        in_specs=[pl.BlockSpec(memory_space=pltpu.VMEM)],
        out_specs=pl.BlockSpec(memory_space=pltpu.VMEM),
        scratch_shapes=[
            pltpu.VMEM(row.shape, row.dtype),
            pltpu.SemaphoreType.DMA((10,)),
            pltpu.SemaphoreType.DMA((10,)),
        ],
        compiler_params=pltpu.CompilerParams(collective_id=2, has_side_effects=True),
        name="gather_pooled",
    )(row)


def pull_kernel(x_ref, o_ref, first, total_one, second, total_two, third, mine, other, send, recv):
    at = place()
    sems = (send, recv)
    greet(at)

    def stage(number, axis, views, landing):
        copies = []
        for by in (1, 2, 3):
            copy = remote(
                views(moved(at, axis, by)), landing.at[by - 1], sems, number * 3 + by - 1, moved(at, axis, by)
            )
            copy.start()
            copies.append(copy)
        for copy in copies:
            copy.wait()
        return (views(at)[...] + landing[0]) + (landing[1] + landing[2])

    total_one[...] = stage(0, "y", lambda where: box(x_ref, where, ("x", "z")), first)
    total_two[...] = stage(1, "x", lambda where: total_one.at[where["x"]], second)
    mine[...] = stage(2, "z", lambda where: total_two.at[where["z"]], third)
    swap = remote(mine, other, sems, 9, moved(at, "core", 1))
    swap.start()
    swap.wait()
    o_ref[...] = mine[...] + other[...]


def pull_rows(rows):
    block = rows.shape[4:]
    return pl.pallas_call(
        pull_kernel,
        out_shape=jax.ShapeDtypeStruct(block, rows.dtype),
        in_specs=[pl.BlockSpec(memory_space=pltpu.VMEM)],
        out_specs=pl.BlockSpec(memory_space=pltpu.VMEM),
        scratch_shapes=[
            pltpu.VMEM((3, 4, 4) + block, rows.dtype),
            pltpu.VMEM((4, 4) + block, rows.dtype),
            pltpu.VMEM((3, 4) + block, rows.dtype),
            pltpu.VMEM((4,) + block, rows.dtype),
            pltpu.VMEM((3,) + block, rows.dtype),
            pltpu.VMEM(block, rows.dtype),
            pltpu.VMEM(block, rows.dtype),
            pltpu.SemaphoreType.DMA((10,)),
            pltpu.SemaphoreType.DMA((10,)),
        ],
        compiler_params=pltpu.CompilerParams(collective_id=3, has_side_effects=True),
        name="pull_rows",
    )(rows)


def total_kernel(x_ref, o_ref, slots, sums, send, recv):
    at = place()
    sems = (send, recv)
    greet(at)
    number = 0
    source = x_ref
    for stage, axis in enumerate(("core", "z", "x", "y")):
        size = 2 if axis == "core" else 4
        copies = []
        for by in range(1, size):
            copy = remote(source, slots.at[stage, at[axis]], sems, number, moved(at, axis, by))
            copy.start()
            copies.append(copy)
            number += 1
        slots[stage, at[axis]] = source[...]
        for copy in copies:
            copy.wait()
        total = slots[stage, 0]
        for index in range(1, size):
            total = total + slots[stage, index]
        if stage == 3:
            o_ref[...] = total
        else:
            sums[stage] = total
            source = sums.at[stage]


def total_all(value):
    return pl.pallas_call(
        total_kernel,
        out_shape=jax.ShapeDtypeStruct(value.shape, value.dtype),
        in_specs=[pl.BlockSpec(memory_space=pltpu.VMEM)],
        out_specs=pl.BlockSpec(memory_space=pltpu.VMEM),
        scratch_shapes=[
            pltpu.VMEM((4, 4) + value.shape, value.dtype),
            pltpu.VMEM((3,) + value.shape, value.dtype),
            pltpu.SemaphoreType.DMA((10,)),
            pltpu.SemaphoreType.DMA((10,)),
        ],
        compiler_params=pltpu.CompilerParams(collective_id=4, has_side_effects=True),
        name="total_all",
    )(value)


def swap_kernel(count, x_ref, o_ref, send, recv, local):
    me = lax.axis_index("exp")
    barrier = pltpu.get_barrier_semaphore()
    for by in range(1, count):
        peer = lax.rem(me + by, count)
        pl.semaphore_signal(barrier, inc=1, device_id={"exp": peer}, device_id_type=MESH)
    own = pltpu.make_async_copy(x_ref.at[me], o_ref.at[me], local)
    own.start()
    pl.semaphore_wait(barrier, count - 1)
    copies = []
    for by in range(1, count):
        peer = lax.rem(me + by, count)
        copy = pltpu.make_async_remote_copy(
            src_ref=x_ref.at[peer],
            dst_ref=o_ref.at[me],
            send_sem=send.at[by],
            recv_sem=recv.at[by],
            device_id={"exp": peer},
            device_id_type=MESH,
        )
        copy.start()
        copies.append(copy)
    own.wait()
    for copy in copies:
        copy.wait()


def swap_experts(rows):
    count = rows.shape[0]
    return pl.pallas_call(
        functools.partial(swap_kernel, count),
        out_shape=jax.ShapeDtypeStruct(rows.shape, rows.dtype),
        in_specs=[pl.BlockSpec(memory_space=pltpu.VMEM)],
        out_specs=pl.BlockSpec(memory_space=pltpu.VMEM),
        scratch_shapes=[
            pltpu.SemaphoreType.DMA((count,)),
            pltpu.SemaphoreType.DMA((count,)),
            pltpu.SemaphoreType.DMA(()),
        ],
        compiler_params=pltpu.CompilerParams(collective_id=5, has_side_effects=True),
        name="swap_experts",
    )(rows)


def across_cores(value):
    return lax.ppermute(value, "rep", CORE_SWAP)


def across_y(value):
    return lax.ppermute(value, "rep", Y_SWAP)


def shards(
    patches,
    expert_ids,
    labels,
    label_count,
    square_weights,
    router_weight,
    position_table,
    head_weight,
    expert_weights,
    vector_params,
    square_rows,
    square_cols,
    router_rows,
    router_cols,
    position_rows,
    position_cols,
    head_rows,
    head_cols,
    expert_rows,
    expert_cols,
    vector_moment,
):
    bfloat = jnp.bfloat16
    num_rep = lax.axis_size("rep")
    num_exp = lax.axis_size("exp")
    rep_index = lax.axis_index("rep")
    my_image = lax.axis_index("exp")
    device_index = lax.axis_index(("rep", "exp"))
    micro, core = rep_index // 2, rep_index % 2
    num_expert = router_weight.shape[1]
    vocab_dev = head_weight.shape[1]
    ff_dev = expert_weights.shape[3]
    block = patches.shape[2]
    rows, width = 2 * block, patches.shape[3]
    num_top = expert_ids.shape[3]
    heads = width // HEAD
    scale = HEAD ** (-0.5)
    own_rows = square_weights.shape[1]

    def pad_rows(value):
        return jnp.pad(value, ((0, PAD - own_rows), (0, width - value.shape[1])))

    quarter = expert_weights[0].astype(bfloat)
    quarter_y = across_y(quarter)
    quarter_pair = across_cores(jnp.stack([quarter, quarter_y]))
    quarters = [quarter, quarter_y, quarter_pair[0], quarter_pair[1]]

    mine = lax.dynamic_index_in_dim(patches, micro, 0, keepdims=False)[0]
    theirs = across_y(lax.dynamic_index_in_dim(patches, 1 - micro, 0, keepdims=False)[0])
    patch_rows = jnp.where(
        micro == 0, jnp.concatenate([mine, theirs]), jnp.concatenate([theirs, mine])
    )
    mine = lax.dynamic_index_in_dim(expert_ids, micro, 0, keepdims=False)[0]
    theirs = across_y(lax.dynamic_index_in_dim(expert_ids, 1 - micro, 0, keepdims=False)[0])
    ids = jnp.where(micro == 0, jnp.concatenate([mine, theirs]), jnp.concatenate([theirs, mine]))

    table_t = position_table.T
    table_high = lax.reduce_precision(table_t, 8, 7)
    table_low = (table_t - table_high).astype(bfloat)
    vector_t = vector_params.T
    vector_high = lax.reduce_precision(vector_t, 8, 7)
    vector_low = (vector_t - vector_high).astype(bfloat)
    extra = jnp.concatenate(
        [table_high.astype(bfloat), router_weight.astype(bfloat), vector_high.astype(bfloat), vector_low],
        axis=1,
    )
    square_low = square_weights.astype(bfloat)
    spare = jnp.pad(table_low, ((0, 0), (0, width - PATCHES))).reshape(3, 2, width)
    payload = jnp.concatenate(
        [square_low[0], spare[0], square_low[1], spare[1], square_low[2], spare[2]]
        + [pad_rows(square_low[3]), pad_rows(square_low[4]), pad_rows(extra)],
        axis=0,
    ).reshape(3, 16, width)
    gathered = [part.reshape(-1, 2, PAD, width) for part in gather_all(payload)]
    squares = [gathered[k // 2][:, k % 2, :own_rows].reshape(width, width) for k in range(5)]
    extra = gathered[2][:, 1, :own_rows, :].reshape(width, width)
    low = jnp.stack(
        [gathered[0][:, 0, 6:], gathered[0][:, 1, 6:], gathered[1][:, 0, 6:]], axis=1
    ).reshape(width, width)
    table = (
        extra[:, :PATCHES].astype(jnp.float32) + low[:, :PATCHES].astype(jnp.float32)
    ).T
    router = extra[:, PATCHES : PATCHES + num_expert]
    begin = PATCHES + num_expert
    vectors = (
        extra[:, begin : begin + 10].astype(jnp.float32)
        + extra[:, begin + 10 : begin + 20].astype(jnp.float32)
    ).T
    table_rows = jnp.concatenate(
        [
            lax.dynamic_slice_in_dim(table, core * block, block, 0),
            lax.dynamic_slice_in_dim(table, (2 + core) * block, block, 0),
        ]
    )
    head_low = head_weight.astype(bfloat)
    valid = (label_count > 0).astype(jnp.float32)
    image_count = jnp.sum(valid)
    columns = device_index * vocab_dev + jnp.arange(vocab_dev, dtype=jnp.int32)
    slot_range = jnp.arange(num_expert * 2 * CAP, dtype=jnp.int32)
    expert_range = jnp.arange(num_expert, dtype=jnp.int32)
    label_range = jnp.arange(labels.shape[2], dtype=jnp.int32)

    slot_index = jnp.arange(num_exp * 2 * PAD, dtype=jnp.int32)

    def picker(which):
        first = (slot_index // (num_exp * PAD)) * (2 * num_exp) + which * num_exp
        owner = first + (slot_index % (num_exp * PAD)) // PAD
        inside = slot_index % PAD
        row = jnp.where(inside < own_rows, owner * own_rows + inside, -1)
        return jnp.arange(width, dtype=jnp.int32)[:, None] == row[None, :]

    pick_mine, pick_theirs = picker(core), picker(1 - core)
    pick_mine_low, pick_theirs_low = pick_mine.astype(bfloat), pick_theirs.astype(bfloat)

    def share_left(value):
        theirs = across_cores(plain_dot(value, pick_theirs_low).astype(bfloat))
        return jnp.concatenate([plain_dot(value, pick_mine_low).astype(bfloat), theirs])

    def share_right(value):
        return jnp.concatenate([value, across_cores(value)])

    left_patches = share_left(patch_rows)
    embed = plain_dot(patch_rows, squares[0]) + vectors[0] + table_rows
    norm_one, pull_one = jax.vjp(layer_norm, embed, vectors[1], vectors[2])
    hidden_one = norm_one.astype(bfloat)
    query = (plain_dot(hidden_one, squares[1]) + vectors[3]).astype(bfloat)
    key_rows = plain_dot(hidden_one, squares[2]).astype(bfloat)
    value_rows = (plain_dot(hidden_one, squares[3]) + vectors[4]).astype(bfloat)
    both = jnp.concatenate([key_rows, value_rows], axis=1)
    both_all = jnp.concatenate([both, across_cores(both)])
    left_one = share_left(hidden_one)
    query_h = query.reshape(rows, heads, HEAD)
    key_h = both_all[:, :width].reshape(-1, heads, HEAD)
    value_h = both_all[:, width:].reshape(-1, heads, HEAD)
    scores = jnp.einsum("qhd,khd->hqk", query_h, key_h, preferred_element_type=jnp.float32) * scale
    probs = jax.nn.softmax(scores, axis=-1)
    probs_low = probs.astype(bfloat)
    mixed = jnp.einsum("hqk,khd->qhd", probs_low, value_h, preferred_element_type=jnp.float32)
    mixed = mixed.reshape(rows, width).astype(bfloat)
    left_mixed = share_left(mixed)
    after_attn = embed + plain_dot(mixed, squares[4]) + vectors[5]
    norm_two, pull_two = jax.vjp(layer_norm, after_attn, vectors[6], vectors[7])
    hidden_two = norm_two.astype(bfloat)
    gate_probs = jax.nn.softmax(plain_dot(hidden_two, router), axis=-1)
    chosen = ids[:, :, None] == expert_range[None, None, :]
    chosen_float = chosen.astype(jnp.float32)
    gates = jnp.sum(gate_probs[:, None, :] * chosen_float, axis=-1)
    flat_hit = chosen.reshape(2, block * num_top, num_expert).astype(jnp.int32)
    before = jnp.cumsum(flat_hit, axis=1) - flat_hit
    slot = jnp.sum(before * flat_hit, axis=2) + jnp.array([[0], [CAP]], jnp.int32)
    target = ids.reshape(-1) * (2 * CAP) + slot.reshape(-1)
    placing = (target[:, None] == slot_range[None, :]).astype(bfloat)
    copies = jnp.repeat(hidden_two, num_top, axis=0)
    outgoing = over_rows(placing, copies).astype(bfloat).reshape(num_expert, 2 * CAP, width)
    received = swap_experts(outgoing).reshape(-1, width)
    pre_act = [plain_dot(received, part[0]) for part in quarters]
    act = [jax.nn.gelu(part).astype(bfloat) for part in pre_act]
    result = sum(over_last(left, part[1]) for left, part in zip(act, quarters))
    returned = swap_experts(result.astype(bfloat).reshape(num_expert, 2 * CAP, width))
    gathered_rows = plain_dot(placing, returned.reshape(-1, width)).reshape(rows, num_top, width)
    after_moe = after_attn + jnp.sum(gates[:, :, None] * gathered_rows, axis=1)
    norm_final, pull_final = jax.vjp(layer_norm, after_moe, vectors[8], vectors[9])

    partial_pool = jnp.sum(norm_final, axis=0) / PATCHES
    lanes = jnp.pad(partial_pool, (0, PAD * LANES - width)).reshape(PAD, LANES)
    pooled = gather_pooled(lanes).reshape(2 * num_exp, PAD * LANES)[:, :width].astype(bfloat)
    logits = plain_dot(pooled, head_low)
    label_rows = labels.reshape(2 * num_exp, -1)
    live = label_range[None, :] < label_count.reshape(-1)[:, None]
    targets = jnp.any(
        (label_rows[:, :, None] == columns[None, None, :]) & live[:, :, None], axis=1
    ).astype(jnp.float32)
    valid_rows = valid.reshape(-1)
    loss_part = jnp.sum(valid_rows[:, None] * (jax.nn.softplus(logits) - targets * logits))
    dlogits = (valid_rows[:, None] * (jax.nn.sigmoid(logits) - targets) / image_count).astype(
        bfloat
    )
    head_g = over_rows(pooled, dlogits)
    pool_grad = jnp.pad(over_last(dlogits, head_low), ((0, 0), (0, PAD * LANES - width)))
    my_grad = pull_rows(pool_grad.reshape(2, 4, 2, 4, PAD, LANES)).reshape(-1)[:width] / PATCHES

    dmoe_in, dgain_final, dshift_final = pull_final(jnp.broadcast_to(my_grad, (rows, width)))
    dout_rows = (
        (gates[:, :, None] * dmoe_in[:, None, :]).astype(bfloat).reshape(rows * num_top, width)
    )
    dgates = jnp.sum(dmoe_in[:, None, :] * gathered_rows, axis=-1)
    dsend = over_rows(placing, dout_rows).astype(bfloat).reshape(num_expert, 2 * CAP, width)
    dreceived = swap_experts(dsend).reshape(-1, width)
    dact = [plain_dot(dreceived, part[1]) for part in quarters]
    dpre = [
        jax.vjp(jax.nn.gelu, pre)[1](grad)[0].astype(bfloat) for pre, grad in zip(pre_act, dact)
    ]
    dback = sum(over_last(left, part[0]) for left, part in zip(dpre, quarters))
    dreturn = swap_experts(dback.astype(bfloat).reshape(num_expert, 2 * CAP, width))
    quarter_grads = [
        jnp.stack([over_rows(received, dpre[k]), over_rows(dreceived, act[k])]) for k in range(4)
    ]
    from_core = across_cores(jnp.stack([quarter_grads[2], quarter_grads[3]]))
    from_y = across_y((quarter_grads[1] + from_core[1]).astype(bfloat))
    expert_g = (quarter_grads[0] + from_core[0] + from_y.astype(jnp.float32))[None]

    dcopies = plain_dot(placing, dreturn.reshape(-1, width)).reshape(rows, num_top, width)
    dprobs = jnp.sum(dgates[:, :, None] * chosen_float, axis=1)
    dgate_logits = (
        gate_probs * (dprobs - jnp.sum(gate_probs * dprobs, axis=-1, keepdims=True))
    ).astype(bfloat)
    router_grad = over_rows(hidden_two, dgate_logits)
    dhidden_two = over_last(dgate_logits, router) + jnp.sum(dcopies, axis=1)
    dnorm_two, dgain_two, dshift_two = pull_two(dhidden_two)
    dafter = dmoe_in + dnorm_two
    dafter_low = dafter.astype(bfloat)
    right_after = share_right(dafter_low)

    dmixed = over_last(dafter_low, squares[4]).astype(bfloat).reshape(rows, heads, HEAD)
    dprob = jnp.einsum("qhd,khd->hqk", dmixed, value_h, preferred_element_type=jnp.float32)
    row_shift = jnp.sum(probs * dprob, axis=-1, keepdims=True)
    dscores = (probs * (dprob - row_shift)).astype(bfloat)
    dquery = (
        jnp.einsum("hqk,khd->qhd", dscores, key_h, preferred_element_type=jnp.float32) * scale
    )
    dkey = jnp.einsum("hqk,qhd->khd", dscores, query_h, preferred_element_type=jnp.float32) * scale
    dvalue = jnp.einsum("hqk,qhd->khd", probs_low, dmixed, preferred_element_type=jnp.float32)
    dboth = jnp.concatenate([dkey.reshape(-1, width), dvalue.reshape(-1, width)], axis=1)
    dboth_own = dboth[:rows] + across_cores(dboth[rows:])
    dquery_low = dquery.reshape(rows, width).astype(bfloat)
    dkey_low = dboth_own[:, :width].astype(bfloat)
    dvalue_low = dboth_own[:, width:].astype(bfloat)
    right_qkv = share_right(jnp.concatenate([dquery_low, dkey_low, dvalue_low], axis=1))
    dhidden_one = (
        over_last(dquery_low, squares[1])
        + over_last(dkey_low, squares[2])
        + over_last(dvalue_low, squares[3])
    )
    bias_query = jnp.sum(dquery_low.astype(jnp.float32), axis=0)
    bias_value = jnp.sum(dvalue_low.astype(jnp.float32), axis=0)
    dnorm_one, dgain_one, dshift_one = pull_one(dhidden_one)
    dembed = dafter + dnorm_one
    right_embed = share_right(dembed.astype(bfloat))

    vector_grad = jnp.stack(
        [
            jnp.sum(dembed, axis=0),
            dgain_one,
            dshift_one,
            bias_query,
            bias_value,
            jnp.sum(dafter, axis=0),
            dgain_two,
            dshift_two,
            dgain_final,
            dshift_final,
        ]
    )
    few = jnp.concatenate([vector_grad, router_grad.T], axis=0)
    few = few + across_cores(few)
    pick_float = pick_mine.astype(jnp.float32)
    few_t = lax.dot_general(
        pick_float, few, (((0,), (1,)), ((), ())), precision=HIGHEST, preferred_element_type=jnp.float32
    )
    table_mine, table_theirs = (
        lax.dot_general(
            pick.astype(jnp.float32),
            dembed,
            (((0,), (1,)), ((), ())),
            precision=HIGHEST,
            preferred_element_type=jnp.float32,
        )
        for pick in (pick_mine, pick_theirs)
    )
    table_theirs = across_cores(table_theirs)
    extra_grad = jnp.concatenate(
        [
            jnp.where(core == 0, table_mine, table_theirs),
            jnp.where(core == 0, table_theirs, table_mine),
            few_t,
            jnp.zeros((few_t.shape[0], width - PATCHES - few_t.shape[1]), jnp.float32),
        ],
        axis=1,
    )
    shared = [
        over_rows(left_patches, right_embed),
        over_rows(left_one, right_qkv[:, :width]),
        over_rows(left_one, right_qkv[:, width : 2 * width]),
        over_rows(left_one, right_qkv[:, 2 * width :]),
        over_rows(left_mixed, right_after),
        extra_grad,
    ]
    owned = scatter_all([part.reshape(2, 4, 2, 4, PAD, width) for part in shared])
    square_g = jnp.stack([part[:own_rows] for part in owned[:5]])
    extra_g = owned[5][:own_rows]
    table_g = extra_g[:, :PATCHES].reshape(own_rows, 2, 2, block)
    table_g = table_g.transpose(0, 2, 1, 3).reshape(own_rows, PATCHES).T
    vector_g = extra_g[:, PATCHES : PATCHES + 10].T
    router_g = extra_g[:, PATCHES + 10 : PATCHES + 10 + num_expert]
    norm_part = (
        jnp.sum(square_g * square_g)
        + jnp.sum(router_g * router_g)
        + jnp.sum(table_g * table_g)
        + jnp.sum(vector_g * vector_g)
        + jnp.sum(head_g * head_g)
        + jnp.sum(expert_g * expert_g)
    )
    square_rowmean = jnp.mean(square_g * square_g, axis=2)
    router_rowmean = jnp.mean(router_g * router_g, axis=1)
    expert_rowsq = jnp.sum(expert_g * expert_g, axis=-1)
    expert_rowsq = expert_rowsq + across_cores(expert_rowsq)
    expert_mine = expert_rowsq + across_y(expert_rowsq)
    terms = (
        loss_part,
        norm_part,
        jnp.sum(square_g * square_g, axis=1),
        jnp.sum(square_rows, axis=1),
        jnp.sum(square_rowmean, axis=1),
        jnp.sum(router_g * router_g, axis=0),
        jnp.sum(router_rows),
        jnp.sum(router_rowmean),
        jnp.sum(table_g * table_g, axis=1),
        jnp.sum(head_g * head_g, axis=1),
    )
    flat = jnp.concatenate([term.reshape(-1) for term in terms])
    length = flat.shape[0]
    padded = -(-length // (8 * LANES)) * 8 * LANES
    flat = total_all(jnp.pad(flat, (0, padded - length)).reshape(-1, LANES)).reshape(-1)
    totals = []
    begin = 0
    for term in terms:
        totals.append(flat[begin : begin + term.size].reshape(term.shape))
        begin += term.size
    (
        loss_total,
        norm_total,
        square_colsq,
        square_rows_sum,
        square_mean_sum,
        router_colsq,
        router_rows_sum,
        router_mean_sum,
        table_rowsq,
        head_rowsq,
    ) = totals
    grad_norm = jnp.sqrt(norm_total)
    clip = jnp.minimum(1.0, CLIP_NORM / grad_norm)
    clip_sq = clip * clip
    keep = 1.0 - DECAY
    square_clip = clip * square_g
    square_rows_next = DECAY * square_rows + keep * (clip_sq * square_rowmean + EPS_SQ)
    square_cols_next = DECAY * square_cols + keep * (clip_sq * square_colsq / width + EPS_SQ)
    square_mean = (
        DECAY * square_rows_sum + keep * (clip_sq * square_mean_sum + width * EPS_SQ)
    ) / width
    square_rate = jnp.array([1.0, 1.0, 1.0, 1.0, 4.0], jnp.float32)[:, None, None] * (
        0.3 / math.sqrt(D)
    )
    square_next = factored_step(
        square_weights,
        square_clip,
        square_rows_next,
        square_cols_next,
        square_mean[:, None, None],
        square_rate,
    )
    router_clip = clip * router_g
    router_rows_next = DECAY * router_rows + keep * (clip_sq * router_rowmean + EPS_SQ)
    router_cols_next = DECAY * router_cols + keep * (clip_sq * router_colsq / width + EPS_SQ)
    router_mean = (
        DECAY * router_rows_sum + keep * (clip_sq * router_mean_sum + width * EPS_SQ)
    ) / width
    router_next = factored_step(
        router_weight,
        router_clip,
        router_rows_next,
        router_cols_next,
        router_mean,
        0.2 / math.sqrt(D),
    )
    table_clip = clip * table_g
    table_rows_next = DECAY * position_rows + keep * (clip_sq * table_rowsq / width + EPS_SQ)
    table_cols_next = DECAY * position_cols + keep * (
        clip_sq * jnp.mean(table_g * table_g, axis=0) + EPS_SQ
    )
    table_next = factored_step(
        position_table,
        table_clip,
        table_rows_next,
        table_cols_next,
        jnp.mean(table_rows_next),
        0.15,
    )
    head_clip = clip * head_g
    head_rows_next = DECAY * head_rows + keep * (
        clip_sq * head_rowsq / (vocab_dev * num_rep * num_exp) + EPS_SQ
    )
    head_cols_next = DECAY * head_cols + keep * (
        clip_sq * jnp.mean(head_g * head_g, axis=0) + EPS_SQ
    )
    head_next = factored_step(
        head_weight,
        head_clip,
        head_rows_next,
        head_cols_next,
        jnp.mean(head_rows_next),
        0.5 / math.sqrt(D),
    )
    expert_clip = clip * expert_g
    expert_rows_next = DECAY * expert_rows + keep * (
        clip_sq * expert_mine / (ff_dev * num_rep) + EPS_SQ
    )
    expert_cols_next = DECAY * expert_cols + keep * (
        clip_sq * jnp.mean(expert_g * expert_g, axis=2) + EPS_SQ
    )
    expert_rate = jnp.array([0.3 / math.sqrt(D), 4.8 / math.sqrt(FF)], jnp.float32)[
        None, :, None, None
    ]
    expert_next = factored_step(
        expert_weights,
        expert_clip,
        expert_rows_next,
        expert_cols_next,
        jnp.mean(expert_rows_next, axis=-1)[..., None, None],
        expert_rate,
    )
    vector_clip = clip * vector_g
    moment_next = DECAY * vector_moment + keep * (vector_clip * vector_clip + EPS_SQ)
    vector_next = vector_params - 0.3 * vector_clip * lax.rsqrt(moment_next)
    return (
        loss_total,
        image_count,
        grad_norm,
        square_clip,
        square_rows_next,
        square_cols_next,
        square_next,
        router_clip,
        router_rows_next,
        router_cols_next,
        router_next,
        table_clip,
        table_rows_next,
        table_cols_next,
        table_next,
        head_clip,
        head_rows_next,
        head_cols_next,
        head_next,
        expert_clip,
        expert_rows_next,
        expert_cols_next,
        expert_next,
        vector_clip,
        moment_next,
        vector_next,
    )


def solution(mesh):
    in_specs = (
        P(None, "exp", "rep", None),
        P(None, "exp", "rep", None),
        P(),
        P(),
        P(None, ("rep", "exp"), None),
        P(("rep", "exp"), None),
        P(None, ("rep", "exp")),
        P(None, ("rep", "exp")),
        P("exp", None, None, "rep"),
        P(None, ("rep", "exp")),
        P(None, ("rep", "exp")),
        P(),
        P(("rep", "exp")),
        P(),
        P(),
        P(("rep", "exp")),
        P(),
        P(("rep", "exp")),
        P("exp", None, None),
        P("exp", None, "rep"),
        P(None, ("rep", "exp")),
    )
    out_specs = (
        P(),
        P(),
        P(),
        P(None, ("rep", "exp"), None),
        P(None, ("rep", "exp")),
        P(),
        P(None, ("rep", "exp"), None),
        P(("rep", "exp"), None),
        P(("rep", "exp")),
        P(),
        P(("rep", "exp"), None),
        P(None, ("rep", "exp")),
        P(),
        P(("rep", "exp")),
        P(None, ("rep", "exp")),
        P(None, ("rep", "exp")),
        P(),
        P(("rep", "exp")),
        P(None, ("rep", "exp")),
        P("exp", None, None, "rep"),
        P("exp", None, None),
        P("exp", None, "rep"),
        P("exp", None, None, "rep"),
        P(None, ("rep", "exp")),
        P(None, ("rep", "exp")),
        P(None, ("rep", "exp")),
    )
    return jax.shard_map(shards, mesh=mesh, in_specs=in_specs, out_specs=out_specs, check_vma=False)
```

time: 2740 us -> 732 us (0.27)
  blocking collectives: 1340 us -> 0 us
  waiting for transfers between devices: 953 us -> 1.89 us
  Pallas kernels: 0 us -> 341 us
    all_gather x8 -> x0, blocking collectives: 1170 us -> none  [the longest x2 559 us: micro_pass(): lax.all_gather(partial_pool[None, :], ('rep', 'exp'), axis=0, tiled=True)]
    pallas_call x0 -> x9, Pallas kernels: none -> 341 us  [the longest x4 104 us: swap_experts(): pl.pallas_call(functools.partial(swap_kernel, count), out_shape=jax.Shape...]
    reduce_scatter x6 -> x0, waiting for transfers between devices: 339 us -> none  [the longest x2 264 us: reduce_experts(): return lax.psum_scatter(value, 'rep', scatter_dimension=2, tiled=True)]
    psum x2 -> x0, waiting for transfers between devices: 335 us -> none  [micro_pass(): pool_grad = lax.psum(over_last(dlogits, head_low), ('rep', 'exp'))]
    all_gather x3 -> x0, waiting for transfers between devices: 111 us -> none  [the longest x1 63.2 us: shards(): lax.all_gather(expert_weights.astype(bfloat), 'rep', axis=3, tiled=True)[0]]
    unnamed x5 -> x0, waiting for transfers between devices: 102 us -> none
    unnamed x1 -> x0, blocking collectives: 68.2 us -> none
    psum x1 -> x0, blocking collectives: 65.7 us -> none  [shards(): lax.psum((result[0], norm_part, jnp.sum(square_g * square_g, axis=1), jnp...]
  transfers between devices with their start and end apart: 18 -> 18, of which waited for: 16 -> 1; matrix products, arithmetic and copies ran while one was open for 5% -> 42% of each run, Pallas kernels for 0% -> 45%
where the time goes in v1:
time: 732 us; the launch traced here: 726 us
  Pallas kernels  341 us (47%)
  matrix products  147 us (20%)
  local copies, waits for them, and re-layouts  111 us (15%)
  other arithmetic  96 us (13%)
  starting transfers between devices  17.6 us (2%)
  between operations  11.8 us (2%)
    pallas_call x4, Pallas kernels, swap_experts(): pl.pallas_call(functools.partial(swap_kernel, count), out_shape=jax.Shape...  104 us
    pallas_call x1, Pallas kernels, scatter_all(): pl.pallas_call(scatter_kernel, out_shape=[jax.ShapeDtypeStruct(block, jnp...  96.7 us
    pallas_call x1, Pallas kernels, gather_all(): pl.pallas_call(gather_kernel, out_shape=[jax.ShapeDtypeStruct(shape, payl...  82.8 us
    dot_general x23, matrix products, plain_dot(): return jnp.dot(left, right, preferred_element_type=jnp.float32)  43.9 us
    dot_general x17, matrix products, over_rows(): lax.dot_general(left, right, (((0,), (0,)), ((), ())), preferred_element_...  43.8 us
    dot_general x14, matrix products, over_last(): lax.dot_general(left, right, (((1,), (1,)), ((), ())), preferred_element_...  25.7 us
    unnamed x349, local copies, waits for them, and re-layouts  23 us
    pallas_call x1, Pallas kernels, gather_pooled(): pl.pallas_call(pool_kernel, out_shape=jax.ShapeDtypeStruct((2, 4, 2, 4) +...  21.9 us
  transfers between devices with their start and end apart: 18, of which 1 were waited for; matrix products, arithmetic and copies ran while one was open for 42% of the time, Pallas kernels for 45%

profile of v1, /device:TPU:1, one launch (start us, length us, event | category | flops | bytes accessed | tf_op | source)
XLA Modules:
  0.0 726.4 jit_solution(12298200131608117799)
XLA Ops:
  2.6 3.7 collective-permute-start
  7.7 4.0 convert_bitcast_fusion.1
  11.7 3.0 collective-permute-start.3
  15.5 3.7 concatenate.81
  19.2 82.8 %gather_weights.1 = (bf16[2,2,4,2,4,16,768]{6,5,4,3,2,1,0:T(8,128)(2,1)}, bf16[2,2,4,2,4,16,768]{6,5,4,3,2,1,0:T(8,128)(2,1)}, bf16[2,2,4,2,4,16,768]{6,5,4,3,2,1,0:T(8,128)(2,1)}) custom-call(bf16[3,16,768]{2,1,0:T(8,128)(2,1)} %bitcast.339), custom_call_target="tpu_custom_call" | custom-call | tf_op jit(solution)/shard_map/gather_weights/pallas_call | solution.py:163
  102.0 3.3 slice_bitcast_fusion.2
  106.1 2.9 slice.337
  109.1 3.8 slice_bitcast_fusion.3
  114.7 3.8 slice_bitcast_fusion.5
  135.6 3.3 reshape_squeeze.18
  138.9 3.2 reshape_squeeze.21
  142.1 3.2 reshape_squeeze.20
  145.3 3.2 reshape_squeeze.22
  148.6 3.3 reshape_squeeze.23
  182.5 7.8 %fusion.235 = (f32[12,288]{1,0:T(8,128)S(1)}, f32[12,288,576]{2,1,0:T(8,128)}) fusion(bf16[288,12,64]{0,2,1:T(8,128)(2,1)} %bitcast.325, bf16[576,12,64]{0,2,1:T(8,128)(2,1)} %bitcast.322), kind=kOutput, calls=%fused_computation.456 | convolution fusion | flops 260776512 | bytes 9303552 | tf_op jit(solution)/shard_map/sub | solution.py:592
  190.3 4.6 pad_maximum_fusion.1
  196.2 2.9 fusion.66
  205.7 24.3 %swap_experts.4 = bf16[32,20,768]{2,1,0:T(8,128)(2,1)} custom-call(bf16[32,20,768]{2,1,0:T(8,128)(2,1)} %reshape.633.x_ref), custom_call_target="tpu_custom_call" | custom-call | tf_op jit(solution)/shard_map/swap_experts/pallas_call | solution.py:433
  243.6 3.3 fusion.86
  249.2 2.9 fusion.92
  252.1 3.3 fusion.90
  259.4 27.8 %swap_experts.5 = bf16[32,20,768]{2,1,0:T(8,128)(2,1)} custom-call(bf16[32,20,768]{2,1,0:T(8,128)(2,1)} %reshape.635.x_ref), custom_call_target="tpu_custom_call" | custom-call | tf_op jit(solution)/shard_map/swap_experts/pallas_call | solution.py:433
  292.4 21.9 %gather_pooled.1 = f32[2,4,2,4,8,128]{5,4,3,2,1,0:T(8,128)} custom-call(f32[8,128]{1,0:T(8,128)} %pad_bitcast_fusion.2.x_ref), custom_call_target="tpu_custom_call" | custom-call | tf_op jit(solution)/shard_map/gather_pooled/pallas_call | solution.py:296
  318.6 18.4 %pull_rows.1 = f32[8,128]{1,0:T(8,128)} custom-call(f32[2,4,2,4,8,128]{5,4,3,2,1,0:T(8,128)} %bitcast.328), custom_call_target="tpu_custom_call" | custom-call | tf_op jit(solution)/shard_map/pull_rows/pallas_call | solution.py:339
  343.6 3.4 mul.1020
  347.0 3.7 fusion.61
  352.9 20.1 %swap_experts.6 = bf16[32,20,768]{2,1,0:T(8,128)(2,1)} custom-call(bf16[32,20,768]{2,1,0:T(8,128)(2,1)} %reshape.641.x_ref), custom_call_target="tpu_custom_call" | custom-call | tf_op jit(solution)/shard_map/swap_experts/pallas_call | solution.py:433
  375.3 4.1 fusion.19
  385.9 3.2 fusion.33
  391.7 3.1 fusion.40
  399.7 3.5 fusion.26
  406.5 3.2 add_convert_fusion
  411.8 32.0 %swap_experts.7 = bf16[32,20,768]{2,1,0:T(8,128)(2,1)} custom-call(bf16[32,20,768]{2,1,0:T(8,128)(2,1)} %reshape.643.x_ref), custom_call_target="tpu_custom_call" | custom-call | tf_op jit(solution)/shard_map/swap_experts/pallas_call | solution.py:433
  457.0 7.5 %multiply_reduce_fusion = (f32[12,288]{1,0:T(8,128)}, f32[12,288,576]{2,1,0:T(8,128)}) fusion(f32[12,288,576]{2,1,0:T(8,128)} %get-tuple-element.143, f32[12,288]{1,0:T(8,128)S(1)} %copy-done.94, bf16[288,12,64]{0,2,1:T(8,128)(2,1)S(1)} %bitcast.331, bf16[576,12,64]{0,2,1:T(8,128)(2,1)S(1)} %bitcast.330), kind=kOutput, calls=%fused_computation.3 | convolution fusion | flops 260772480 | bytes 17280000 | tf_op jit(solution)/shard_map/qhd,khd->hqk/dot_general | solution.py:671
  464.5 3.3 maximum_bitcast_fusion
  467.8 4.3 pad_maximum_fusion
  472.8 5.9 fusion.9
  480.7 7.0 multiply_convert_fusion
  490.4 2.8 copy.166
  496.5 4.1 convert_reduce_fusion
  512.2 4.2 convolution_bitcast_fusion.1
  540.6 3.0 fusion.103
  552.0 4.2 fusion.5
  561.8 96.7 %scatter_grads.1 = (f32[8,768]{1,0:T(8,128)S(1)}, f32[8,768]{1,0:T(8,128)S(1)}, f32[8,768]{1,0:T(8,128)S(1)}, f32[8,768]{1,0:T(8,128)S(1)}, f32[8,768]{1,0:T(8,128)S(1)}, /*index=5*/f32[8,768]{1,0:T(8,128)S(1)}) custom-call(f32[2,4,2,4,8,768]{5,4,3,2,1,0:T(8,128)S(1)} %bitcast.311, f32[2,4,2,4,8,768]{5,4,3,2,1,0:T(8,128)S(1)} %bitcast.312, ...), custom_call_target="tpu_custom_call" | custom-call | tf_op jit(solution)/shard_map/scatter_grads/pallas_call | solution.py:259
  665.4 7.8 %multiply_reduce_fusion.2 = (f32[2,768]{1,0:T(2,128)S(1)}, f32[2,768]{1,0:T(2,128)S(1)}, f32[]{:T(128)}, f32[2,768,768]{2,1,0:T(8,128)}) fusion(bf16[2,768,768]{2,1,0:T(8,128)(2,1)} %collective-permute-done.15, f32[2,2,768,768]{3,2,1,0:T(8,128)} %collective-permute-done.14, f32[1,768,768]{2,1,0:T(8,128)} %convolution_bitcast_fusion.6, ...), kind=kLoop, calls=%fused_computation.21 | loop fusion | flops 9434111 | bytes 16527364 | tf_op jit(solution)/shard_map/reduce_sum | solution.py:865
  676.4 17.4 %total_all.1 = f32[48,128]{1,0:T(8,128)} custom-call(f32[48,128]{1,0:T(8,128)} %pad_bitcast_fusion.1.x_ref), custom_call_target="tpu_custom_call" | custom-call | tf_op jit(solution)/shard_map/total_all/pallas_call | solution.py:388
  702.8 4.9 multiply_bitcast_fusion
  719.2 5.8 bitcast_subtract_fusion
  (605 shorter events, 214.9 us)
Async XLA Ops:
  2.6 156.2 %collective-permute-start = (bf16[144,768]{1,0:T(8,128)(2,1)}, bf16[144,768]{1,0:T(8,128)(2,1)}, u32[]{:S(2)}, u32[]{:S(2)}) collective-permute-start(bf16[144,768]{1,0:T(8,128)(2,1)} %get-tuple-element.118), channel_id=1, source_target_pairs={{0,64},{32,96},{64,0},{96,32},{1,65},{33,97},{65,1},{97,33},{2,66}... | collective-permute-start | bytes 663560 | tf_op jit(solution)/shard_map/ppermute | solution.py:453
  7.6 146.4 %collective-permute-start.2 = (s32[144,2]{0,1:T(2,128)}, s32[144,2]{0,1:T(2,128)}, u32[]{:S(2)}, u32[]{:S(2)}) collective-permute-start(s32[144,2]{0,1:T(2,128)} %get-tuple-element.137), channel_id=1, source_target_pairs={{0,64},{32,96},{64,0},{96,32},{1,65},{33,97},{65,1},{97,33},{2,66}... | collective-permute-start | bytes 3464 | tf_op jit(solution)/shard_map/ppermute | solution.py:453
  11.7 178.6 %collective-permute-start.3 = (bf16[2,768,768]{2,1,0:T(8,128)(2,1)}, bf16[2,768,768]{2,1,0:T(8,128)(2,1)}, u32[]{:S(2)}, u32[]{:S(2)}) collective-permute-start(bf16[2,768,768]{2,1,0:T(8,128)(2,1)} %convert_bitcast_fusion.1), channel_id=1, source_target_pairs={{0,64},{32,96},{64,0},{96,32},{1,65},{33,97},{65,1},{97,33},{2,66}... | collective-permute-start | bytes 7077896 | tf_op jit(solution)/shard_map/ppermute | solution.py:453
  134.9 55.4 %copy-start.5 = (bf16[1,2,768,768]{3,2,1,0:T(8,128)(2,1)}, bf16[1,2,768,768]{3,2,1,0:T(8,128)(2,1)S(1)}, u32[]{:S(2)}) copy-start(bf16[1,2,768,768]{3,2,1,0:T(8,128)(2,1)S(1)} %convert_element_type.225) | copy-start | bytes 7077892
  148.6 10.2 %copy-start.59 = (bf16[144,768]{1,0:T(8,128)(2,1)S(1)}, bf16[144,768]{1,0:T(8,128)(2,1)}, u32[]{:S(2)}) copy-start(bf16[144,768]{1,0:T(8,128)(2,1)} %get-tuple-element.117) | copy-start | bytes 663556
  148.6 10.2 %copy-start.138 = (f32[768]{0:T(1024)S(1)}, f32[768]{0:T(1024)}, u32[]{:S(2)}) copy-start(f32[768]{0:T(1024)} %get-tuple-element.67) | copy-start | bytes 9220
  158.3 74.9 %copy-start.80 = (s32[288,2]{0,1:T(2,128)}, s32[288,2]{0,1:T(2,128)S(1)}, u32[]{:S(2)}) copy-start(s32[288,2]{0,1:T(2,128)S(1)} %get-tuple-element.104) | copy-start | bytes 6916
  158.3 130.3 %copy-start.122 = (s32[288,2]{0,1:T(2,128)}, s32[288,2]{0,1:T(2,128)S(1)}, u32[]{:S(2)}) copy-start(s32[288,2]{0,1:T(2,128)S(1)} %get-tuple-element.103) | copy-start | bytes 6916
  158.7 43.5 %copy-start.133 = (s32[576]{0:T(1024)}, s32[576]{0:T(1024)S(1)}, u32[]{:S(2)}) copy-start(s32[576]{0:T(1024)S(1)} %add.562) | copy-start | bytes 6916
  164.6 10.7 %collective-permute-start.1 = (bf16[288,1536]{1,0:T(8,128)(2,1)}, bf16[288,1536]{1,0:T(8,128)(2,1)}, u32[]{:S(2)}, u32[]{:S(2)}) collective-permute-start(bf16[288,1536]{1,0:T(8,128)(2,1)} %pad_maximum_fusion.7), channel_id=1, source_target_pairs={{0,32},{32,0},{64,96},{96,64},{1,33},{33,1},{65,97},{97,65},{2,34}... | collective-permute-start | bytes 2654216 | tf_op jit(solution)/shard_map/ppermute | solution.py:449
  194.9 52.0 %collective-permute-start.4 = (bf16[2,2,768,768]{3,2,1,0:T(8,128)(2,1)}, bf16[2,2,768,768]{3,2,1,0:T(8,128)(2,1)}, u32[]{:S(2)}, u32[]{:S(2)}) collective-permute-start(bf16[2,2,768,768]{3,2,1,0:T(8,128)(2,1)} %pad_maximum_fusion.1), channel_id=1, source_target_pairs={{0,32},{32,0},{64,96},{96,64},{1,33},{33,1},{65,97},{97,65},{2,34}... | collective-permute-start | bytes 14155784 | tf_op jit(solution)/shard_map/ppermute | solution.py:449
  200.4 31.7 %copy-start.13 = (bf16[288,768]{1,0:T(8,128)(2,1)}, bf16[288,768]{1,0:T(8,128)(2,1)S(1)}, u32[]{:S(2)}) copy-start(bf16[288,768]{1,0:T(8,128)(2,1)S(1)} %add_convert_fusion.2) | copy-start | bytes 1327108
  205.7 26.4 %copy-start.10 = (bf16[768,768]{1,0:T(8,128)(2,1)S(1)}, bf16[768,768]{1,0:T(8,128)(2,1)}, u32[]{:S(2)}) copy-start(bf16[768,768]{1,0:T(8,128)(2,1)} %copy-done.9) | copy-start | bytes 3538948
  236.5 297.5 %collective-permute-start.10 = (bf16[288,512]{1,0:T(8,128)(2,1)}, bf16[288,512]{1,0:T(8,128)(2,1)}, u32[]{:S(2)}, u32[]{:S(2)}) collective-permute-start(bf16[288,512]{1,0:T(8,128)(2,1)} %fusion.78), channel_id=1, source_target_pairs={{0,32},{32,0},{64,96},{96,64},{1,33},{33,1},{65,97},{97,65},{2,34}... | collective-permute-start | bytes 884744 | tf_op jit(solution)/shard_map/ppermute | solution.py:449
  291.1 24.3 %copy-start.15 = (f32[768,171]{0,1:T(8,128)S(1)}, f32[768,171]{0,1:T(8,128)}, u32[]{:S(2)}) copy-start(f32[768,171]{0,1:T(8,128)} %param.31) | copy-start | bytes 1575940
  291.1 24.3 %copy-start.144 = (f32[64]{0:T(128)S(1)}, f32[64]{0:T(128)}, u32[]{:S(2)}) copy-start(f32[64]{0:T(128)} %mul.947) | copy-start | bytes 772
  291.1 48.1 %copy-start.62 = (f32[288]{0:T(512)}, f32[288]{0:T(512)S(1)}, u32[]{:S(2)}) copy-start(f32[288]{0:T(512)S(1)} %broadcast_multiply_fusion.4) | copy-start | bytes 3460
  291.4 47.9 %copy-start.72 = (f32[288]{0:T(512)}, f32[288]{0:T(512)S(1)}, u32[]{:S(2)}) copy-start(f32[288]{0:T(512)S(1)} %fusion.202) | copy-start | bytes 3460
  472.0 79.9 %collective-permute-start.14 = (f32[2,2,768,768]{3,2,1,0:T(8,128)}, f32[2,2,768,768]{3,2,1,0:T(8,128)}, u32[]{:S(2)}, u32[]{:S(2)}) collective-permute-start(f32[2,2,768,768]{3,2,1,0:T(8,128)} %pad_maximum_fusion), channel_id=1, source_target_pairs={{0,32},{32,0},{64,96},{96,64},{1,33},{33,1},{65,97},{97,65},{2,34}... | collective-permute-start | bytes 28311560 | tf_op jit(solution)/shard_map/ppermute | solution.py:449
  478.7 55.9 %collective-permute-start.11 = (bf16[288,768]{1,0:T(8,128)(2,1)}, bf16[288,768]{1,0:T(8,128)(2,1)}, u32[]{:S(2)}, u32[]{:S(2)}) collective-permute-start(bf16[288,768]{1,0:T(8,128)(2,1)} %convert_element_type.245), channel_id=1, source_target_pairs={{0,32},{32,0},{64,96},{96,64},{1,33},{33,1},{65,97},{97,65},{2,34}... | collective-permute-start | bytes 1327112 | tf_op jit(solution)/shard_map/ppermute | solution.py:449
  496.0 29.6 %collective-permute-start.6 = (f32[288,1536]{1,0:T(8,128)}, f32[288,1536]{1,0:T(8,128)}, u32[]{:S(2)}, u32[]{:S(2)}) collective-permute-start(f32[288,1536]{1,0:T(8,128)} %pad_maximum_fusion.3), channel_id=1, source_target_pairs={{0,32},{32,0},{64,96},{96,64},{1,33},{33,1},{65,97},{97,65},{2,34}... | collective-permute-start | bytes 5308424 | tf_op jit(solution)/shard_map/ppermute | solution.py:449
  530.6 10.1 %collective-permute-start.7 = (bf16[288,768]{1,0:T(8,128)(2,1)S(1)}, bf16[288,768]{1,0:T(8,128)(2,1)}, u32[]{:S(2)}, u32[]{:S(2)}) collective-permute-start(bf16[288,768]{1,0:T(8,128)(2,1)S(1)} %convert_element_type.251), channel_id=1, source_target_pairs={{0,32},{32,0},{64,96},{96,64},{1,33},{33,1},{65,97},{97,65},{2,34}... | collective-permute-start | bytes 1327112 | tf_op jit(solution)/shard_map/ppermute | solution.py:449
  532.4 15.6 %collective-permute-start.9 = (bf16[288,2304]{1,0:T(8,128)(2,1)}, bf16[288,2304]{1,0:T(8,128)(2,1)}, u32[]{:S(2)}, u32[]{:S(2)}) collective-permute-start(bf16[288,2304]{1,0:T(8,128)(2,1)} %pad_maximum_fusion.5), channel_id=1, source_target_pairs={{0,32},{32,0},{64,96},{96,64},{1,33},{33,1},{65,97},{97,65},{2,34}... | collective-permute-start | bytes 3981320 | tf_op jit(solution)/shard_map/ppermute | solution.py:449
  534.1 3.0 collective-permute-start.13
  534.6 9.1 %collective-permute-start.12 = (f32[512,288]{0,1:T(8,128)S(1)}, f32[512,288]{0,1:T(8,128)S(1)}, u32[]{:S(2)}, u32[]{:S(2)}) collective-permute-start(f32[512,288]{0,1:T(8,128)S(1)} %fusion.44), channel_id=1, source_target_pairs={{0,32},{32,0},{64,96},{96,64},{1,33},{33,1},{65,97},{97,65},{2,34}... | collective-permute-start | bytes 1769480 | tf_op jit(solution)/shard_map/ppermute | solution.py:449
  537.1 3.3 collective-permute-start.5
  540.5 9.6 %collective-permute-start.8 = (bf16[288,512]{1,0:T(8,128)(2,1)S(1)}, bf16[288,512]{1,0:T(8,128)(2,1)}, u32[]{:S(2)}, u32[]{:S(2)}) collective-permute-start(bf16[288,512]{1,0:T(8,128)(2,1)S(1)} %copy-done.155), channel_id=1, source_target_pairs={{0,32},{32,0},{64,96},{96,64},{1,33},{33,1},{65,97},{97,65},{2,34}... | collective-permute-start | bytes 884744 | tf_op jit(solution)/shard_map/ppermute | solution.py:449
  556.2 109.2 %collective-permute-start.15 = (bf16[2,768,768]{2,1,0:T(8,128)(2,1)}, bf16[2,768,768]{2,1,0:T(8,128)(2,1)}, u32[]{:S(2)}, u32[]{:S(2)}) collective-permute-start(bf16[2,768,768]{2,1,0:T(8,128)(2,1)} %fusion.5), channel_id=1, source_target_pairs={{0,64},{32,96},{64,0},{96,32},{1,65},{33,97},{65,1},{97,33},{2,66}... | collective-permute-start | bytes 7077896 | tf_op jit(solution)/shard_map/ppermute | solution.py:453
  665.3 32.2 %copy-start.106 = (f32[5,6]{1,0:T(8,128)S(1)}, f32[5,6]{1,0:T(8,128)}, u32[]{:S(2)}) copy-start(f32[5,6]{1,0:T(8,128)} %param.34) | copy-start | bytes 364
  665.3 32.2 %copy-start.151 = (f32[32]{0:T(128)S(1)}, f32[32]{0:T(128)}, u32[]{:S(2)}) copy-start(f32[32]{0:T(128)} %param.37) | copy-start | bytes 388
  665.4 33.2 %copy-start.134 = (f32[576]{0:T(1024)S(1)}, f32[576]{0:T(1024)}, u32[]{:S(2)}) copy-start(f32[576]{0:T(1024)} %param.38) | copy-start | bytes 6916
  665.4 35.3 %copy-start.135 = (f32[768]{0:T(1024)S(1)}, f32[768]{0:T(1024)}, u32[]{:S(2)}) copy-start(f32[768]{0:T(1024)} %param.40) | copy-start | bytes 9220
  697.6 13.4 %copy-start.102 = (f32[5,6]{1,0:T(8,128)}, f32[5,6]{1,0:T(8,128)S(1)}, u32[]{:S(2)}) copy-start(f32[5,6]{1,0:T(8,128)S(1)} %multiply_add_fusion.3) | copy-start | bytes 364
  698.4 18.1 %copy-start.141 = (f32[32]{0:T(128)}, f32[32]{0:T(128)S(1)}, u32[]{:S(2)}) copy-start(f32[32]{0:T(128)S(1)} %fusion.208) | copy-start | bytes 388
  698.6 13.2 %copy-start.67 = (f32[6,576]{1,0:T(8,128)}, f32[6,576]{1,0:T(8,128)S(1)}, u32[]{:S(2)}) copy-start(f32[6,576]{1,0:T(8,128)S(1)} %mul.1140) | copy-start | bytes 41476
  700.0 11.8 %copy-start.109 = (f32[576]{0:T(1024)}, f32[576]{0:T(1024)S(1)}, u32[]{:S(2)}) copy-start(f32[576]{0:T(1024)S(1)} %get-tuple-element.87) | copy-start | bytes 6916
  702.0 10.4 %copy-start.104 = (f32[768]{0:T(1024)}, f32[768]{0:T(1024)S(1)}, u32[]{:S(2)}) copy-start(f32[768]{0:T(1024)S(1)} %get-tuple-element.85) | copy-start | bytes 9220
  702.8 9.7 %copy-start.16 = (f32[768,171]{0,1:T(8,128)S(1)}, f32[768,171]{0,1:T(8,128)}, u32[]{:S(2)}) copy-start(f32[768,171]{0,1:T(8,128)} %param.31) | copy-start | bytes 1575940
  702.8 9.7 %copy-start.48 = (f32[768,171]{0,1:T(8,128)S(1)}, f32[768,171]{0,1:T(8,128)}, u32[]{:S(2)}) copy-start(f32[768,171]{0,1:T(8,128)} %get-tuple-element.158) | copy-start | bytes 1575940
  707.7 11.3 %copy-start.130 = (f32[1,2,768]{2,1,0:T(2,128)S(1)}, f32[1,2,768]{2,1,0:T(2,128)}, u32[]{:S(2)}) copy-start(f32[1,2,768]{2,1,0:T(2,128)} %param.42) | copy-start | bytes 18436
  707.7 11.4 %copy-start.149 = (f32[2]{0:T(128)S(1)}, f32[2]{0:T(128)}, u32[]{:S(2)}) copy-start(f32[2]{0:T(128)} %constant.282.clone) | copy-start | bytes 28
  707.7 7.2 collective-permute-start.16
  710.8 14.1 %copy-start.64 = (f32[5,768]{1,0:T(8,128)}, f32[5,768]{1,0:T(8,128)S(1)}, u32[]{:S(2)}) copy-start(f32[5,768]{1,0:T(8,128)S(1)} %multiply_add_fusion) | copy-start | bytes 46084
  710.9 14.1 %copy-start.131 = (f32[171]{0:T(256)}, f32[171]{0:T(256)S(1)}, u32[]{:S(2)}) copy-start(f32[171]{0:T(256)S(1)} %multiply_add_fusion.7) | copy-start | bytes 2056
  710.9 14.0 %copy-start.91 = (f32[1,2,768]{2,1,0:T(2,128)}, f32[1,2,768]{2,1,0:T(2,128)S(1)}, u32[]{:S(2)}) copy-start(f32[1,2,768]{2,1,0:T(2,128)S(1)} %bitcast_add_fusion) | copy-start | bytes 18436
  711.0 14.0 %copy-start.140 = (f32[6]{0:T(128)}, f32[6]{0:T(128)S(1)}, u32[]{:S(2)}) copy-start(f32[6]{0:T(128)S(1)} %multiply_add_fusion.8) | copy-start | bytes 76
  713.6 11.4 %copy-start.142 = (f32[6]{0:T(128)}, f32[6]{0:T(128)S(1)}, u32[]{:S(2)}) copy-start(f32[6]{0:T(128)S(1)} %multiply_add_fusion.9) | copy-start | bytes 76
  714.9 4.1 collective-permute-start.17
  (139 other events, 454.7 us)

commit v2 on v1

v2 whole, which is shorter than its diff:
```python
import functools
import math

import jax
import jax.numpy as jnp
from jax import lax
from jax.experimental import pallas as pl
from jax.experimental.pallas import tpu as pltpu
from jax.sharding import PartitionSpec as P

D = 768
HEAD = 64
FF = 3072
PATCHES = 576
CAP = 10
VOCAB_DEV = 171
PAD = 8
LANES = 128


DECAY = 0.8
EPS_SQ = 1e-30
CLIP_NORM = 0.25
HIGHEST = lax.Precision.HIGHEST
MESH = pl.DeviceIdType.MESH

Y_SWAP = ((0, 2), (1, 3), (2, 0), (3, 1))
CORE_SWAP = ((0, 1), (1, 0), (2, 3), (3, 2))


def layer_norm(value, gain, shift):
    centred = value - jnp.mean(value, axis=-1, keepdims=True)
    spread = jnp.mean(centred * centred, axis=-1, keepdims=True)
    return centred * lax.rsqrt(spread + 1e-06) * gain + shift


def plain_dot(left, right):
    return jnp.dot(left, right, preferred_element_type=jnp.float32)


def over_rows(left, right):
    return lax.dot_general(
        left, right, (((0,), (0,)), ((), ())), preferred_element_type=jnp.float32
    )


def over_last(left, right):
    return lax.dot_general(
        left, right, (((1,), (1,)), ((), ())), preferred_element_type=jnp.float32
    )


def factored_step(weight, clipped, rows_next, cols_next, rows_mean, rate):
    estimate = rows_next[..., :, None] * cols_next[..., None, :] / rows_mean
    return weight - rate * clipped * lax.rsqrt(estimate)


def place():
    rep = lax.axis_index("rep")
    line = lax.axis_index("exp")
    y = lax.div(rep, 2) * 2 + lax.rem(lax.div(line, 4), 2)
    return {"y": y, "core": lax.rem(rep, 2), "x": lax.div(line, 8), "z": lax.rem(line, 4)}


def device(at):
    return {
        "rep": lax.div(at["y"], 2) * 2 + at["core"],
        "exp": at["x"] * 8 + lax.rem(at["y"], 2) * 4 + at["z"],
    }


def moved(at, axis, by):
    return {**at, axis: lax.rem(at[axis] + by, 2 if axis == "core" else 4)}


def box(ref, at, free, core=False):
    whole = slice(None)
    hi = whole if "y" in free else lax.div(at["y"], 2)
    low = whole if "y" in free else lax.rem(at["y"], 2)
    x = whole if "x" in free else at["x"]
    z = whole if "z" in free else at["z"]
    if core:
        return ref.at[hi, at["core"], x, low, z]
    return ref.at[hi, x, low, z]


def greet(at):
    barrier = pltpu.get_barrier_semaphore()
    peers = [moved(at, axis, by) for axis in ("x", "y", "z") for by in (1, 2, 3)]
    peers.append(moved(at, "core", 1))
    for peer in peers:
        pl.semaphore_signal(barrier, inc=1, device_id=device(peer), device_id_type=MESH)
    pl.semaphore_wait(barrier, len(peers))


def remote(src, dst, sems, index, peer):
    return pltpu.make_async_remote_copy(
        src_ref=src,
        dst_ref=dst,
        send_sem=sems[0].at[index],
        recv_sem=sems[1].at[index],
        device_id=device(peer),
        device_id_type=MESH,
    )


ORDERS = (("x", "y", "z"), ("y", "z", "x"), ("z", "x", "y"))


def gather_kernel(x_ref, *refs):
    squares, extra, spare = refs[:5], refs[5], refs[6]
    outs, (send, recv, local) = refs[7:10], refs[10:]
    at = place()
    sems = (send, recv)
    own = []
    for part in range(3):
        own.append(
            pltpu.make_async_copy(
                x_ref.at[part], box(outs[part], at, (), True), local.at[part]
            )
        )
        own[part].start()
    greet(at)
    flights = {}

    def launch(part, stage):
        axes = ORDERS[part]
        view = box(outs[part], at, axes[:stage], True)
        source = x_ref.at[part] if stage == 0 else view
        for by in (1, 2, 3):
            copy = remote(source, view, sems, part * 13 + stage * 3 + by - 1, moved(at, axes[stage], by))
            copy.start()
            flights[part, stage, by] = copy

    def forward(part, by):
        axes = ORDERS[part]
        view = box(outs[part], moved(at, axes[2], 4 - by), axes[:2], True)
        copy = remote(view, view, sems, part * 13 + 9 + by, moved(at, "core", 1))
        copy.start()
        flights[part, 3, by] = copy

    for part in range(3):
        launch(part, 0)
    for stage in (1, 2):
        for part in range(3):
            if stage == 1:
                own[part].wait()
            for by in (1, 2, 3):
                flights[part, stage - 1, by].wait_recv()
            launch(part, stage)
            if stage == 2:
                forward(part, 0)
    for by in (1, 3, 2):
        for part in range(3):
            flights[part, 2, by].wait_recv()
            forward(part, by)

    row = lax.broadcasted_iota(jnp.int32, (96, 256), 0)
    column = lax.broadcasted_iota(jnp.int32, (96, 256), 1)
    base = lax.div(row, 6) * 16
    inside = lax.rem(row, 6)

    def packer(offset):
        return (column == base + offset + inside).astype(jnp.bfloat16)

    first, second = packer(0), packer(8)
    low_first = jnp.where(inside < 2, packer(6), jnp.where(inside < 4, packer(12), 0)).astype(jnp.bfloat16)
    low_second = jnp.where(inside < 4, 0, packer(2)).astype(jnp.bfloat16)
    packers = [
        jnp.concatenate([first, second, low_first]),
        jnp.concatenate([first, second, low_second]),
        jnp.concatenate([first, second]),
    ]

    def pack(core):
        def step(index, carry):
            high, half = lax.div(index, 2), lax.rem(index, 2)
            place_out = pl.ds(pl.multiple_of((high * 4 + core * 2 + half) * 96, 96), 96)
            packed = []
            for part in range(3):
                block = outs[part][high, core, pl.ds(half * 2, 2)].reshape(256, D)
                packed.append(plain_dot(packers[part], block))
            for k in range(5):
                low = packed[k // 2][96 * (k % 2) : 96 * (k % 2) + 96]
                squares[k][place_out, :] = low.astype(jnp.bfloat16)
            extra[place_out, :] = packed[2][96:].astype(jnp.bfloat16)
            spare[place_out, :] = (packed[0][192:] + packed[1][192:]).astype(jnp.bfloat16)
            return carry

        lax.fori_loop(0, 4, step, 0)

    pack(at["core"])
    for key, copy in flights.items():
        if key[1] == 3:
            copy.wait_recv()
    pack(1 - at["core"])
    for copy in flights.values():
        copy.wait_send()


def gather_all(payload):
    shape = (2, 2, 4, 2, 4, 16, D)
    return pl.pallas_call(
        gather_kernel,
        out_shape=[jax.ShapeDtypeStruct((D, D), payload.dtype)] * 7,
        in_specs=[pl.BlockSpec(memory_space=pltpu.VMEM)],
        out_specs=[pl.BlockSpec(memory_space=pltpu.VMEM)] * 7,
        scratch_shapes=[pltpu.VMEM(shape, payload.dtype)] * 3
        + [
            pltpu.SemaphoreType.DMA((39,)),
            pltpu.SemaphoreType.DMA((39,)),
            pltpu.SemaphoreType.DMA((3,)),
        ],
        compiler_params=pltpu.CompilerParams(
            collective_id=0, has_side_effects=True, vmem_limit_bytes=40 * 2**20
        ),
        name="gather_weights",
    )(payload)


def scatter_kernel(*refs):
    grads, outs = refs[:3], refs[3:6]
    first, total_one, second, total_two, third = (refs[6 + 3 * i : 9 + 3 * i] for i in range(5))
    sems = refs[21:23]
    at = place()
    greet(at)

    def names(axis):
        return ("h", "l") if axis == "y" else (axis,)

    def pick(letter, where, axis):
        if letter not in names(axis):
            return slice(None)
        if letter == "h":
            return lax.div(where["y"], 2)
        if letter == "l":
            return lax.rem(where["y"], 2)
        return where[axis]

    def part_of(source, where, axes, stage):
        if stage == 0:
            return box(source, where, axes[:2])
        if stage == 1:
            left = [letter for letter in ("h", "x", "l", "z") if letter not in names(axes[2])]
            return source.at[tuple(pick(letter, where, axes[1]) for letter in left)]
        return source.at[tuple(pick(letter, where, axes[0]) for letter in names(axes[0]))]

    sources = (grads, total_one, total_two)
    landings = (first, second, third)
    targets = (total_one, total_two, outs)
    flights = {}

    def launch(part, stage):
        axes = ORDERS[part]
        axis = axes[2 - stage]
        flights[part, stage] = []
        for by in (1, 2, 3):
            peer = moved(at, axis, by)
            view = part_of(sources[stage][part], peer, axes, stage)
            copy = remote(view, landings[stage][part].at[by - 1], sems, part * 9 + stage * 3 + by - 1, peer)
            copy.start()
            flights[part, stage].append(copy)

    for part in range(3):
        launch(part, 0)
    for stage in range(3):
        for part in range(3):
            for copy in flights[part, stage]:
                copy.wait_recv()
            landing = landings[stage][part]
            terms = [part_of(sources[stage][part], at, ORDERS[part], stage)[...]]
            terms = [term.astype(jnp.float32) for term in terms + [landing[i] for i in range(3)]]
            targets[stage][part][...] = (terms[0] + terms[1]) + (terms[2] + terms[3])
            if stage < 2:
                launch(part, stage + 1)
    for copies in flights.values():
        for copy in copies:
            copy.wait_send()


def scatter_all(grads):
    block = (2 * PAD, D)
    ones = [{"x": (2, 2, 4), "y": (4, 4), "z": (2, 4, 2)}[axes[2]] for axes in ORDERS]
    twos = [(2, 2) if axes[0] == "y" else (4,) for axes in ORDERS]
    scratch = [pltpu.VMEM((3,) + one + block, jnp.bfloat16) for one in ones]
    scratch += [pltpu.VMEM(one + block, jnp.float32) for one in ones]
    scratch += [pltpu.VMEM((3,) + two + block, jnp.float32) for two in twos]
    scratch += [pltpu.VMEM(two + block, jnp.float32) for two in twos]
    scratch += [pltpu.VMEM((3,) + block, jnp.float32)] * 3
    scratch += [pltpu.SemaphoreType.DMA((27,)), pltpu.SemaphoreType.DMA((27,))]
    return pl.pallas_call(
        scatter_kernel,
        out_shape=[jax.ShapeDtypeStruct(block, jnp.float32)] * 3,
        in_specs=[pl.BlockSpec(memory_space=pltpu.VMEM)] * 3,
        out_specs=[pl.BlockSpec(memory_space=pltpu.VMEM)] * 3,
        scratch_shapes=scratch,
        compiler_params=pltpu.CompilerParams(
            collective_id=1, has_side_effects=True, vmem_limit_bytes=40 * 2**20
        ),
        name="scatter_grads",
    )(*grads)


def meet_core(at):
    barrier = pltpu.get_barrier_semaphore()
    other = moved(at, "core", 1)
    pl.semaphore_signal(barrier, inc=1, device_id=device(other), device_id_type=MESH)
    pl.semaphore_wait(barrier, 1)
    return other


CHUNK = 48


def chunks(count, step, start=0):
    lax.fori_loop(0, count // CHUNK, lambda i, c: step(pl.ds(pl.multiple_of(i * CHUNK, CHUNK), CHUNK), c), start)


def centre(value):
    centred = value - jnp.mean(value, axis=-1, keepdims=True)
    spread = jnp.mean(centred * centred, axis=-1, keepdims=True)
    return centred * lax.rsqrt(spread + 1e-06), lax.rsqrt(spread + 1e-06)


def norm_back(value, grad, gain):
    normed, rate = centre(value)
    scaled = grad * gain
    inner = (
        scaled
        - jnp.mean(scaled, axis=-1, keepdims=True)
        - normed * jnp.mean(scaled * normed, axis=-1, keepdims=True)
    )
    return rate * inner, jnp.sum(grad * normed, axis=0, keepdims=True), jnp.sum(grad, axis=0, keepdims=True)


def attend_kernel(
    x_ref, w0, w1, w2, w3, w4, vec, table, router, ids,
    embed, hidden_one, query, keys, values, mixed, after, hidden_two, gate_probs, gates, lse,
    send, recv,
):
    at = place()
    sems = (send, recv)
    other = meet_core(at)
    rows = x_ref.shape[0]
    embed[...] = plain_dot(x_ref[...], w0[...])

    def first_norm(part, carry):
        value = embed[part, :] + vec[0:1, :] + table[part, :]
        embed[part, :] = value
        normed, _ = centre(value)
        hidden_one[part, :] = (normed * vec[1:2, :] + vec[2:3, :]).astype(jnp.bfloat16)
        return carry

    chunks(rows, first_norm)
    keys[0] = plain_dot(hidden_one[...], w2[...]).astype(jnp.bfloat16)
    send_keys = remote(keys.at[0], keys.at[1], sems, 0, other)
    send_keys.start()
    values[0] = (plain_dot(hidden_one[...], w3[...]) + vec[4:5, :]).astype(jnp.bfloat16)
    send_values = remote(values.at[0], values.at[1], sems, 1, other)
    send_values.start()
    query[...] = (plain_dot(hidden_one[...], w1[...]) + vec[3:4, :]).astype(jnp.bfloat16)
    send_keys.wait()
    send_values.wait()

    def heads(index, carry):
        lanes = pl.ds(pl.multiple_of(index * LANES, LANES), LANES)
        query_two = query[:, lanes]
        key_two = keys[:, :, lanes].reshape(2 * rows, LANES)
        value_t = values[:, :, lanes].reshape(2 * rows, LANES).T
        left = lax.broadcasted_iota(jnp.int32, (rows, LANES), 1) < HEAD
        outs = []
        for half in range(2):
            own = jnp.where(left if half == 0 else ~left, query_two, jnp.zeros_like(query_two))
            scores = over_last(key_two, own) * HEAD ** (-0.5)
            most = jnp.max(scores, axis=0, keepdims=True)
            raw = jnp.exp(scores - most)
            total = jnp.sum(raw, axis=0, keepdims=True)
            lse[pl.ds(index * 2 + half, 1), :] = most + jnp.log(total)
            probs = (raw * (1.0 / total)).astype(jnp.bfloat16)
            outs.append(plain_dot(value_t[half * HEAD : (half + 1) * HEAD], probs))
        mixed[:, lanes] = jnp.concatenate(outs).T.astype(jnp.bfloat16)
        return carry

    lax.fori_loop(0, D // LANES, heads, 0)
    after[...] = plain_dot(mixed[...], w4[...])

    def second_norm(part, carry):
        value = embed[part, :] + after[part, :] + vec[5:6, :]
        after[part, :] = value
        normed, _ = centre(value)
        low = (normed * vec[6:7, :] + vec[7:8, :]).astype(jnp.bfloat16)
        hidden_two[part, :] = low
        logits = plain_dot(low, router[...])
        lane = lax.broadcasted_iota(jnp.int32, logits.shape, 1)
        logits = jnp.where(lane < 32, logits, -jnp.inf)
        raw = jnp.exp(logits - jnp.max(logits, axis=-1, keepdims=True))
        probs = raw / jnp.sum(raw, axis=-1, keepdims=True)
        gate_probs[part, :] = probs
        first, second = (
            jnp.sum(jnp.where(lane == ids[part, k : k + 1], probs, 0.0), axis=-1, keepdims=True) for k in range(2)
        )
        gates[part, :] = jnp.where(lane == 0, first, second)
        return carry

    chunks(rows, second_norm)


def attend(patch_rows, squares, vectors, table_rows, router, ids):
    rows = patch_rows.shape[0]
    low, wide = jnp.bfloat16, jnp.float32
    shapes = [
        ((rows, D), wide), ((rows, D), low), ((rows, D), low), ((2, rows, D), low), ((2, rows, D), low),
        ((rows, D), low), ((rows, D), wide), ((rows, D), low), ((rows, LANES), wide), ((rows, LANES), wide), ((16, rows), wide),
    ]
    return pl.pallas_call(
        attend_kernel,
        out_shape=[jax.ShapeDtypeStruct(*shape) for shape in shapes],
        in_specs=[pl.BlockSpec(memory_space=pltpu.VMEM)] * 10,
        out_specs=[pl.BlockSpec(memory_space=pltpu.VMEM)] * 11,
        scratch_shapes=[pltpu.SemaphoreType.DMA((2,)), pltpu.SemaphoreType.DMA((2,))],
        compiler_params=pltpu.CompilerParams(
            collective_id=6, has_side_effects=True, vmem_limit_bytes=48 * 2**20
        ),
        name="attend",
    )(patch_rows, *squares, vectors, table_rows, router, ids)


def attend_back_kernel(
    dafter_in, dhidden, dgate, embed, after, hidden_one, query, keys, values, lse, w1, w2, w3, w4, vec, router,
    dafter_low, dquery, dkey, dvalue, dembed_low, sums,
    dafter, dmixed, dkey_own, dvalue_own, dkey_other, dvalue_other, dkey_got, dvalue_got, wide, send, recv,
):
    at = place()
    sems = (send, recv)
    other = meet_core(at)
    rows = dafter_in.shape[0]
    pairs = D // LANES
    zero = jnp.zeros((1, D), jnp.float32)
    wide[...] = over_last(dgate[...], router[...])

    def second_norm(index, carry):
        part = pl.ds(pl.multiple_of(index * CHUNK, CHUNK), CHUNK)
        grad = wide[part, :] + dhidden[part, :]
        back, gain, shift = norm_back(after[part, :], grad, vec[6:7, :])
        total = dafter_in[part, :] + back
        dafter[part, :] = total
        dafter_low[part, :] = total.astype(jnp.bfloat16)
        return carry[0] + jnp.sum(total, axis=0, keepdims=True), carry[1] + gain, carry[2] + shift

    bias, gain, shift = lax.fori_loop(0, rows // CHUNK, second_norm, (zero, zero, zero))
    sums[5:6, :] = bias
    sums[6:7, :] = gain
    sums[7:8, :] = shift
    dmixed[...] = over_last(dafter_low[...], w4[...]).astype(jnp.bfloat16)

    def flights(index):
        return (
            remote(dkey_other.at[index], dkey_got.at[index], sems, index, other),
            remote(dvalue_other.at[index], dvalue_got.at[index], sems, pairs + index, other),
        )

    def heads(index, carry):
        lanes = pl.ds(pl.multiple_of(index * LANES, LANES), LANES)
        query_two = query[:, lanes]
        dmixed_two = dmixed[:, lanes]
        key_two = keys[:, :, lanes].reshape(2 * rows, LANES)
        value_two = values[:, :, lanes].reshape(2 * rows, LANES)
        key_t = key_two.T
        left = lax.broadcasted_iota(jnp.int32, (rows, LANES), 1) < HEAD
        dkey_two = jnp.zeros((2 * rows, LANES), jnp.float32)
        dvalue_two = jnp.zeros((2 * rows, LANES), jnp.float32)
        outs = []
        for half in range(2):
            mask = left if half == 0 else ~left
            own = jnp.where(mask, query_two, jnp.zeros_like(query_two))
            down = jnp.where(mask, dmixed_two, jnp.zeros_like(dmixed_two))
            scores = over_last(key_two, own) * HEAD ** (-0.5)
            probs = jnp.exp(scores - lse[pl.ds(index * 2 + half, 1), :])
            dprobs = over_last(value_two, down)
            row_shift = jnp.sum(probs * dprobs, axis=0, keepdims=True)
            dscores = (probs * (dprobs - row_shift)).astype(jnp.bfloat16)
            dvalue_two = dvalue_two + plain_dot(probs.astype(jnp.bfloat16), down)
            dkey_two = dkey_two + plain_dot(dscores, own)
            outs.append(plain_dot(key_t[half * HEAD : (half + 1) * HEAD], dscores))
        dkey_two = dkey_two * HEAD ** (-0.5)
        dquery[:, lanes] = (jnp.concatenate(outs).T * HEAD ** (-0.5)).astype(jnp.bfloat16)
        dkey_own[index] = dkey_two[:rows]
        dkey_other[index] = dkey_two[rows:]
        dvalue_own[index] = dvalue_two[:rows]
        dvalue_other[index] = dvalue_two[rows:]
        for copy in flights(index):
            copy.start()
        return carry

    lax.fori_loop(0, pairs, heads, 0)

    def gather(index, carry):
        lanes = pl.ds(pl.multiple_of(index * LANES, LANES), LANES)
        for copy in flights(index):
            copy.wait()
        dkey[:, lanes] = (dkey_own[index] + dkey_got[index]).astype(jnp.bfloat16)
        dvalue[:, lanes] = (dvalue_own[index] + dvalue_got[index]).astype(jnp.bfloat16)
        return carry

    lax.fori_loop(0, pairs, gather, 0)
    wide[...] = (
        over_last(dquery[...], w1[...]) + over_last(dkey[...], w2[...]) + over_last(dvalue[...], w3[...])
    )

    def first_norm(index, carry):
        part = pl.ds(pl.multiple_of(index * CHUNK, CHUNK), CHUNK)
        back, gain, shift = norm_back(embed[part, :], wide[part, :], vec[1:2, :])
        total = dafter[part, :] + back
        dembed_low[part, :] = total.astype(jnp.bfloat16)
        return (
            carry[0] + jnp.sum(total, axis=0, keepdims=True),
            carry[1] + gain,
            carry[2] + shift,
            carry[3] + jnp.sum(dquery[part, :].astype(jnp.float32), axis=0, keepdims=True),
            carry[4] + jnp.sum(dvalue[part, :].astype(jnp.float32), axis=0, keepdims=True),
        )

    for index, total in enumerate(lax.fori_loop(0, rows // CHUNK, first_norm, (zero,) * 5)):
        sums[index : index + 1, :] = total


def attend_back(*operands):
    rows = operands[0].shape[0]
    low, wide = jnp.bfloat16, jnp.float32
    pairs = D // LANES
    return pl.pallas_call(
        attend_back_kernel,
        out_shape=[jax.ShapeDtypeStruct((rows, D), low)] * 5 + [jax.ShapeDtypeStruct((8, D), wide)],
        in_specs=[pl.BlockSpec(memory_space=pltpu.VMEM)] * 16,
        out_specs=[pl.BlockSpec(memory_space=pltpu.VMEM)] * 6,
        scratch_shapes=[pltpu.VMEM((rows, D), wide), pltpu.VMEM((rows, D), low)]
        + [pltpu.VMEM((pairs, rows, LANES), wide)] * 6
        + [pltpu.VMEM((rows, D), wide)]
        + [pltpu.SemaphoreType.DMA((2 * pairs,)), pltpu.SemaphoreType.DMA((2 * pairs,))],
        compiler_params=pltpu.CompilerParams(
            collective_id=7, has_side_effects=True, vmem_limit_bytes=48 * 2**20
        ),
        name="attend_back",
    )(*operands)


SLOTS = 16
TAIL = 2 * CAP - SLOTS
WIRE = D + 2 * LANES
GROUP = 32
MAIN = GROUP * SLOTS
TOTAL = GROUP * (SLOTS + TAIL)


def iota(shape, axis):
    return lax.broadcasted_iota(jnp.int32, shape, axis)


def pack(block, main, tail):
    count = block.shape[0]
    block[:, :, :D] = main.astype(jnp.bfloat16).reshape(count, SLOTS, D)
    shape = (count * SLOTS, count * TAIL)
    row, column = iota(shape, 0), iota(shape, 1)
    spread = (lax.div(row, SLOTS) == lax.div(column, TAIL)) & (lax.rem(row, TAIL) == lax.rem(column, TAIL))
    wide = plain_dot(spread.astype(jnp.bfloat16), tail.astype(jnp.bfloat16))
    turn = lax.div(lax.rem(iota((count * SLOTS, LANES), 0), SLOTS), TAIL)
    for half, tiles in ((0, (0, 1, 2, 3)), (1, (4, 5))):
        packed = jnp.zeros((count * SLOTS, LANES), jnp.float32)
        for place_in, tile in enumerate(tiles):
            packed = jnp.where(turn == place_in, wide[:, tile * LANES : (tile + 1) * LANES], packed)
        block[:, :, D + half * LANES : D + (half + 1) * LANES] = packed.astype(jnp.bfloat16).reshape(
            count, SLOTS, LANES
        )


def unpack(block, rows, first, first_tail):
    count = block.shape[0]
    rows[first : first + count * SLOTS, :] = block[:, :, :D].reshape(count * SLOTS, D)
    shape = (count * TAIL, count * SLOTS)
    row, column = iota(shape, 0), iota(shape, 1)
    same = lax.div(column, SLOTS) == lax.div(row, TAIL)
    packed = block[:, :, D:].reshape(count * SLOTS, 2 * LANES)
    for turn in range(4):
        chosen = same & (lax.rem(column, SLOTS) == turn * TAIL + lax.rem(row, TAIL))
        part = plain_dot(chosen.astype(jnp.bfloat16), packed).astype(jnp.bfloat16)
        rows[first_tail : first_tail + count * TAIL, turn * LANES : (turn + 1) * LANES] = part[:, :LANES]
        if turn < 2:
            rows[first_tail : first_tail + count * TAIL, (4 + turn) * LANES : (5 + turn) * LANES] = part[
                :, LANES:
            ]


def meet_experts(at):
    barrier = pltpu.get_barrier_semaphore()
    me = lax.axis_index("exp")

    def greet_one(by, carry):
        peer = lax.rem(me + by, GROUP)
        pl.semaphore_signal(barrier, inc=1, device_id={"exp": peer}, device_id_type=MESH)
        return carry

    lax.fori_loop(1, GROUP, greet_one, 0)
    other = moved(at, "core", 1)
    pl.semaphore_signal(barrier, inc=1, device_id=device(other), device_id_type=MESH)
    return other


def met_experts():
    pl.semaphore_wait(pltpu.get_barrier_semaphore(), GROUP)


def deal(source, target, sems, forth, low, high, act):
    me = lax.axis_index("exp")

    def one(by, carry):
        peer = lax.rem(me + by, GROUP) if forth else lax.rem(me + GROUP - by, GROUP)
        copy = pltpu.make_async_remote_copy(
            src_ref=source.at[peer] if forth else source.at[by],
            dst_ref=target.at[by] if forth else target.at[me],
            send_sem=sems[0].at[by],
            recv_sem=sems[1].at[by],
            device_id={"exp": peer},
            device_id_type=MESH,
        )
        act(copy)
        return carry

    lax.fori_loop(low, high, one, 0)


def start_copy(copy):
    copy.start()


def wait_send(copy):
    copy.wait_send()


def wait_recv(copy):
    copy.wait_recv()


def load_experts(own, across, weights, sems, local, other):
    near = [pltpu.make_async_copy(own, weights.at[0], local.at[0])]
    near.append(pltpu.make_async_copy(across, weights.at[1], local.at[1]))
    far = [remote(own, weights.at[2], sems, 0, other), remote(across, weights.at[3], sems, 1, other)]
    return near, far


GELU_SCALE = math.sqrt(2 / math.pi)


def gelu_tanh(value):
    return jnp.tanh(GELU_SCALE * (value + 0.044715 * (value * value * value)))


def halves(rows, half):
    count = MAIN // 2
    tail = (TOTAL - MAIN) // 2
    return jnp.concatenate(
        [
            rows[half * count : (half + 1) * count, :],
            rows[MAIN + half * tail : MAIN + (half + 1) * tail, :],
        ]
    )


HALF = TOTAL // 2


def experts_kernel(
    hidden, target_row, target_column, gates, after, vec, own, across,
    rows, chosen, total, pool,
    weights, sends, lands, backs, returns, act, result, gathered,
    forth_send, forth_recv, back_send, back_recv, weight_send, weight_recv, local,
):
    at = place()
    me = lax.axis_index("exp")
    other = meet_experts(at)
    near, far = load_experts(own, across, weights, (weight_send, weight_recv), local, other)
    for copy in near:
        copy.start()
    count = hidden.shape[0]
    slot = iota((TOTAL, count), 0)
    placing = ((slot == target_row[0:1, :]) | (slot == target_row[1:2, :])).astype(jnp.bfloat16)
    placed = plain_dot(placing, hidden[...])
    pack(sends, placed[:MAIN], placed[MAIN:])
    met_experts()
    deal(sends, lands, (forth_send, forth_recv), True, 1, GROUP, start_copy)
    for copy in far:
        copy.start()
    keep = pltpu.make_async_copy(sends.at[me], lands.at[0], local.at[2])
    keep.start()
    keep.wait()
    deal(sends, lands, (forth_send, forth_recv), True, 1, GROUP // 2, wait_recv)
    for copy in near:
        copy.wait()
    for half in range(2):
        if half == 1:
            deal(sends, lands, (forth_send, forth_recv), True, GROUP // 2, GROUP, wait_recv)
        sources = pl.ds(half * (GROUP // 2), GROUP // 2)
        first, first_tail = half * (MAIN // 2), MAIN + half * (TOTAL - MAIN) // 2
        unpack(lands.at[sources], rows, first, first_tail)
        if half == 0:
            for copy in far:
                copy.wait_recv()
        given = halves(rows, half)

        def hidden_units(index, carry):
            quarter, part = lax.div(index, 3), lax.rem(index, 3)
            columns = pl.ds(pl.multiple_of(part * 256, 256), 256)
            value = plain_dot(given, weights[quarter, 0, :, columns])
            act[quarter, :, columns] = (0.5 * value * (1.0 + gelu_tanh(value))).astype(jnp.bfloat16)
            return carry

        lax.fori_loop(0, 12, hidden_units, 0)

        def outputs(index, carry):
            columns = pl.ds(pl.multiple_of(index * 256, 256), 256)
            value = over_last(act[0], weights[0, 1, columns, :])
            for quarter in range(1, 4):
                value = value + over_last(act[quarter], weights[quarter, 1, columns, :])
            result[:, columns] = value
            return carry

        lax.fori_loop(0, 3, outputs, 0)
        pack(backs.at[sources], result[: MAIN // 2, :], result[MAIN // 2 :, :])
        deal(backs, returns, (back_send, back_recv), False, max(1, half * (GROUP // 2)), (half + 1) * (GROUP // 2), start_copy)
    keep = pltpu.make_async_copy(backs.at[0], returns.at[me], local.at[2])
    keep.start()
    keep.wait()
    deal(backs, returns, (back_send, back_recv), False, 1, GROUP, wait_recv)
    unpack(returns, gathered, 0, MAIN)
    slot = iota((count, TOTAL), 1)
    for k in range(2):
        placing = (slot == target_column[:, k : k + 1]).astype(jnp.bfloat16)
        chosen[k] = plain_dot(placing, gathered[...]).astype(jnp.bfloat16)

    def final_norm(index, carry):
        part = pl.ds(pl.multiple_of(index * CHUNK, CHUNK), CHUNK)
        value = after[part, :] + (
            gates[part, 0:1] * chosen[0, part, :].astype(jnp.float32)
            + gates[part, 1:2] * chosen[1, part, :].astype(jnp.float32)
        )
        total[part, :] = value
        normed, _ = centre(value)
        return carry + jnp.sum(normed * vec[8:9, :] + vec[9:10, :], axis=0, keepdims=True)

    summed = lax.fori_loop(0, count // CHUNK, final_norm, jnp.zeros((1, D), jnp.float32)) / PATCHES
    pool[...] = jnp.zeros_like(pool)
    for tile in range(D // LANES):
        pool[tile : tile + 1, :] = summed[:, tile * LANES : (tile + 1) * LANES]
    deal(sends, lands, (forth_send, forth_recv), True, 1, GROUP, wait_send)
    deal(backs, returns, (back_send, back_recv), False, 1, GROUP, wait_send)
    for copy in far:
        copy.wait_send()


def experts_forward(*operands):
    count = operands[0].shape[0]
    low, wide = jnp.bfloat16, jnp.float32
    wire = pltpu.VMEM((GROUP, SLOTS, WIRE), low)
    shapes = [((TOTAL, D), low), ((2, count, D), low), ((count, D), wide), ((PAD, LANES), wide)]
    sems = pltpu.SemaphoreType.DMA((GROUP,))
    return pl.pallas_call(
        experts_kernel,
        out_shape=[jax.ShapeDtypeStruct(*shape) for shape in shapes],
        in_specs=[pl.BlockSpec(memory_space=pltpu.VMEM)] * 6 + [pl.BlockSpec(memory_space=pl.ANY)] * 2,
        out_specs=[pl.BlockSpec(memory_space=pltpu.VMEM)] * 4,
        scratch_shapes=[pltpu.VMEM((4, 2, D, D), low)]
        + [wire] * 4
        + [pltpu.VMEM((4, HALF, D), low), pltpu.VMEM((HALF, D), wide), pltpu.VMEM((TOTAL, D), low)]
        + [sems] * 4
        + [pltpu.SemaphoreType.DMA((2,))] * 2
        + [pltpu.SemaphoreType.DMA((3,))],
        compiler_params=pltpu.CompilerParams(
            collective_id=5, has_side_effects=True, vmem_limit_bytes=48 * 2**20
        ),
        name="experts_forward",
    )(*operands)


def experts_back_kernel(
    row_grad, total, chosen, gates, gate_probs, ids, rows, target_row, target_column, vec, own, across,
    dtotal, dgate, sums, dhidden, to_y, kept,
    weights, sends, lands, backs, returns, act, slope, dpre, drows, result, dreturned, rows_t, drows_t, outward,
    forth_send, forth_recv, back_send, back_recv, weight_send, weight_recv, grad_send, grad_recv, local, ready,
):
    at = place()
    me = lax.axis_index("exp")
    other = meet_experts(at)
    near, far = load_experts(own, across, weights, (weight_send, weight_recv), local, other)
    for copy in near:
        copy.start()
    count = total.shape[0]
    grad = jnp.concatenate([row_grad[tile : tile + 1, :] for tile in range(D // LANES)], axis=1) / PATCHES
    zero = jnp.zeros((1, D), jnp.float32)

    def final_norm(index, carry):
        part = pl.ds(pl.multiple_of(index * CHUNK, CHUNK), CHUNK)
        back, gain, shift = norm_back(total[part, :], jnp.broadcast_to(grad, (CHUNK, D)), vec[8:9, :])
        dtotal[part, :] = back
        dgates = [
            jnp.sum(back * chosen[k, part, :].astype(jnp.float32), axis=-1, keepdims=True) for k in range(2)
        ]
        for k in range(2):
            outward[k, part, :] = (gates[part, k : k + 1] * back).astype(jnp.bfloat16)
        lane = iota((CHUNK, LANES), 1)
        probs = gate_probs[part, :]
        dprobs = jnp.where(lane == ids[part, 0:1], dgates[0], 0.0) + jnp.where(
            lane == ids[part, 1:2], dgates[1], 0.0
        )
        inner = dprobs - jnp.sum(probs * dprobs, axis=-1, keepdims=True)
        dgate[part, :] = (probs * inner).astype(jnp.bfloat16)
        return carry[0] + gain, carry[1] + shift

    gain, shift = lax.fori_loop(0, count // CHUNK, final_norm, (zero, zero))
    sums[0:1, :] = gain
    sums[1:2, :] = shift
    slot = iota((TOTAL, count), 0)
    placed = [
        plain_dot((slot == target_row[k : k + 1, :]).astype(jnp.bfloat16), outward[k]) for k in range(2)
    ]
    placed = placed[0] + placed[1]
    pack(sends, placed[:MAIN], placed[MAIN:])
    met_experts()
    deal(sends, lands, (forth_send, forth_recv), True, 1, GROUP, start_copy)
    for copy in far:
        copy.start()
    keep = pltpu.make_async_copy(sends.at[me], lands.at[0], local.at[2])
    keep.start()
    keep.wait()
    for copy in near:
        copy.wait()

    def hidden_units(index, carry):
        quarter, rest = lax.div(index, 6), lax.rem(index, 6)
        half, part = lax.div(rest, 3), lax.rem(rest, 3)
        columns = pl.ds(pl.multiple_of(part * 256, 256), 256)
        lines = pl.ds(pl.multiple_of(half * HALF, HALF), HALF)
        value = plain_dot(rows[lines, :], weights[quarter, 0, :, columns])
        tanh = gelu_tanh(value)
        act[quarter, lines, columns] = (0.5 * value * (1.0 + tanh)).astype(jnp.bfloat16)
        slope[quarter, lines, columns] = 0.5 * (1.0 + tanh) + 0.5 * value * (1.0 - tanh * tanh) * (
            GELU_SCALE * (1.0 + 3 * 0.044715 * (value * value))
        )
        return carry

    lax.fori_loop(0, 12, hidden_units, 0)
    for copy in far:
        copy.wait_recv()
    lax.fori_loop(12, 24, hidden_units, 0)
    rows_t[...] = rows[...].T
    deal(sends, lands, (forth_send, forth_recv), True, 1, GROUP, wait_recv)
    unpack(lands, drows, 0, MAIN)

    def hidden_back(index, carry):
        quarter, rest = lax.div(index, 6), lax.rem(index, 6)
        half, part = lax.div(rest, 3), lax.rem(rest, 3)
        columns = pl.ds(pl.multiple_of(part * 256, 256), 256)
        lines = pl.ds(pl.multiple_of(half * HALF, HALF), HALF)
        value = plain_dot(drows[lines, :], weights[quarter, 1, :, columns])
        dpre[quarter, lines, columns] = (value * slope[quarter, lines, columns]).astype(jnp.bfloat16)
        return carry

    lax.fori_loop(0, 24, hidden_back, 0)

    def inputs_back(index, carry):
        half, part = lax.div(index, 3), lax.rem(index, 3)
        columns = pl.ds(pl.multiple_of(part * 256, 256), 256)
        lines = pl.ds(pl.multiple_of(half * HALF, HALF), HALF)
        value = over_last(dpre[0, lines, :], weights[0, 0, columns, :])
        for quarter in range(1, 4):
            value = value + over_last(dpre[quarter, lines, :], weights[quarter, 0, columns, :])
        result[lines, columns] = value
        return carry

    lax.fori_loop(0, 6, inputs_back, 0)
    pl.semaphore_signal(ready, inc=1, device_id=device(other), device_id_type=MESH)
    pack(backs, result[:MAIN, :], result[MAIN:, :])
    deal(backs, returns, (back_send, back_recv), False, 1, GROUP, start_copy)
    keep = pltpu.make_async_copy(backs.at[0], returns.at[me], local.at[2])
    keep.start()
    drows_t[...] = drows[...].T

    def gradient(quarter, which, columns):
        if which == 0:
            return plain_dot(rows_t[...], dpre[quarter, :, columns])
        return plain_dot(drows_t[...], act[quarter, :, columns])

    def far_grads(index, carry):
        quarter, part = lax.div(index, 3) + 2, lax.rem(index, 3)
        columns = pl.ds(pl.multiple_of(part * 256, 256), 256)
        for which in range(2):
            weights[quarter, which, :, columns] = gradient(quarter, which, columns).astype(jnp.bfloat16)
        return carry

    for copy in far:
        copy.wait_send()
    lax.fori_loop(0, 6, far_grads, 0)
    pl.semaphore_wait(ready, 1)
    swaps = [remote(weights.at[2 + k], weights.at[k], (grad_send, grad_recv), k, other) for k in range(2)]
    for swap in swaps:
        swap.start()

    def kept_grads(index, carry):
        columns = pl.ds(pl.multiple_of(index * 256, 256), 256)
        for which in range(2):
            kept[which, :, columns] = gradient(0, which, columns)
        return carry

    lax.fori_loop(0, 3, kept_grads, 0)
    keep.wait()
    deal(backs, returns, (back_send, back_recv), False, 1, GROUP, wait_recv)
    unpack(returns, dreturned, 0, MAIN)
    slot = iota((count, TOTAL), 1)
    placing = (slot == target_column[:, 0:1]) | (slot == target_column[:, 1:2])
    dhidden[...] = plain_dot(placing.astype(jnp.bfloat16), dreturned[...])
    for swap in swaps:
        swap.wait_recv()

    def sent_grads(index, carry):
        columns = pl.ds(pl.multiple_of(index * 256, 256), 256)
        for which in range(2):
            value = gradient(1, which, columns) + weights[1, which, :, columns].astype(jnp.float32)
            to_y[which, :, columns] = value.astype(jnp.bfloat16)
            kept[which, :, columns] = kept[which, :, columns] + weights[0, which, :, columns].astype(
                jnp.float32
            )
        return carry

    lax.fori_loop(0, 3, sent_grads, 0)
    deal(sends, lands, (forth_send, forth_recv), True, 1, GROUP, wait_send)
    deal(backs, returns, (back_send, back_recv), False, 1, GROUP, wait_send)
    for swap in swaps:
        swap.wait_send()


def experts_backward(*operands):
    count = operands[1].shape[0]
    low, wide = jnp.bfloat16, jnp.float32
    wire = pltpu.VMEM((GROUP, SLOTS, WIRE), low)
    shapes = [
        ((count, D), wide), ((count, LANES), low), ((PAD, D), wide),
        ((count, D), wide), ((2, D, D), low), ((2, D, D), wide),
    ]
    sems = pltpu.SemaphoreType.DMA((GROUP,))
    return pl.pallas_call(
        experts_back_kernel,
        out_shape=[jax.ShapeDtypeStruct(*shape) for shape in shapes],
        in_specs=[pl.BlockSpec(memory_space=pltpu.VMEM)] * 10 + [pl.BlockSpec(memory_space=pl.ANY)] * 2,
        out_specs=[pl.BlockSpec(memory_space=pltpu.VMEM)] * 6,
        scratch_shapes=[pltpu.VMEM((4, 2, D, D), low)]
        + [wire] * 4
        + [pltpu.VMEM((4, TOTAL, D), low), pltpu.VMEM((4, TOTAL, D), wide), pltpu.VMEM((4, TOTAL, D), low)]
        + [pltpu.VMEM((TOTAL, D), low), pltpu.VMEM((TOTAL, D), wide), pltpu.VMEM((TOTAL, D), low)]
        + [pltpu.VMEM((D, TOTAL), low)] * 2
        + [pltpu.VMEM((2, count, D), low)]
        + [sems] * 4
        + [pltpu.SemaphoreType.DMA((2,))] * 4
        + [pltpu.SemaphoreType.DMA((3,)), pltpu.SemaphoreType.REGULAR],
        compiler_params=pltpu.CompilerParams(
            collective_id=8, has_side_effects=True, vmem_limit_bytes=58 * 2**20
        ),
        name="experts_backward",
    )(*operands)


NEAR = tuple((y, core) for y in range(4) for core in range(2) if y or core)
PLANE = tuple((x, z) for x in range(4) for z in range(4) if x or z)


def near_peer(at, by):
    return moved(moved(at, "y", by[0]), "core", by[1])


def plane_peer(at, by):
    return moved(moved(at, "x", by[0]), "z", by[1])


def greet_all(at):
    barrier = pltpu.get_barrier_semaphore()
    peers = [near_peer(at, by) for by in NEAR] + [plane_peer(at, by) for by in PLANE]
    for peer in peers:
        pl.semaphore_signal(barrier, inc=1, device_id=device(peer), device_id_type=MESH)
    pl.semaphore_wait(barrier, len(peers))


def send_near(at, source, target, sems, first):
    copies = []
    for index, by in enumerate(NEAR):
        peer = near_peer(at, by)
        copies.append(remote(source(peer), target.at[at["y"], at["core"]], sems, first + index, peer))
        copies[-1].start()
    return copies


def send_plane(at, source, target, sems, first):
    copies = []
    for index, by in enumerate(PLANE):
        peer = plane_peer(at, by)
        copies.append(remote(source(peer), target.at[at["x"], at["z"]], sems, first + index, peer))
        copies[-1].start()
    return copies


def head_kernel(
    pool, head, targets, valid, count,
    row_grad, head_grad, loss,
    near, every, pooled, pulls, got, summed, last, send, recv,
):
    at = place()
    sems = (send, recv)
    greet_all(at)
    copies = send_near(at, lambda peer: pool, near, sems, 0)
    near[at["y"], at["core"]] = pool[...]
    for copy in copies:
        copy.wait()
    rows = near[:, 0] + near[:, 1]
    every[at["x"], at["z"]] = rows.astype(jnp.bfloat16).astype(jnp.float32)
    mine = every.at[at["x"], at["z"]]
    for copy in send_plane(at, lambda peer: mine, every, sems, 7):
        copy.wait()
    images = pooled.shape[0]
    for tile in range(D // LANES):
        lanes = slice(tile * LANES, (tile + 1) * LANES)
        pooled[:, lanes] = every[:, :, :, tile, :].reshape(images, LANES).astype(jnp.bfloat16)
    logits = plain_dot(pooled[...], head[...])
    soft = jnp.maximum(logits, 0.0) + jnp.log1p(jnp.exp(-jnp.abs(logits)))
    inside = iota(logits.shape, 1) < VOCAB_DEV
    terms = jnp.where(inside, valid[...] * (soft - targets[...] * logits), 0.0)
    loss[...] = jnp.sum(jnp.sum(terms, axis=1, keepdims=True), axis=0, keepdims=True)
    sigmoid = 1.0 / (1.0 + jnp.exp(-logits))
    down = jnp.where(inside, valid[...] * (sigmoid - targets[...]) / count[...], 0.0).astype(jnp.bfloat16)
    back = over_last(down, head[...])
    pulls[...] = jnp.zeros_like(pulls)
    for tile in range(D // LANES):
        lanes = slice(tile * LANES, (tile + 1) * LANES)
        pulls[:, :, :, tile, :] = back[:, lanes].reshape(4, 4, 4, LANES)
    copies = send_plane(at, lambda peer: pulls.at[peer["x"], peer["z"]], got, sems, 22)
    got[at["x"], at["z"]] = pulls[at["x"], at["z"]]
    head_grad[...] = plain_dot(pooled[...].T, down)
    for copy in copies:
        copy.wait()
    summed[...] = jnp.sum(got[...].reshape((16,) + summed.shape), axis=0)
    copies = send_near(at, lambda peer: summed.at[peer["y"]], last, sems, 37)
    last[at["y"], at["core"]] = summed[at["y"]]
    for copy in copies:
        copy.wait()
    row_grad[...] = jnp.sum(last[...].reshape((8,) + row_grad.shape), axis=0)


def head_step(pool, head, targets, valid, count):
    images, classes = targets.shape
    wide = jnp.float32
    block = (PAD, LANES)
    return pl.pallas_call(
        head_kernel,
        out_shape=[
            jax.ShapeDtypeStruct(block, wide),
            jax.ShapeDtypeStruct((D, classes), wide),
            jax.ShapeDtypeStruct((1, 1), wide),
        ],
        in_specs=[pl.BlockSpec(memory_space=pltpu.VMEM)] * 5,
        out_specs=[pl.BlockSpec(memory_space=pltpu.VMEM)] * 3,
        scratch_shapes=[
            pltpu.VMEM((4, 2) + block, wide),
            pltpu.VMEM((4, 4, 4) + block, wide),
            pltpu.VMEM((images, D), jnp.bfloat16),
            pltpu.VMEM((4, 4, 4) + block, wide),
            pltpu.VMEM((4, 4, 4) + block, wide),
            pltpu.VMEM((4,) + block, wide),
            pltpu.VMEM((4, 2) + block, wide),
            pltpu.SemaphoreType.DMA((44,)),
            pltpu.SemaphoreType.DMA((44,)),
        ],
        compiler_params=pltpu.CompilerParams(collective_id=2, has_side_effects=True),
        name="head_step",
    )(pool, head, targets, valid, count)


def total_kernel(x_ref, o_ref, near, every, summed, send, recv):
    at = place()
    sems = (send, recv)
    greet_all(at)
    copies = send_near(at, lambda peer: x_ref, near, sems, 0)
    near[at["y"], at["core"]] = x_ref[...]
    for copy in copies:
        copy.wait()
    summed[...] = jnp.sum(near[...].reshape((8,) + summed.shape), axis=0)
    copies = send_plane(at, lambda peer: summed, every, sems, 7)
    every[at["x"], at["z"]] = summed[...]
    for copy in copies:
        copy.wait()
    o_ref[...] = jnp.sum(every[...].reshape((16,) + summed.shape), axis=0)


def total_all(value):
    return pl.pallas_call(
        total_kernel,
        out_shape=jax.ShapeDtypeStruct(value.shape, value.dtype),
        in_specs=[pl.BlockSpec(memory_space=pltpu.VMEM)],
        out_specs=pl.BlockSpec(memory_space=pltpu.VMEM),
        scratch_shapes=[
            pltpu.VMEM((4, 2) + value.shape, value.dtype),
            pltpu.VMEM((4, 4) + value.shape, value.dtype),
            pltpu.VMEM(value.shape, value.dtype),
            pltpu.SemaphoreType.DMA((22,)),
            pltpu.SemaphoreType.DMA((22,)),
        ],
        compiler_params=pltpu.CompilerParams(collective_id=4, has_side_effects=True),
        name="total_all",
    )(value)


def across_cores(value):
    return lax.ppermute(value, "rep", CORE_SWAP)


def across_y(value):
    return lax.ppermute(value, "rep", Y_SWAP)


def shards(
    patches,
    expert_ids,
    labels,
    label_count,
    square_weights,
    router_weight,
    position_table,
    head_weight,
    expert_weights,
    vector_params,
    square_rows,
    square_cols,
    router_rows,
    router_cols,
    position_rows,
    position_cols,
    head_rows,
    head_cols,
    expert_rows,
    expert_cols,
    vector_moment,
):
    bfloat = jnp.bfloat16
    num_rep = lax.axis_size("rep")
    num_exp = lax.axis_size("exp")
    rep_index = lax.axis_index("rep")
    my_image = lax.axis_index("exp")
    device_index = lax.axis_index(("rep", "exp"))
    micro, core = rep_index // 2, rep_index % 2
    num_expert = router_weight.shape[1]
    vocab_dev = head_weight.shape[1]
    ff_dev = expert_weights.shape[3]
    block = patches.shape[2]
    rows, width = 2 * block, patches.shape[3]
    num_top = expert_ids.shape[3]
    heads = width // HEAD
    scale = HEAD ** (-0.5)
    own_rows = square_weights.shape[1]

    def pad_rows(value):
        return jnp.pad(value, ((0, PAD - own_rows), (0, width - value.shape[1])))

    mine = lax.dynamic_index_in_dim(patches, micro, 0, keepdims=False)[0]
    theirs = across_y(lax.dynamic_index_in_dim(patches, 1 - micro, 0, keepdims=False)[0])
    patch_rows = jnp.where(
        micro == 0, jnp.concatenate([mine, theirs]), jnp.concatenate([theirs, mine])
    )
    mine = lax.dynamic_index_in_dim(expert_ids, micro, 0, keepdims=False)[0]
    theirs = across_y(lax.dynamic_index_in_dim(expert_ids, 1 - micro, 0, keepdims=False)[0])
    ids = jnp.where(micro == 0, jnp.concatenate([mine, theirs]), jnp.concatenate([theirs, mine]))

    table_t = position_table.T
    table_high = lax.reduce_precision(table_t, 8, 7)
    table_low = (table_t - table_high).astype(bfloat)
    vector_t = vector_params.T
    vector_high = lax.reduce_precision(vector_t, 8, 7)
    vector_low = (vector_t - vector_high).astype(bfloat)
    extra = jnp.concatenate(
        [table_high.astype(bfloat), router_weight.astype(bfloat), vector_high.astype(bfloat), vector_low],
        axis=1,
    )
    square_low = square_weights.astype(bfloat)
    spare = jnp.pad(table_low, ((0, 0), (0, width - PATCHES))).reshape(3, 2, width)
    payload = jnp.concatenate(
        [square_low[0], spare[0], square_low[1], spare[1], square_low[2], spare[2]]
        + [pad_rows(square_low[3]), pad_rows(square_low[4]), pad_rows(extra)],
        axis=0,
    ).reshape(3, 16, width)
    *squares, extra, low = gather_all(payload)

    quarter = lax.optimization_barrier((expert_weights, extra))[0][0].astype(bfloat)
    quarter_y = across_y(quarter)
    table = (
        extra[:, :PATCHES].astype(jnp.float32) + low[:, :PATCHES].astype(jnp.float32)
    ).T
    router = extra[:, PATCHES : PATCHES + num_expert]
    begin = PATCHES + num_expert
    vectors = (
        extra[:, begin : begin + 10].astype(jnp.float32)
        + extra[:, begin + 10 : begin + 20].astype(jnp.float32)
    ).T
    table_rows = jnp.concatenate(
        [
            lax.dynamic_slice_in_dim(table, core * block, block, 0),
            lax.dynamic_slice_in_dim(table, (2 + core) * block, block, 0),
        ]
    )
    head_low = head_weight.astype(bfloat)
    valid = (label_count > 0).astype(jnp.float32)
    image_count = jnp.sum(valid)
    expert_range = jnp.arange(num_expert, dtype=jnp.int32)
    label_range = jnp.arange(labels.shape[2], dtype=jnp.int32)

    flat_hit = ids[:, :, None] == expert_range[None, None, :]
    flat_hit = flat_hit.reshape(2, block * num_top, num_expert).astype(jnp.int32)
    before = jnp.cumsum(flat_hit, axis=1) - flat_hit
    slot = jnp.sum(before * flat_hit, axis=2) + jnp.array([[0], [CAP]], jnp.int32)
    slot = slot.reshape(rows, num_top)
    target = jnp.where(slot < SLOTS, ids * SLOTS + slot, MAIN + ids * TAIL + slot - SLOTS)
    target_t = target.T

    def by_place(value):
        return value.reshape(2, 4, 2, 4, -1).transpose(1, 3, 0, 2, 4).reshape(2 * num_exp, -1)

    label_rows, count_rows = by_place(labels), by_place(label_count)
    live = label_range[None, :] < count_rows
    head_cols_pad = -(-vocab_dev // LANES) * LANES
    columns = device_index * vocab_dev + jnp.arange(head_cols_pad, dtype=jnp.int32)
    targets = jnp.any(
        (label_rows[:, :, None] == columns[None, None, :]) & live[:, :, None], axis=1
    ).astype(jnp.float32)
    valid_rows = (count_rows > 0).astype(jnp.float32)
    head_low = jnp.pad(head_low, ((0, 0), (0, head_cols_pad - vocab_dev)))

    slot_index = jnp.arange(num_exp * 4 * PAD, dtype=jnp.int32)

    def picker(which, offset):
        first = (slot_index // (num_exp * 2 * PAD)) * (2 * num_exp) + which * num_exp
        owner = first + (slot_index % (num_exp * 2 * PAD)) // (2 * PAD)
        inside = slot_index % (2 * PAD) - offset
        row = jnp.where((inside >= 0) & (inside < own_rows), owner * own_rows + inside, -1)
        return (jnp.arange(width, dtype=jnp.int32)[:, None] == row[None, :]).astype(bfloat)

    picks = {offset: (picker(core, offset), picker(1 - core, offset)) for offset in (0, PAD)}

    def share_left(value, offset):
        mine, theirs = (plain_dot(value, pick).astype(bfloat) for pick in picks[offset])
        return jnp.concatenate([mine, across_cores(theirs)])

    def share_right(value):
        return jnp.concatenate([value, across_cores(value)])

    left_patches = share_left(patch_rows, 0)
    vectors = jnp.pad(vectors, ((0, 6), (0, 0)))
    router = jnp.pad(router, ((0, 0), (0, LANES - num_expert)))
    embed, hidden_one, query, keys, values, mixed, after_attn, hidden_two, gate_probs, gates, lse = attend(
        patch_rows, squares, vectors, table_rows, router, ids
    )
    quarter_y, hidden_two = lax.optimization_barrier((quarter_y, hidden_two))
    received, chosen, after_moe, pool = experts_forward(
        hidden_two, target_t, target, gates, after_attn, vectors, quarter, quarter_y
    )
    row_grad, head_g, loss_part = head_step(
        pool, head_low, targets, valid_rows, image_count.reshape(1, 1)
    )
    head_g = head_g[:, :vocab_dev]
    loss_part = loss_part[0, 0]
    dmoe_in, dgate_logits, final_sums, dhidden, to_y, expert_g = experts_backward(
        row_grad, after_moe, chosen, gates, gate_probs, ids, received, target_t, target, vectors, quarter, quarter_y
    )
    from_y = across_y(to_y)
    left_one = [share_left(hidden_one, offset) for offset in (0, PAD)]
    left_mixed = share_left(mixed, 0)
    router_grad = over_rows(hidden_two, dgate_logits)[:, :num_expert]
    dafter_low, dquery_low, dkey_low, dvalue_low, dembed_low, sums = attend_back(
        dmoe_in,
        dhidden,
        dgate_logits,
        embed,
        after_attn,
        hidden_one,
        query,
        keys,
        values,
        lse,
        *squares[1:],
        vectors,
        router,
    )
    right_after = share_right(dafter_low)
    right_query, right_key, right_value = (
        share_right(value) for value in (dquery_low, dkey_low, dvalue_low)
    )
    right_embed = share_right(dembed_low)

    vector_grad = jnp.concatenate([sums, final_sums[:2]])
    few = jnp.concatenate([vector_grad, router_grad.T], axis=0)
    few = few + across_cores(few)
    count = few.shape[0]
    few_high = lax.reduce_precision(few, 8, 7)
    embed_all = jnp.where(
        core == 0, right_embed, jnp.concatenate([right_embed[rows:], right_embed[:rows]])
    )
    extra_right = jnp.concatenate(
        [embed_all, few_high.astype(bfloat), (few - few_high).astype(bfloat)]
        + [jnp.zeros((width - PATCHES - 2 * count, width), bfloat)],
        axis=0,
    ).T
    def pair(lefts, rights):
        total = over_rows(jnp.concatenate(lefts), jnp.concatenate(rights))
        return total.astype(bfloat).reshape(2, 4, 2, 4, 2 * PAD, width)

    owned = scatter_all(
        [
            pair([left_patches, left_one[1]], [right_embed, right_query]),
            pair([left_one[0], left_one[1]], [right_key, right_value]),
            pair([left_mixed, picks[PAD][0]], [right_after, extra_right]),
        ]
    )
    owned = [half for part in owned for half in (part[:own_rows], part[PAD : PAD + own_rows])]
    owned, from_y = lax.optimization_barrier((owned, from_y))
    expert_g = (expert_g + from_y.astype(jnp.float32))[None]
    square_g = jnp.stack(owned[:5])
    extra_g = owned[5]
    table_g = extra_g[:, :PATCHES].reshape(own_rows, 2, 2, block)
    table_g = table_g.transpose(0, 2, 1, 3).reshape(own_rows, PATCHES).T
    few_g = extra_g[:, PATCHES : PATCHES + count] + extra_g[:, PATCHES + count : PATCHES + 2 * count]
    vector_g = few_g[:, :10].T
    router_g = few_g[:, 10:]
    norm_part = (
        jnp.sum(square_g * square_g)
        + jnp.sum(router_g * router_g)
        + jnp.sum(table_g * table_g)
        + jnp.sum(vector_g * vector_g)
        + jnp.sum(head_g * head_g)
        + jnp.sum(expert_g * expert_g)
    )
    square_rowmean = jnp.mean(square_g * square_g, axis=2)
    router_rowmean = jnp.mean(router_g * router_g, axis=1)
    expert_rowsq = jnp.sum(expert_g * expert_g, axis=-1)
    expert_rowsq = expert_rowsq + across_cores(expert_rowsq)
    expert_mine = expert_rowsq + across_y(expert_rowsq)
    terms = (
        loss_part,
        norm_part,
        jnp.sum(square_g * square_g, axis=1),
        jnp.sum(square_rows, axis=1),
        jnp.sum(square_rowmean, axis=1),
        jnp.sum(router_g * router_g, axis=0),
        jnp.sum(router_rows),
        jnp.sum(router_rowmean),
        jnp.sum(table_g * table_g, axis=1),
        jnp.sum(head_g * head_g, axis=1),
    )
    flat = jnp.concatenate([term.reshape(-1) for term in terms])
    length = flat.shape[0]
    padded = -(-length // (8 * LANES)) * 8 * LANES
    flat = total_all(jnp.pad(flat, (0, padded - length)).reshape(-1, LANES)).reshape(-1)
    totals = []
    begin = 0
    for term in terms:
        totals.append(flat[begin : begin + term.size].reshape(term.shape))
        begin += term.size
    (
        loss_total,
        norm_total,
        square_colsq,
        square_rows_sum,
        square_mean_sum,
        router_colsq,
        router_rows_sum,
        router_mean_sum,
        table_rowsq,
        head_rowsq,
    ) = totals
    grad_norm = jnp.sqrt(norm_total)
    clip = jnp.minimum(1.0, CLIP_NORM / grad_norm)
    clip_sq = clip * clip
    keep = 1.0 - DECAY
    square_clip = clip * square_g
    square_rows_next = DECAY * square_rows + keep * (clip_sq * square_rowmean + EPS_SQ)
    square_cols_next = DECAY * square_cols + keep * (clip_sq * square_colsq / width + EPS_SQ)
    square_mean = (
        DECAY * square_rows_sum + keep * (clip_sq * square_mean_sum + width * EPS_SQ)
    ) / width
    square_rate = jnp.array([1.0, 1.0, 1.0, 1.0, 4.0], jnp.float32)[:, None, None] * (
        0.3 / math.sqrt(D)
    )
    square_next = factored_step(
        square_weights,
        square_clip,
        square_rows_next,
        square_cols_next,
        square_mean[:, None, None],
        square_rate,
    )
    router_clip = clip * router_g
    router_rows_next = DECAY * router_rows + keep * (clip_sq * router_rowmean + EPS_SQ)
    router_cols_next = DECAY * router_cols + keep * (clip_sq * router_colsq / width + EPS_SQ)
    router_mean = (
        DECAY * router_rows_sum + keep * (clip_sq * router_mean_sum + width * EPS_SQ)
    ) / width
    router_next = factored_step(
        router_weight,
        router_clip,
        router_rows_next,
        router_cols_next,
        router_mean,
        0.2 / math.sqrt(D),
    )
    table_clip = clip * table_g
    table_rows_next = DECAY * position_rows + keep * (clip_sq * table_rowsq / width + EPS_SQ)
    table_cols_next = DECAY * position_cols + keep * (
        clip_sq * jnp.mean(table_g * table_g, axis=0) + EPS_SQ
    )
    table_next = factored_step(
        position_table,
        table_clip,
        table_rows_next,
        table_cols_next,
        jnp.mean(table_rows_next),
        0.15,
    )
    head_clip = clip * head_g
    head_rows_next = DECAY * head_rows + keep * (
        clip_sq * head_rowsq / (vocab_dev * num_rep * num_exp) + EPS_SQ
    )
    head_cols_next = DECAY * head_cols + keep * (
        clip_sq * jnp.mean(head_g * head_g, axis=0) + EPS_SQ
    )
    head_next = factored_step(
        head_weight,
        head_clip,
        head_rows_next,
        head_cols_next,
        jnp.mean(head_rows_next),
        0.5 / math.sqrt(D),
    )
    expert_clip = clip * expert_g
    expert_rows_next = DECAY * expert_rows + keep * (
        clip_sq * expert_mine / (ff_dev * num_rep) + EPS_SQ
    )
    expert_cols_next = DECAY * expert_cols + keep * (
        clip_sq * jnp.mean(expert_g * expert_g, axis=2) + EPS_SQ
    )
    expert_rate = jnp.array([0.3 / math.sqrt(D), 4.8 / math.sqrt(FF)], jnp.float32)[
        None, :, None, None
    ]
    expert_next = factored_step(
        expert_weights,
        expert_clip,
        expert_rows_next,
        expert_cols_next,
        jnp.mean(expert_rows_next, axis=-1)[..., None, None],
        expert_rate,
    )
    vector_clip = clip * vector_g
    moment_next = DECAY * vector_moment + keep * (vector_clip * vector_clip + EPS_SQ)
    vector_next = vector_params - 0.3 * vector_clip * lax.rsqrt(moment_next)
    return (
        loss_total,
        image_count,
        grad_norm,
        square_clip,
        square_rows_next,
        square_cols_next,
        square_next,
        router_clip,
        router_rows_next,
        router_cols_next,
        router_next,
        table_clip,
        table_rows_next,
        table_cols_next,
        table_next,
        head_clip,
        head_rows_next,
        head_cols_next,
        head_next,
        expert_clip,
        expert_rows_next,
        expert_cols_next,
        expert_next,
        vector_clip,
        moment_next,
        vector_next,
    )


def solution(mesh):
    in_specs = (
        P(None, "exp", "rep", None),
        P(None, "exp", "rep", None),
        P(),
        P(),
        P(None, ("rep", "exp"), None),
        P(("rep", "exp"), None),
        P(None, ("rep", "exp")),
        P(None, ("rep", "exp")),
        P("exp", None, None, "rep"),
        P(None, ("rep", "exp")),
        P(None, ("rep", "exp")),
        P(),
        P(("rep", "exp")),
        P(),
        P(),
        P(("rep", "exp")),
        P(),
        P(("rep", "exp")),
        P("exp", None, None),
        P("exp", None, "rep"),
        P(None, ("rep", "exp")),
    )
    out_specs = (
        P(),
        P(),
        P(),
        P(None, ("rep", "exp"), None),
        P(None, ("rep", "exp")),
        P(),
        P(None, ("rep", "exp"), None),
        P(("rep", "exp"), None),
        P(("rep", "exp")),
        P(),
        P(("rep", "exp"), None),
        P(None, ("rep", "exp")),
        P(),
        P(("rep", "exp")),
        P(None, ("rep", "exp")),
        P(None, ("rep", "exp")),
        P(),
        P(("rep", "exp")),
        P(None, ("rep", "exp")),
        P("exp", None, None, "rep"),
        P("exp", None, None),
        P("exp", None, "rep"),
        P("exp", None, None, "rep"),
        P(None, ("rep", "exp")),
        P(None, ("rep", "exp")),
        P(None, ("rep", "exp")),
    )
    return jax.shard_map(shards, mesh=mesh, in_specs=in_specs, out_specs=out_specs, check_vma=False)
```

time: 732 us -> 466 us (0.64)
  matrix products: 147 us -> 26.5 us
  local copies, waits for them, and re-layouts: 111 us -> 34 us
  other arithmetic: 96 us -> 54.4 us
  Pallas kernels: 341 us -> 312 us
  starting transfers between devices: 17.6 us -> 25.4 us
    dot_general x22 -> x0, matrix products: 51.6 us -> none  [the longest x14 25.7 us: over_last(): lax.dot_general(left, right, (((1,), (1,)), ((), ())), preferred_element_...]
    pallas_call x1, Pallas kernels: 96.7 us -> 64.3 us  [scatter_all(): pl.pallas_call(scatter_kernel, out_shape=[jax.ShapeDtypeStruct(block, jnp...]
    dot_general x23 -> x8, matrix products: 43.9 us -> 12.7 us  [plain_dot(): return jnp.dot(left, right, preferred_element_type=jnp.float32)]
    dot_general x17 -> x4, matrix products: 43.8 us -> 13.8 us  [over_rows(): lax.dot_general(left, right, (((0,), (0,)), ((), ())), preferred_element_...]
    reshape x18 -> x3, local copies, waits for them, and re-layouts: 25.8 us -> 0.71 us  [by_place(): value.reshape(2, 4, 2, 4, -1).transpose(1, 3, 0, 2, 4)]
    another operation x13 -> x3, local copies, waits for them, and re-layouts: 19.4 us -> 0.01 us  [the longest x5 16.2 us: shards(): gathered[k // 2][:, k % 2, :own_rows].reshape(width, width)]
    another operation x10 -> x4, other arithmetic: 18.3 us -> 1.86 us  [the longest x2 7.53 us: shards(): from_core = across_cores(jnp.stack([quarter_grads[2], quarter_grads[3]]))]
    slice x11 -> x7, local copies, waits for them, and re-layouts: 13.5 us -> 1.07 us  [the longest x1 0.74 us: shards(): vector_grad = jnp.concatenate([sums, final_sums[:2]])]
  transfers between devices with their start and end apart: 18 -> 16, of which waited for: 1 -> 0; matrix products, arithmetic and copies ran while one was open for 42% -> 17% of each run, Pallas kernels for 45% -> 63%
where the time goes in v2:
time: 466 us; the launch traced here: 463 us
  Pallas kernels  312 us (67%)
  other arithmetic  54.4 us (12%)
  local copies, waits for them, and re-layouts  34 us (7%)
  matrix products  26.5 us (6%)
  starting transfers between devices  25.4 us (5%)
  between operations  10.5 us (2%)
    pallas_call x1, Pallas kernels, scatter_all(): pl.pallas_call(scatter_kernel, out_shape=[jax.ShapeDtypeStruct(block, jnp...  64.3 us
    pallas_call x1, Pallas kernels, experts_backward(): pl.pallas_call(experts_back_kernel, out_shape=[jax.ShapeDtypeStruct(*shap...  60.6 us
    pallas_call x1, Pallas kernels, experts_forward(): pl.pallas_call(experts_kernel, out_shape=[jax.ShapeDtypeStruct(*shape) fo...  48.8 us
    pallas_call x1, Pallas kernels, gather_all(): pl.pallas_call(gather_kernel, out_shape=[jax.ShapeDtypeStruct((D, D), pay...  42.8 us
    pallas_call x1, Pallas kernels, head_step(): pl.pallas_call(head_kernel, out_shape=[jax.ShapeDtypeStruct(block, wide),...  31.6 us
    pallas_call x1, Pallas kernels, attend_back(): pl.pallas_call(attend_back_kernel, out_shape=[jax.ShapeDtypeStruct((rows,...  22.5 us
    pallas_call x1, Pallas kernels, total_all(): pl.pallas_call(total_kernel, out_shape=jax.ShapeDtypeStruct(value.shape,...  20.6 us
    pallas_call x1, Pallas kernels, attend(): pl.pallas_call(attend_kernel, out_shape=[jax.ShapeDtypeStruct(*shape) for...  20.5 us
  transfers between devices with their start and end apart: 16, of which 0 were waited for; matrix products, arithmetic and copies ran while one was open for 17% of the time, Pallas kernels for 63%

profile of v2, /device:TPU:1, one launch (start us, length us, event | category | flops | bytes accessed | tf_op | source)
XLA Modules:
  0.0 462.7 jit_solution(8991434215527735660)
XLA Ops:
  0.7 1.3 fusion.132
  2.0 3.7 collective-permute-start.2
  5.7 1.8 dynamic-slice_bitcast_fusion.3
  10.8 42.8 %gather_weights.1 = (bf16[768,768]{1,0:T(8,128)(2,1)S(1)}, bf16[768,768]{1,0:T(8,128)(2,1)S(1)}, bf16[768,768]{1,0:T(8,128)(2,1)S(1)}, bf16[768,768]{1,0:T(8,128...) custom-call(bf16[3,16,768]{2,1,0:T(8,128)(2,1)S(1)} %bitcast.127), custom_call_target="tpu_custom_call" | custom-call | tf_op jit(solution)/shard_map/gather_weights/pallas_call | solution.py:203
  53.7 6.0 %convert_bitcast_fusion.own = bf16[2,768,768]{2,1,0:T(8,128)(2,1)} fusion(f32[1,2,768,768]{3,2,1,0:T(8,128)} %param.32), kind=kLoop, calls=%fused_computation.38 | loop fusion | flops 1179648 | bytes 7077888 | tf_op jit(solution)/shard_map/convert_element_type | solution.py:1195
  59.7 1.5 collective-permute-start
  63.1 1.3 fusion.133
  65.6 1.4 copy.171
  67.7 1.6 convert_add_fusion.1
  70.9 1.7 fusion
  73.7 1.4 and_reduce_fusion
  75.3 1.2 copy.191
  81.2 1.8 reduce-window.6
  84.8 1.2 maximum_select_fusion.1.x_ref
  86.0 20.5 %attend.1 = (f32[288,768]{1,0:T(8,128)S(1)}, bf16[288,768]{1,0:T(8,128)(2,1)S(1)}, bf16[288,768]{1,0:T(8,128)(2,1)S(1)}, bf16[2,288,768]{2,1,0:T(8,128)(2,1)S(1)...) custom-call(bf16[288,768]{1,0:T(8,128)(2,1)S(1)} %maximum_select_fus, ...), custom_call_target="tpu_custom_call" | custom-call | tf_op jit(solution)/shard_map/attend/pallas_call | solution.py:415
  106.7 1.6 fusion.54
  108.2 11.8 %collective-permute-start.4 = (bf16[288,1024]{1,0:T(8,128)(2,1)}, bf16[288,1024]{1,0:T(8,128)(2,1)}, u32[]{:S(2)}, u32[]{:S(2)}) collective-permute-start(bf16[288,1024]{1,0:T(8,128)(2,1)} %fusion.54), channel_id=1, source_target_pairs={{0,32},{32,0},{64,96},{96,64},{1,33},{33,1},{65,97},{97,65},{2,34}... | collective-permute-start | bytes 1769480 | tf_op jit(solution)/shard_map/ppermute | solution.py:1117
  120.0 1.6 fusion.58
  122.0 1.6 fusion.59
  123.6 1.6 fusion.60
  125.2 1.6 fusion.57
  126.8 1.6 fusion.56
  128.4 1.6 fusion.61
  130.0 1.6 fusion.55
  131.6 48.8 %experts_forward.1 = (bf16[640,768]{1,0:T(8,128)(2,1)S(1)}, bf16[2,288,768]{2,1,0:T(8,128)(2,1)S(1)}, f32[288,768]{1,0:T(8,128)S(1)}, f32[8,128]{1,0:T(8,128)S(1)}) custom-call(bf16[288,768]{1,0:T(8,128)(2,1)S(1)} %get-tuple-element.85.hidden, s32[2,288]{1,0:T(2,128)S(1)} %copy.179.target_row, s32[288,2]{1,0:T(8,128)S(1)} %get-tuple-element.312.target_column, ...), custom_call_target="tpu_custom_call" | custom-call | tf_op jit(solution)/shard_map/experts_forward/pallas_call | solution.py:765
  183.8 31.6 %head_step.1 = (f32[8,128]{1,0:T(8,128)}, f32[768,256]{1,0:T(8,128)}, f32[1,1]{1,0:T(1,128)}) custom-call(f32[8,128]{1,0:T(8,128)} %copy-done.23, bf16[768,256]{1,0:T(8,128)(2,1)} %pad.42.head, f32[64,256]{1,0:T(8,128)} %convert_element_type.130.targets, f32[64,1]{1,0:T(8,128)} %reshape.376.valid, f32[1,1]{1,0:T(1,128)} %bitcast.25.count), custom_call_target="tpu_custom_call" | custom-call | tf_op jit(solution)/shard_map/head_step/pallas_call | solution.py:1057
  215.5 60.6 %experts_backward.1 = (f32[288,768]{1,0:T(8,128)}, bf16[288,128]{1,0:T(8,128)(2,1)}, f32[8,768]{1,0:T(8,128)}, f32[288,768]{1,0:T(8,128)}, bf16[2,768,768]{2,1,0:T(8,128)(2,1)}, /*index=5*/f32[2,768,768]{2,1,0:T(8,128)}) custom-call(f32[8,128]{1,0:T(8,128)} %get-tuple-element.92.row_grad, f32[288,768]{1,0:T(8,128)} %copy-done.12, ...), custom_call_target="tpu_custom_call" | custom-call | tf_op jit(solution)/shard_map/experts_backward/pallas_call | solution.py:948
  276.1 1.1 convolution_bitcast_fusion
  277.3 1.2 copy-done.15
  278.4 1.2 copy-done.16
  280.5 22.5 %attend_back.1 = (bf16[288,768]{1,0:T(8,128)(2,1)S(1)}, bf16[288,768]{1,0:T(8,128)(2,1)S(1)}, bf16[288,768]{1,0:T(8,128)(2,1)}, bf16[288,768]{1,0:T(8,128)(2,1)}...) custom-call(f32[288,768]{1,0:T(8,128)S(1)} %copy-done.15, f32[288,768]{1,0:T(8,128)S(1)} %copy-done.16, ...), custom_call_target="tpu_custom_call" | custom-call | tf_op jit(solution)/shard_map/attend_back/pallas_call | solution.py:531
  304.8 1.1 copy.187
  305.8 1.9 fusion.62
  309.7 2.8 collective-permute-start.13
  312.5 4.4 fusion.40
  318.3 2.1 copy.188
  320.4 4.9 %concatenate.92 = bf16[1344,768]{0,1:T(8,128)(2,1)} concatenate(bf16[288,768]{0,1:T(8,128)(2,1)S(1)} %copy-done.27, bf16[288,768]{0,1:T(8,128)(2,1)} %copy.188, bf16[768,768]{0,1:T(8,128)(2,1)S(1)} %maximum_bitcast_fusion), dimensions={0} | concatenate | bytes 4128768 | tf_op jit(solution)/shard_map/concatenate | solution.py:1314
  325.4 4.5 fusion.37
  329.9 3.8 fusion.43
  333.7 64.3 %scatter_grads.1 = (f32[16,768]{1,0:T(8,128)S(1)}, f32[16,768]{1,0:T(8,128)S(1)}, f32[16,768]{1,0:T(8,128)S(1)}) custom-call(bf16[2,4,2,4,16,768]{5,4,3,2,1,0:T(8,128)(2,1)S(1)} %bitcast.124, bf16[2,4,2,4,16,768]{5,4,3,2,1,0:T(8,128)(2,1)S(1)} %bitcast.125, bf16[2,4,2,4,16,768]{5,4,3,2,1,0:T(8,128)(2,1)S(1)} %bitcast.126), custom_call_target="tpu_custom_call" | custom-call | tf_op jit(solution)/shard_map/scatter_grads/pallas_call | solution.py:291
  401.7 5.2 %multiply_reduce_fusion = (f32[2,768]{1,0:T(2,128)S(1)}, f32[2,768]{1,0:T(2,128)S(1)}, f32[]{:T(128)}) fusion(f32[2,768,768]{2,1,0:T(8,128)} %get-tuple-element.124, bf16[2,768,768]{2,1,0:T(8,128)(2,1)} %collective-permute-done.13), kind=kLoop, calls=%fused_computation.4 | loop fusion | flops 7074815 | bytes 7090180 | tf_op jit(solution)/shard_map/reduce_sum | solution.py:1448
  410.8 2.1 concatenate.93
  413.5 20.6 %total_all.1 = f32[48,128]{1,0:T(8,128)} custom-call(f32[48,128]{1,0:T(8,128)} %pad_bitcast_fusion.x_ref), custom_call_target="tpu_custom_call" | custom-call | tf_op jit(solution)/shard_map/total_all/pallas_call | solution.py:1099
  434.1 1.4 fusion.153
  436.3 5.8 %multiply_bitcast_fusion = f32[1,2,768,768]{3,2,1,0:T(8,128)} fusion(f32[]{:T(128)S(6)} %min_shard_map.3, f32[2,768,768]{2,1,0:T(8,128)} %get-tuple-element.124, bf16[2,768,768]{2,1,0:T(8,128)(2,1)} %collective-permute-done.13), kind=kLoop, calls=%fused_computation.2 | loop fusion | flops 3538944 | bytes 11796484 | tf_op jit(solution)/shard_map/mul | solution.py:1443
  443.0 1.3 collective-permute-start.14
  450.5 1.3 collective-permute-start.15
  454.8 6.5 %bitcast_subtract_fusion = f32[1,2,768,768]{3,2,1,0:T(8,128)} fusion(f32[1,2,768,768]{3,2,1,0:T(8,128)} %param.32, f32[2]{0:T(128)S(1)} %broadcast_multiply_fusion.1, f32[2,768]{1,0:T(2,128)S(1)} %bitcast.139, f32[2,768]{1,0:T(2,128)S(1)} %bitcast.140, f32[2]{0:T(128)S(1)} %copy-done.69, f32[]{:T(128)S(6)} %min_shard_map.3, ...), kind=kLoop, calls=%fused_computation | loop fusion | flops 9437184 | bytes 16527380 | tf_op jit(solution)/shard_map/sub | solution.py:55
  (290 shorter events, 37.5 us)
Async XLA Ops:
  2.0 78.0 %collective-permute-start.2 = (s32[144,2]{0,1:T(2,128)}, s32[144,2]{0,1:T(2,128)}, u32[]{:S(2)}, u32[]{:S(2)}) collective-permute-start(s32[144,2]{0,1:T(2,128)} %get-tuple-element.344), channel_id=1, source_target_pairs={{0,64},{32,96},{64,0},{96,32},{1,65},{33,97},{65,1},{97,33},{2,66}... | collective-permute-start | bytes 3464 | tf_op jit(solution)/shard_map/ppermute | solution.py:1121
  7.6 77.2 %collective-permute-start.1 = (bf16[144,768]{1,0:T(8,128)(2,1)}, bf16[144,768]{1,0:T(8,128)(2,1)}, u32[]{:S(2)}, u32[]{:S(2)}) collective-permute-start(bf16[144,768]{1,0:T(8,128)(2,1)} %get-tuple-element.317), channel_id=1, source_target_pairs={{0,64},{32,96},{64,0},{96,32},{1,65},{33,97},{65,1},{97,33},{2,66}... | collective-permute-start | bytes 663560 | tf_op jit(solution)/shard_map/ppermute | solution.py:1121
  53.6 8.8 %copy-start.67 = (s32[2,32]{1,0:T(2,128)S(1)}, s32[2,32]{1,0:T(2,128)}, u32[]{:S(2)}) copy-start(s32[2,32]{1,0:T(2,128)} %param.27) | copy-start | bytes 772
  59.7 71.8 %collective-permute-start = (bf16[2,768,768]{2,1,0:T(8,128)(2,1)}, bf16[2,768,768]{2,1,0:T(8,128)(2,1)}, u32[]{:S(2)}, u32[]{:S(2)}) collective-permute-start(bf16[2,768,768]{2,1,0:T(8,128)(2,1)} %convert_bitcast_fusion.own), channel_id=1, source_target_pairs={{0,64},{32,96},{64,0},{96,32},{1,65},{33,97},{65,1},{97,33},{2,66}... | collective-permute-start | bytes 7077896 | tf_op jit(solution)/shard_map/ppermute | solution.py:1121
  75.3 8.2 %copy-start.52 = (s32[144,2]{0,1:T(2,128)S(1)}, s32[144,2]{0,1:T(2,128)}, u32[]{:S(2)}) copy-start(s32[144,2]{0,1:T(2,128)} %get-tuple-element.342) | copy-start | bytes 3460
  75.3 9.5 %copy-start.31 = (bf16[144,768]{1,0:T(8,128)(2,1)S(1)}, bf16[144,768]{1,0:T(8,128)(2,1)}, u32[]{:S(2)}) copy-start(bf16[144,768]{1,0:T(8,128)(2,1)} %get-tuple-element.316) | copy-start | bytes 663556
  79.2 52.4 %copy-start.7 = (f32[16,768]{1,0:T(8,128)}, f32[16,768]{1,0:T(8,128)S(1)}, u32[]{:S(2)}) copy-start(f32[16,768]{1,0:T(8,128)S(1)} %pad.39.vec) | copy-start | bytes 147460
  84.7 21.9 %copy-start.6 = (s32[288,2]{1,0:T(8,128)}, s32[288,2]{1,0:T(8,128)S(1)}, u32[]{:S(2)}) copy-start(s32[288,2]{1,0:T(8,128)S(1)} %get-tuple-element.313.ids) | copy-start | bytes 6916
  84.7 46.9 %copy-start.5 = (s32[288,2]{1,0:T(8,128)}, s32[288,2]{1,0:T(8,128)S(1)}, u32[]{:S(2)}) copy-start(s32[288,2]{1,0:T(8,128)S(1)} %get-tuple-element.312.target_column) | copy-start | bytes 6916
  84.8 46.8 %copy-start.22 = (s32[2,288]{1,0:T(2,128)}, s32[2,288]{1,0:T(2,128)S(1)}, u32[]{:S(2)}) copy-start(s32[2,288]{1,0:T(2,128)S(1)} %copy.179.target_row) | copy-start | bytes 6916
  86.0 20.6 %copy-start.59 = (s32[1024]{0:T(1024)S(1)}, s32[1024]{0:T(1024)}, u32[]{:S(2)}) copy-start(s32[1024]{0:T(1024)} %add_select_fusion.4) | copy-start | bytes 12292
  106.6 15.0 %copy-start.13 = (bf16[2,288,768]{2,1,0:T(8,128)(2,1)}, bf16[2,288,768]{2,1,0:T(8,128)(2,1)S(1)}, u32[]{:S(2)}) copy-start(bf16[2,288,768]{2,1,0:T(8,128)(2,1)S(1)} %get-tuple-element.102.keys) | copy-start | bytes 2654212
  106.6 15.0 %copy-start.14 = (bf16[2,288,768]{2,1,0:T(8,128)(2,1)}, bf16[2,288,768]{2,1,0:T(8,128)(2,1)S(1)}, u32[]{:S(2)}) copy-start(bf16[2,288,768]{2,1,0:T(8,128)(2,1)S(1)} %get-tuple-element.103.values) | copy-start | bytes 2654212
  106.6 14.9 %copy-start.21 = (f32[288,128]{1,0:T(8,128)}, f32[288,128]{1,0:T(8,128)S(1)}, u32[]{:S(2)}) copy-start(f32[288,128]{1,0:T(8,128)S(1)} %get-tuple-element.95.gate_probs) | copy-start | bytes 442372
  106.6 25.0 %copy-start.17 = (f32[288,128]{1,0:T(8,128)}, f32[288,128]{1,0:T(8,128)S(1)}, u32[]{:S(2)}) copy-start(f32[288,128]{1,0:T(8,128)S(1)} %get-tuple-element.86.gates) | copy-start | bytes 442372
  106.6 13.4 %copy-start.58 = (s32[1024]{0:T(1024)S(1)}, s32[1024]{0:T(1024)}, u32[]{:S(2)}) copy-start(s32[1024]{0:T(1024)} %add_select_fusion.6) | copy-start | bytes 12292
  108.2 199.7 %collective-permute-start.4 = (bf16[288,1024]{1,0:T(8,128)(2,1)}, bf16[288,1024]{1,0:T(8,128)(2,1)}, u32[]{:S(2)}, u32[]{:S(2)}) collective-permute-start(bf16[288,1024]{1,0:T(8,128)(2,1)} %fusion.54), channel_id=1, source_target_pairs={{0,32},{32,0},{64,96},{96,64},{1,33},{33,1},{65,97},{97,65},{2,34}... | collective-permute-start | bytes 1769480 | tf_op jit(solution)/shard_map/ppermute | solution.py:1117
  121.6 186.9 %collective-permute-start.3 = (bf16[288,1024]{1,0:T(8,128)(2,1)}, bf16[288,1024]{1,0:T(8,128)(2,1)}, u32[]{:S(2)}, u32[]{:S(2)}) collective-permute-start(bf16[288,1024]{1,0:T(8,128)(2,1)} %fusion.58), channel_id=1, source_target_pairs={{0,32},{32,0},{64,96},{96,64},{1,33},{33,1},{65,97},{97,65},{2,34}... | collective-permute-start | bytes 1769480 | tf_op jit(solution)/shard_map/ppermute | solution.py:1117
  215.5 61.8 %copy-start.8 = (f32[16,768]{1,0:T(8,128)S(1)}, f32[16,768]{1,0:T(8,128)}, u32[]{:S(2)}) copy-start(f32[16,768]{1,0:T(8,128)} %copy-done.7) | copy-start | bytes 147460
  303.0 5.6 %collective-permute-start.5 = (bf16[288,768]{1,0:T(8,128)(2,1)S(1)}, bf16[288,768]{1,0:T(8,128)(2,1)S(1)}, u32[]{:S(2)}, u32[]{:S(2)}) collective-permute-start(bf16[288,768]{1,0:T(8,128)(2,1)S(1)} %get-tuple-element.105), channel_id=1, source_target_pairs={{0,32},{32,0},{64,96},{96,64},{1,33},{33,1},{65,97},{97,65},{2,34}... | collective-permute-start | bytes 1327112 | tf_op jit(solution)/shard_map/ppermute | solution.py:1117
  304.2 4.8 %collective-permute-start.6 = (bf16[288,768]{1,0:T(8,128)(2,1)S(1)}, bf16[288,768]{1,0:T(8,128)(2,1)S(1)}, u32[]{:S(2)}, u32[]{:S(2)}) collective-permute-start(bf16[288,768]{1,0:T(8,128)(2,1)S(1)} %get-tuple-element.106), channel_id=1, source_target_pairs={{0,32},{32,0},{64,96},{96,64},{1,33},{33,1},{65,97},{97,65},{2,34}... | collective-permute-start | bytes 1327112 | tf_op jit(solution)/shard_map/ppermute | solution.py:1117
  304.3 3.4 collective-permute-start.12
  307.8 17.5 %collective-permute-start.7 = (bf16[288,1024]{1,0:T(8,128)(2,1)}, bf16[288,1024]{1,0:T(8,128)(2,1)}, u32[]{:S(2)}, u32[]{:S(2)}) collective-permute-start(bf16[288,1024]{1,0:T(8,128)(2,1)} %fusion.59), channel_id=1, source_target_pairs={{0,32},{32,0},{64,96},{96,64},{1,33},{33,1},{65,97},{97,65},{2,34}... | collective-permute-start | bytes 1769480 | tf_op jit(solution)/shard_map/ppermute | solution.py:1117
  308.0 9.3 %collective-permute-start.11 = (bf16[288,768]{1,0:T(8,128)(2,1)S(1)}, bf16[288,768]{1,0:T(8,128)(2,1)S(1)}, u32[]{:S(2)}, u32[]{:S(2)}) collective-permute-start(bf16[288,768]{1,0:T(8,128)(2,1)S(1)} %get-tuple-element.110), channel_id=1, source_target_pairs={{0,32},{32,0},{64,96},{96,64},{1,33},{33,1},{65,97},{97,65},{2,34}... | collective-permute-start | bytes 1327112 | tf_op jit(solution)/shard_map/ppermute | solution.py:1117
  308.4 16.9 %collective-permute-start.8 = (bf16[288,768]{1,0:T(8,128)(2,1)}, bf16[288,768]{1,0:T(8,128)(2,1)}, u32[]{:S(2)}, u32[]{:S(2)}) collective-permute-start(bf16[288,768]{1,0:T(8,128)(2,1)} %get-tuple-element.107), channel_id=1, source_target_pairs={{0,32},{32,0},{64,96},{96,64},{1,33},{33,1},{65,97},{97,65},{2,34}... | collective-permute-start | bytes 1327112 | tf_op jit(solution)/shard_map/ppermute | solution.py:1117
  308.6 16.8 %collective-permute-start.9 = (bf16[288,768]{1,0:T(8,128)(2,1)}, bf16[288,768]{1,0:T(8,128)(2,1)}, u32[]{:S(2)}, u32[]{:S(2)}) collective-permute-start(bf16[288,768]{1,0:T(8,128)(2,1)} %get-tuple-element.108), channel_id=1, source_target_pairs={{0,32},{32,0},{64,96},{96,64},{1,33},{33,1},{65,97},{97,65},{2,34}... | collective-permute-start | bytes 1327112 | tf_op jit(solution)/shard_map/ppermute | solution.py:1117
  309.7 88.4 %collective-permute-start.13 = (bf16[2,768,768]{2,1,0:T(8,128)(2,1)}, bf16[2,768,768]{2,1,0:T(8,128)(2,1)}, u32[]{:S(2)}, u32[]{:S(2)}) collective-permute-start(bf16[2,768,768]{2,1,0:T(8,128)(2,1)} %get-tuple-element.116), channel_id=1, source_target_pairs={{0,64},{32,96},{64,0},{96,32},{1,65},{33,97},{65,1},{97,33},{2,66}... | collective-permute-start | bytes 7077896 | tf_op jit(solution)/shard_map/ppermute | solution.py:1121
  317.3 12.6 %collective-permute-start.10 = (bf16[288,1024]{1,0:T(8,128)(2,1)}, bf16[288,1024]{1,0:T(8,128)(2,1)}, u32[]{:S(2)}, u32[]{:S(2)}) collective-permute-start(bf16[288,1024]{1,0:T(8,128)(2,1)} %fusion.60), channel_id=1, source_target_pairs={{0,32},{32,0},{64,96},{96,64},{1,33},{33,1},{65,97},{97,65},{2,34}... | collective-permute-start | bytes 1769480 | tf_op jit(solution)/shard_map/ppermute | solution.py:1117
  436.2 8.0 %copy-start.60 = (f32[768]{0:T(1024)S(1)}, f32[768]{0:T(1024)}, u32[]{:S(2)}) copy-start(f32[768]{0:T(1024)} %param.40) | copy-start | bytes 9220
  436.2 9.4 %copy-start.61 = (f32[576]{0:T(1024)S(1)}, f32[576]{0:T(1024)}, u32[]{:S(2)}) copy-start(f32[576]{0:T(1024)} %param.38) | copy-start | bytes 6916
  436.2 10.9 %copy-start.72 = (f32[32]{0:T(128)S(1)}, f32[32]{0:T(128)}, u32[]{:S(2)}) copy-start(f32[32]{0:T(128)} %param.37) | copy-start | bytes 388
  436.2 11.0 %copy-start.54 = (f32[1,2,768]{2,1,0:T(2,128)S(1)}, f32[1,2,768]{2,1,0:T(2,128)}, u32[]{:S(2)}) copy-start(f32[1,2,768]{2,1,0:T(2,128)} %param.43) | copy-start | bytes 18436
  436.2 11.0 %copy-start.68 = (f32[171]{0:T(256)S(1)}, f32[171]{0:T(256)}, u32[]{:S(2)}) copy-start(f32[171]{0:T(256)} %param.41) | copy-start | bytes 2056
  436.3 11.1 %copy-start.45 = (f32[5,768]{1,0:T(8,128)S(1)}, f32[5,768]{1,0:T(8,128)}, u32[]{:S(2)}) copy-start(f32[5,768]{1,0:T(8,128)} %param.35) | copy-start | bytes 46084
  436.3 11.1 %copy-start.73 = (f32[6]{0:T(128)S(1)}, f32[6]{0:T(128)}, u32[]{:S(2)}) copy-start(f32[6]{0:T(128)} %param.39) | copy-start | bytes 76
  436.3 11.1 %copy-start.25 = (f32[768,171]{1,0:T(8,128)S(1)}, f32[768,171]{1,0:T(8,128)}, u32[]{:S(2)}) copy-start(f32[768,171]{1,0:T(8,128)} %copy.191) | copy-start | bytes 1575940
  436.3 11.1 %copy-start.26 = (f32[768,256]{1,0:T(8,128)S(1)}, f32[768,256]{1,0:T(8,128)}, u32[]{:S(2)}) copy-start(f32[768,256]{1,0:T(8,128)} %get-tuple-element.123) | copy-start | bytes 2359300
  442.2 9.6 %copy-start.51 = (f32[6,32]{1,0:T(8,128)S(1)}, f32[6,32]{1,0:T(8,128)}, u32[]{:S(2)}) copy-start(f32[6,32]{1,0:T(8,128)} %param.29) | copy-start | bytes 2308
  443.0 7.5 %collective-permute-start.14 = (f32[1,2,768]{2,1,0:T(2,128)S(1)}, f32[1,2,768]{2,1,0:T(2,128)S(1)}, u32[]{:S(2)}, u32[]{:S(2)}) collective-permute-start(f32[1,2,768]{2,1,0:T(2,128)S(1)} %bitcast.141), channel_id=1, source_target_pairs={{0,32},{32,0},{64,96},{96,64},{1,33},{33,1},{65,97},{97,65},{2,34}... | collective-permute-start | bytes 18440 | tf_op jit(solution)/shard_map/ppermute | solution.py:1117
  444.9 9.6 %copy-start.47 = (f32[768]{0:T(1024)}, f32[768]{0:T(1024)S(1)}, u32[]{:S(2)}) copy-start(f32[768]{0:T(1024)S(1)} %get-tuple-element.305) | copy-start | bytes 9220
  446.3 8.3 %copy-start.50 = (f32[576]{0:T(1024)}, f32[576]{0:T(1024)S(1)}, u32[]{:S(2)}) copy-start(f32[576]{0:T(1024)S(1)} %get-tuple-element.307) | copy-start | bytes 6916
  447.1 7.4 %copy-start.40 = (f32[6,576]{1,0:T(8,128)}, f32[6,576]{1,0:T(8,128)S(1)}, u32[]{:S(2)}) copy-start(f32[6,576]{1,0:T(8,128)S(1)} %mul.593) | copy-start | bytes 41476
  447.2 7.3 %copy-start.64 = (f32[32]{0:T(128)}, f32[32]{0:T(128)S(1)}, u32[]{:S(2)}) copy-start(f32[32]{0:T(128)S(1)} %fusion.137) | copy-start | bytes 388
  447.2 7.3 %copy-start.46 = (f32[5,6]{1,0:T(8,128)}, f32[5,6]{1,0:T(8,128)S(1)}, u32[]{:S(2)}) copy-start(f32[5,6]{1,0:T(8,128)S(1)} %multiply_add_fusion.3) | copy-start | bytes 364
  447.3 7.5 %copy-start.43 = (f32[1,2,768]{2,1,0:T(2,128)}, f32[1,2,768]{2,1,0:T(2,128)S(1)}, u32[]{:S(2)}) copy-start(f32[1,2,768]{2,1,0:T(2,128)S(1)} %bitcast_add_fusion) | copy-start | bytes 18436
  447.4 7.3 %copy-start.69 = (f32[2]{0:T(128)S(1)}, f32[2]{0:T(128)}, u32[]{:S(2)}) copy-start(f32[2]{0:T(128)} %constant.266.clone) | copy-start | bytes 28
  449.2 12.2 %copy-start.65 = (f32[6]{0:T(128)}, f32[6]{0:T(128)S(1)}, u32[]{:S(2)}) copy-start(f32[6]{0:T(128)S(1)} %multiply_add_fusion.6) | copy-start | bytes 76
  450.5 4.1 collective-permute-start.15
  (46 other events, 205.6 us)

commit v3 on v2

--- a/solution.py
+++ b/solution.py
@@ -14,6 +14,9 @@
 PATCHES = 576
 CAP = 10
 VOCAB_DEV = 171
+EXTRA = 640
+VECTOR_AT = 608
+ROUTER_AT = 64
 PAD = 8
 LANES = 128
 
@@ -104,14 +107,90 @@
     )
 
 
+class Staged:
+    def __init__(self, inputs, outputs):
+        self.inputs, self.outputs, self.given = inputs, outputs, []
+
+    def need(self, *indices):
+        for index in indices:
+            self.inputs[index].wait()
+
+    def give(self, *indices):
+        for index in indices:
+            self.outputs[index].start()
+            self.given.append(self.outputs[index])
+
+
+def pin(value):
+    return pltpu.with_memory_space_constraint(value, pltpu.HBM)
+
+
+def staged_call(body, operands, shapes, scratch, far_in, far_out, **params):
+    inputs, outputs = len(operands), len(shapes)
+    raw, raw_out = params.pop("raw", ()), params.pop("raw_out", ())
+
+    def kernel(*refs):
+        refs = list(refs)
+        stages = refs[inputs + outputs + len(scratch) :]
+        stage_in, stages = stages[: len(far_in)], stages[len(far_in) :]
+        stage_out, (sem_in, sem_out) = stages[: len(far_out)], stages[len(far_out) :]
+        fetches, stores = {}, {}
+        for number, index in enumerate(far_in):
+            fetches[index] = pltpu.make_async_copy(refs[index], stage_in[number], sem_in.at[number])
+            fetches[index].start()
+            refs[index] = stage_in[number]
+        for number, index in enumerate(far_out):
+            stores[index] = pltpu.make_async_copy(stage_out[number], refs[inputs + index], sem_out.at[number])
+            refs[inputs + index] = stage_out[number]
+        staged = Staged(fetches, stores)
+        body(staged, *refs[: inputs + outputs + len(scratch)])
+        for copy in staged.given:
+            copy.wait()
+
+    anywhere, near = pl.BlockSpec(memory_space=pl.ANY), pl.BlockSpec(memory_space=pltpu.VMEM)
+    return pl.pallas_call(
+        kernel,
+        out_shape=[
+            pltpu.HBM(*shape) if index in far_out + raw_out else jax.ShapeDtypeStruct(*shape)
+            for index, shape in enumerate(shapes)
+        ],
+        in_specs=[anywhere if index in far_in or index in raw else near for index in range(inputs)],
+        out_specs=[anywhere if index in far_out + raw_out else near for index in range(outputs)],
+        scratch_shapes=list(scratch)
+        + [pltpu.VMEM(operands[index].shape, operands[index].dtype) for index in far_in]
+        + [pltpu.VMEM(*shapes[index]) for index in far_out]
+        + [pltpu.SemaphoreType.DMA((max(1, len(far_in)),)), pltpu.SemaphoreType.DMA((max(1, len(far_out)),))],
+        compiler_params=pltpu.CompilerParams(
+            collective_id=params["collective_id"],
+            has_side_effects=True,
+            vmem_limit_bytes=params["megabytes"] * 2**20,
+        ),
+        name=params["name"],
+    )(*(pin(value) if index in far_in or index in raw else value for index, value in enumerate(operands)))
+
+
 ORDERS = (("x", "y", "z"), ("y", "z", "x"), ("z", "x", "y"))
 
 
-def gather_kernel(x_ref, *refs):
-    squares, extra, spare = refs[:5], refs[5], refs[6]
-    outs, (send, recv, local) = refs[7:10], refs[10:]
+def gather_kernel(own_squares, own_extra, patches, ids, experts, *refs):
+    squares, extra, spare, image, image_ids, experts_low = refs[:5], *refs[5:10]
+    outs, (x_ref, wide, narrow, send, recv, local, local_in, local_out) = refs[10:13], refs[13:]
     at = place()
     sems = (send, recv)
+    value = own_extra[...]
+    high = value.astype(jnp.bfloat16).astype(jnp.float32)
+    lane = lax.broadcasted_iota(jnp.int32, value.shape, 1)
+    rest = jnp.where(lane < PATCHES, value - high, 0.0)
+    high = jnp.where(lane >= VECTOR_AT + 16, value - high, high)
+    blank = jnp.zeros((2, D), jnp.float32)
+    for part, rows in enumerate(
+        (
+            (own_squares[0], rest[0:2], own_squares[1], rest[2:4]),
+            (own_squares[2], rest[4:6], own_squares[3], blank),
+            (own_squares[4], blank, high, blank),
+        )
+    ):
+        x_ref[part] = jnp.concatenate(rows).astype(jnp.bfloat16)
     own = []
     for part in range(3):
         own.append(
@@ -120,6 +199,33 @@
             )
         )
         own[part].start()
+    micro = lax.div(at["y"], 2)
+    kept = [
+        pltpu.make_async_copy(patches.at[micro], image.at[micro], local.at[3]),
+        pltpu.make_async_copy(ids.at[micro], image_ids.at[micro], local.at[4]),
+    ]
+    for copy in kept:
+        copy.start()
+
+    def lines(ref, step):
+        return ref.at[step // 3, pl.ds(step % 3 * 256, 256)]
+
+    def fetch(step):
+        return pltpu.make_async_copy(lines(experts, step), wide.at[step % 2], local_in.at[step % 2])
+
+    def store(step):
+        return pltpu.make_async_copy(narrow.at[step % 2], lines(experts_low, step), local_out.at[step % 2])
+
+    def round_experts(step):
+        if step < 5:
+            fetch(step + 1).start()
+        fetch(step).wait()
+        if step >= 2:
+            store(step - 2).wait()
+        narrow[step % 2] = wide[step % 2].astype(jnp.bfloat16)
+        store(step).start()
+
+    fetch(0).start()
     greet(at)
     flights = {}
 
@@ -141,6 +247,14 @@
 
     for part in range(3):
         launch(part, 0)
+    trades = [
+        remote(patches.at[1 - micro], image.at[micro], sems, 39, moved(at, "y", 2)),
+        remote(ids.at[1 - micro], image_ids.at[micro], sems, 40, moved(at, "y", 2)),
+    ]
+    for copy in trades:
+        copy.start()
+    round_experts(0)
+    round_experts(1)
     for stage in (1, 2):
         for part in range(3):
             if stage == 1:
@@ -150,6 +264,10 @@
             launch(part, stage)
             if stage == 2:
                 forward(part, 0)
+        round_experts(2 * stage)
+        round_experts(2 * stage + 1)
+    store(4).wait()
+    store(5).wait()
     for by in (1, 3, 2):
         for part in range(3):
             flights[part, 2, by].wait_recv()
@@ -194,36 +312,120 @@
         if key[1] == 3:
             copy.wait_recv()
     pack(1 - at["core"])
+    for copy in kept + trades:
+        copy.wait()
     for copy in flights.values():
         copy.wait_send()
 
 
-def gather_all(payload):
+def gather_all(squares, extra, patches, ids, experts):
     shape = (2, 2, 4, 2, 4, 16, D)
     return pl.pallas_call(
         gather_kernel,
-        out_shape=[jax.ShapeDtypeStruct((D, D), payload.dtype)] * 7,
-        in_specs=[pl.BlockSpec(memory_space=pltpu.VMEM)],
-        out_specs=[pl.BlockSpec(memory_space=pltpu.VMEM)] * 7,
-        scratch_shapes=[pltpu.VMEM(shape, payload.dtype)] * 3
+        out_shape=[jax.ShapeDtypeStruct((D, D), jnp.bfloat16)] * 7
+        + [pltpu.HBM(value.shape, value.dtype) for value in (patches, ids)]
+        + [pltpu.HBM(experts.shape, jnp.bfloat16)],
+        in_specs=[pl.BlockSpec(memory_space=pltpu.VMEM)] * 2 + [pl.BlockSpec(memory_space=pl.ANY)] * 3,
+        out_specs=[pl.BlockSpec(memory_space=pltpu.VMEM)] * 7 + [pl.BlockSpec(memory_space=pl.ANY)] * 3,
+        scratch_shapes=[pltpu.VMEM(shape, jnp.bfloat16)] * 3
         + [
-            pltpu.SemaphoreType.DMA((39,)),
-            pltpu.SemaphoreType.DMA((39,)),
-            pltpu.SemaphoreType.DMA((3,)),
+            pltpu.VMEM((3, 16, D), jnp.bfloat16),
+            pltpu.VMEM((2, 256, D), jnp.float32),
+            pltpu.VMEM((2, 256, D), jnp.bfloat16),
+            pltpu.SemaphoreType.DMA((41,)),
+            pltpu.SemaphoreType.DMA((41,)),
+            pltpu.SemaphoreType.DMA((5,)),
+            pltpu.SemaphoreType.DMA((2,)),
+            pltpu.SemaphoreType.DMA((2,)),
         ],
         compiler_params=pltpu.CompilerParams(
-            collective_id=0, has_side_effects=True, vmem_limit_bytes=40 * 2**20
+            collective_id=0, has_side_effects=True, vmem_limit_bytes=24 * 2**20
         ),
         name="gather_weights",
-    )(payload)
-
-
-def scatter_kernel(*refs):
-    grads, outs = refs[:3], refs[3:6]
-    first, total_one, second, total_two, third = (refs[6 + 3 * i : 9 + 3 * i] for i in range(5))
-    sems = refs[21:23]
+    )(squares, extra, pin(patches), pin(ids), pin(experts))
+
+
+def gradients_kernel(
+    staged, patches, hidden_one, mixed, dembed, dquery, dkey, dvalue, dafter, hidden_two, dgate, sums, final_sums,
+    head_grad, expert_squared, loss, square_rows, router_rows, *refs,
+):
+    outs, totals, refs = refs[:3], refs[3], refs[1:]
+    lefts, tables, rights, left_got, table_got, right_got, few_mine, few_got, few_t, partial, grads = refs[3:14]
+    first, total_one, second, total_two, third = (refs[14 + 3 * i : 17 + 3 * i] for i in range(5))
+    core_sems, sems = refs[29:31], refs[31:33]
+    parts, total_sems = refs[33], refs[34:36]
     at = place()
+    other = moved(at, "core", 1)
+    count = patches.shape[0]
+    part_rows = D // 4
+    for index, ref in enumerate((dembed, dquery, dkey, dvalue, dafter)):
+        rights[index] = ref[...]
     greet(at)
+    copies = [remote(rights, right_got, core_sems, 0, other)]
+    copies[0].start()
+    staged.need(0, 1, 2, 8)
+    for index, ref in enumerate((patches, hidden_one, mixed)):
+        lefts[index] = ref[...].T.reshape(4, part_rows, count)
+    padded = jnp.concatenate([dembed[...], jnp.zeros((3 * LANES - count, D), jnp.bfloat16)])
+    tables[...] = padded.T.reshape(4, part_rows, 3 * LANES)
+    for half in range(2):
+        source = lefts.at[:, 2 * half + other["core"]]
+        copies.append(remote(source, left_got.at[:, half], core_sems, 1 + half, other))
+        source = tables.at[2 * half + other["core"]]
+        copies.append(remote(source, table_got.at[half], core_sems, 3 + half, other))
+    few_mine[:32, :] = plain_dot(dgate[...].T, hidden_two[...])[64:96]
+    few_mine[32:40, :] = sums[...]
+    few_mine[40:48, :] = final_sums[...]
+    copies.append(remote(few_mine, few_got, core_sems, 5, other))
+    for copy in copies[1:]:
+        copy.start()
+
+    pairs = ((0, 0), (1, 1), (1, 2), (1, 3), (2, 4))
+
+    def own_product(half, carry):
+        rows = 2 * half + at["core"]
+        for index, (left, right) in enumerate(pairs):
+            partial[index, half] = plain_dot(lefts[left, rows], rights[right])
+        return carry
+
+    lax.fori_loop(0, 2, own_product, 0)
+    for copy in copies:
+        copy.wait_recv()
+    few = few_mine[...] + few_got[...]
+    few_high = few.astype(jnp.bfloat16)
+    few_low = (few - few_high.astype(jnp.float32)).astype(jnp.bfloat16)
+    blank = jnp.zeros((32, D), jnp.bfloat16)
+    few_rows = jnp.concatenate([blank, few_high[:32], few_low[:32], few_high[32:], few_low[32:]])
+    few_t[...] = few_rows.T.reshape(4, part_rows, LANES)
+
+    def spread(offset):
+        shape = (part_rows // 6 * 2 * PAD, part_rows)
+        row, column = iota(shape, 0), iota(shape, 1)
+        inside = lax.rem(row, 2 * PAD) - offset
+        hit = (inside >= 0) & (inside < 6) & (column == lax.div(row, 2 * PAD) * 6 + inside)
+        return hit.astype(jnp.bfloat16)
+
+    spreads = jnp.concatenate([spread(0), spread(PAD)], axis=1)
+
+    def finish(part, half):
+        rows = 2 * half + at["core"]
+        pieces = []
+        for index in (2 * part, 2 * part + 1):
+            if index < 5:
+                left, right = pairs[index]
+                value = partial[index, half] + plain_dot(left_got[left, half], right_got[right])
+                pieces.append(value.astype(jnp.bfloat16))
+            else:
+                mine, theirs = tables[rows], table_got[half]
+                is_first = at["core"] == 0
+                low = jnp.where(is_first, mine, theirs)
+                high = jnp.where(is_first, theirs, mine)
+                high = jnp.concatenate(
+                    [high[:, : 2 * LANES], high[:, 2 * LANES :] + few_t[rows]], axis=1
+                )
+                pieces.append(jnp.concatenate([low, high], axis=1))
+        value = plain_dot(spreads, jnp.concatenate(pieces)).astype(jnp.bfloat16)
+        grads[part, half] = value.reshape(4, 2, 4, 2 * PAD, D)
 
     def names(axis):
         return ("h", "l") if axis == "y" else (axis,)
@@ -245,7 +447,7 @@
             return source.at[tuple(pick(letter, where, axes[1]) for letter in left)]
         return source.at[tuple(pick(letter, where, axes[0]) for letter in names(axes[0]))]
 
-    sources = (grads, total_one, total_two)
+    sources = ([grads.at[part] for part in range(3)], total_one, total_two)
     landings = (first, second, third)
     targets = (total_one, total_two, outs)
     flights = {}
@@ -262,7 +464,11 @@
             flights[part, stage].append(copy)
 
     for part in range(3):
+        for half in range(2):
+            finish(part, half)
         launch(part, 0)
+    head_squared = jnp.sum(head_grad[...] * head_grad[...], axis=0, keepdims=True)
+    expert_norm = jnp.sum(jnp.sum(expert_squared[0:2, :], axis=1, keepdims=True), axis=0, keepdims=True)
     for stage in range(3):
         for part in range(3):
             for copy in flights[part, stage]:
@@ -273,32 +479,96 @@
             targets[stage][part][...] = (terms[0] + terms[1]) + (terms[2] + terms[3])
             if stage < 2:
                 launch(part, stage + 1)
-    for copies in flights.values():
-        for copy in copies:
+
+    tail = outs[2][PAD:, EXTRA:]
+    lane = iota(tail.shape, 1)
+    router = tail + pltpu.roll(tail, LANES - GROUP, 1)
+    vectors = tail + pltpu.roll(tail, LANES - 16, 1)
+    tail = jnp.where(lane < 32, tail, jnp.where(lane < 64, router, jnp.where((lane >= 96) & (lane < 112), vectors, 0.0)))
+    outs[2][PAD:, EXTRA:] = tail
+    squared = [outs[k // 2][PAD * (k % 2) : PAD * (k % 2) + PAD, :] for k in range(6)]
+    squared = [jnp.sum(value * value, axis=0, keepdims=True) for value in squared]
+    spot = iota((1, D), 1)
+    last = jnp.where(spot == 1, expert_norm, 0.0) + jnp.where(spot == 0, loss[...], 0.0)
+    for k in range(5):
+        last = last + jnp.where(spot == 2 + k, jnp.sum(square_rows[k : k + 1, :], axis=1, keepdims=True), 0.0)
+    last = last + jnp.where(spot == 7, jnp.sum(router_rows[...], axis=1, keepdims=True), 0.0)
+    parts[0, 0] = jnp.concatenate(squared[:5] + [head_squared, squared[5], last])
+    parts[0, 1] = expert_squared[...]
+    total = parts.at[0]
+    number = 0
+    for stage, axis in enumerate(("core", "y", "z", "x")):
+        size = 2 if axis == "core" else 4
+        base = 1 + 5 * stage
+        trips = []
+        for by in range(1, size):
+            whole = axis == "core" or (axis == "y" and by == 2)
+            view = total if whole else total.at[0]
+            slot = parts.at[base + at[axis]]
+            trips.append(remote(view, slot if whole else slot.at[0], total_sems, number, moved(at, axis, by)))
+            trips[-1].start()
+            number += 1
+        parts[base + at[axis]] = total[...]
+        for trip in trips:
+            trip.wait()
+        value = parts[base, 0]
+        for index in range(1, size):
+            value = value + parts[base + index, 0]
+        parts[base + 4, 0] = value
+        if axis == "core":
+            parts[base + 4, 1] = parts[base, 1] + parts[base + 1, 1]
+        elif axis == "y":
+            parts[base + 4, 1] = parts[base + at["y"], 1] + parts[base + lax.rem(at["y"] + 2, 4), 1]
+            totals[PAD:, :] = parts[base + 4, 1]
+        else:
+            parts[base + 4, 1] = jnp.zeros((PAD, D), jnp.float32)
+        total = parts.at[base + 4]
+    totals[:PAD, :] = total[0]
+    for copy in copies:
+        copy.wait_send()
+    for launched in flights.values():
+        for copy in launched:
             copy.wait_send()
 
 
-def scatter_all(grads):
+def shared_gradients(*operands):
+    count = operands[0].shape[0]
+    low, wide = jnp.bfloat16, jnp.float32
     block = (2 * PAD, D)
     ones = [{"x": (2, 2, 4), "y": (4, 4), "z": (2, 4, 2)}[axes[2]] for axes in ORDERS]
     twos = [(2, 2) if axes[0] == "y" else (4,) for axes in ORDERS]
-    scratch = [pltpu.VMEM((3,) + one + block, jnp.bfloat16) for one in ones]
-    scratch += [pltpu.VMEM(one + block, jnp.float32) for one in ones]
-    scratch += [pltpu.VMEM((3,) + two + block, jnp.float32) for two in twos]
-    scratch += [pltpu.VMEM(two + block, jnp.float32) for two in twos]
-    scratch += [pltpu.VMEM((3,) + block, jnp.float32)] * 3
-    scratch += [pltpu.SemaphoreType.DMA((27,)), pltpu.SemaphoreType.DMA((27,))]
-    return pl.pallas_call(
-        scatter_kernel,
-        out_shape=[jax.ShapeDtypeStruct(block, jnp.float32)] * 3,
-        in_specs=[pl.BlockSpec(memory_space=pltpu.VMEM)] * 3,
-        out_specs=[pl.BlockSpec(memory_space=pltpu.VMEM)] * 3,
-        scratch_shapes=scratch,
-        compiler_params=pltpu.CompilerParams(
-            collective_id=1, has_side_effects=True, vmem_limit_bytes=40 * 2**20
-        ),
-        name="scatter_grads",
-    )(*grads)
+    rows = D // 4
+    scratch = [
+        pltpu.VMEM((3, 4, rows, count), low),
+        pltpu.VMEM((4, rows, 3 * LANES), low),
+        pltpu.VMEM((5, count, D), low),
+        pltpu.VMEM((3, 2, rows, count), low),
+        pltpu.VMEM((2, rows, 3 * LANES), low),
+        pltpu.VMEM((5, count, D), low),
+        pltpu.VMEM((48, D), wide),
+        pltpu.VMEM((48, D), wide),
+        pltpu.VMEM((4, rows, LANES), low),
+        pltpu.VMEM((5, 2, rows, D), wide),
+        pltpu.VMEM((3, 2, 4, 2, 4) + block, low),
+    ]
+    scratch += [pltpu.VMEM((3,) + one + block, low) for one in ones]
+    scratch += [pltpu.VMEM(one + block, wide) for one in ones]
+    scratch += [pltpu.VMEM((3,) + two + block, wide) for two in twos]
+    scratch += [pltpu.VMEM(two + block, wide) for two in twos]
+    scratch += [pltpu.VMEM((3,) + block, wide)] * 3
+    scratch += [pltpu.SemaphoreType.DMA((6,))] * 2 + [pltpu.SemaphoreType.DMA((27,))] * 2
+    scratch += [pltpu.VMEM((21, 2, PAD, D), wide)] + [pltpu.SemaphoreType.DMA((10,))] * 2
+    return staged_call(
+        gradients_kernel,
+        operands,
+        [(block, wide)] * 4,
+        scratch,
+        (0, 1, 2, 8),
+        (),
+        collective_id=1,
+        megabytes=36,
+        name="shared_gradients",
+    )
 
 
 def meet_core(at):
@@ -334,24 +604,60 @@
 
 
 def attend_kernel(
-    x_ref, w0, w1, w2, w3, w4, vec, table, router, ids,
+    staged, x_ref, w0, w1, w2, w3, w4, extra, spare, ids,
     embed, hidden_one, query, keys, values, mixed, after, hidden_two, gate_probs, gates, lse,
-    send, recv,
+    vec, router, target, target_t, hidden_kept, w1_kept, w2_kept, w3_kept, w4_kept,
+    turned, local, send, recv,
 ):
     at = place()
     sems = (send, recv)
+    saves = [
+        pltpu.make_async_copy(source, target_ref, local.at[index])
+        for index, (source, target_ref) in enumerate(
+            ((w1, w1_kept), (w2, w2_kept), (w3, w3_kept), (w4, w4_kept), (hidden_two, hidden_kept))
+        )
+    ]
+    for copy in saves[:4]:
+        copy.start()
     other = meet_core(at)
     rows = x_ref.shape[0]
+    staged.need(8)
+    turned[...] = (
+        extra[:, :EXTRA].astype(jnp.float32) + spare[:, :EXTRA].astype(jnp.float32)
+    ).T
+    vec[...] = turned[VECTOR_AT : VECTOR_AT + 16, :] + turned[VECTOR_AT + 16 : VECTOR_AT + 32, :]
+    router[...] = extra[:, EXTRA - LANES : EXTRA]
+
+    block = rows // 2
+    earlier = (iota((block, block), 1) < iota((block, block), 0)).astype(jnp.bfloat16)
+    lane = iota((block, LANES), 1)
+    for number in range(2):
+        part = slice(number * block, (number + 1) * block)
+        hits = [(lane == ids[part, k : k + 1]).astype(jnp.float32) for k in range(2)]
+        before = plain_dot(earlier, (hits[0] + hits[1]).astype(jnp.bfloat16))
+        spots = []
+        for k in range(2):
+            named = ids[part, k : k + 1]
+            slot = jnp.sum(hits[k] * before, axis=-1, keepdims=True).astype(jnp.int32) + number * CAP
+            spots.append(
+                jnp.where(slot < SLOTS, named * SLOTS + slot, MAIN + named * TAIL + slot - SLOTS)
+            )
+        target[part, :] = jnp.where(lane == 0, spots[0], jnp.where(lane == 1, spots[1], 0))
+    target_t[...] = target[...].astype(jnp.float32).T[:PAD].astype(jnp.int32)
+
+    staged.need(0)
     embed[...] = plain_dot(x_ref[...], w0[...])
 
-    def first_norm(part, carry):
-        value = embed[part, :] + vec[0:1, :] + table[part, :]
+    def first_norm(index, carry):
+        part = pl.ds(pl.multiple_of(index * CHUNK, CHUNK), CHUNK)
+        line = at["core"] * block + index * CHUNK + jnp.where(index * CHUNK < block, 0, block)
+        value = embed[part, :] + vec[0:1, :] + turned[pl.ds(pl.multiple_of(line, CHUNK), CHUNK), :]
         embed[part, :] = value
         normed, _ = centre(value)
         hidden_one[part, :] = (normed * vec[1:2, :] + vec[2:3, :]).astype(jnp.bfloat16)
         return carry
 
-    chunks(rows, first_norm)
+    lax.fori_loop(0, rows // CHUNK, first_norm, 0)
     keys[0] = plain_dot(hidden_one[...], w2[...]).astype(jnp.bfloat16)
     send_keys = remote(keys.at[0], keys.at[1], sems, 0, other)
     send_keys.start()
@@ -361,6 +667,7 @@
     query[...] = (plain_dot(hidden_one[...], w1[...]) + vec[3:4, :]).astype(jnp.bfloat16)
     send_keys.wait()
     send_values.wait()
+    staged.give(0, 1, 2, 3, 4)
 
     def heads(index, carry):
         lanes = pl.ds(pl.multiple_of(index * LANES, LANES), LANES)
@@ -382,6 +689,7 @@
         return carry
 
     lax.fori_loop(0, D // LANES, heads, 0)
+    staged.give(5)
     after[...] = plain_dot(mixed[...], w4[...])
 
     def second_norm(part, carry):
@@ -391,42 +699,50 @@
         low = (normed * vec[6:7, :] + vec[7:8, :]).astype(jnp.bfloat16)
         hidden_two[part, :] = low
         logits = plain_dot(low, router[...])
-        lane = lax.broadcasted_iota(jnp.int32, logits.shape, 1)
-        logits = jnp.where(lane < 32, logits, -jnp.inf)
+        lane = iota(logits.shape, 1) - ROUTER_AT
+        logits = jnp.where((lane >= 0) & (lane < GROUP), logits, -jnp.inf)
         raw = jnp.exp(logits - jnp.max(logits, axis=-1, keepdims=True))
         probs = raw / jnp.sum(raw, axis=-1, keepdims=True)
         gate_probs[part, :] = probs
         first, second = (
             jnp.sum(jnp.where(lane == ids[part, k : k + 1], probs, 0.0), axis=-1, keepdims=True) for k in range(2)
         )
-        gates[part, :] = jnp.where(lane == 0, first, second)
+        gates[part, :] = jnp.where(lane == -ROUTER_AT, first, second)
         return carry
 
     chunks(rows, second_norm)
-
-
-def attend(patch_rows, squares, vectors, table_rows, router, ids):
+    staged.give(6)
+    saves[4].start()
+    for copy in saves:
+        copy.wait()
+
+
+def attend(patch_rows, squares, extra, spare, ids):
     rows = patch_rows.shape[0]
     low, wide = jnp.bfloat16, jnp.float32
     shapes = [
         ((rows, D), wide), ((rows, D), low), ((rows, D), low), ((2, rows, D), low), ((2, rows, D), low),
         ((rows, D), low), ((rows, D), wide), ((rows, D), low), ((rows, LANES), wide), ((rows, LANES), wide), ((16, rows), wide),
+        ((16, D), wide), ((D, LANES), low), ((rows, LANES), jnp.int32), ((PAD, rows), jnp.int32),
+        ((rows, D), low), ((D, D), low), ((D, D), low), ((D, D), low), ((D, D), low),
     ]
-    return pl.pallas_call(
+    sems = pltpu.SemaphoreType.DMA
+    return staged_call(
         attend_kernel,
-        out_shape=[jax.ShapeDtypeStruct(*shape) for shape in shapes],
-        in_specs=[pl.BlockSpec(memory_space=pltpu.VMEM)] * 10,
-        out_specs=[pl.BlockSpec(memory_space=pltpu.VMEM)] * 11,
-        scratch_shapes=[pltpu.SemaphoreType.DMA((2,)), pltpu.SemaphoreType.DMA((2,))],
-        compiler_params=pltpu.CompilerParams(
-            collective_id=6, has_side_effects=True, vmem_limit_bytes=48 * 2**20
-        ),
+        (patch_rows, *squares, extra, spare, ids),
+        shapes,
+        [pltpu.VMEM((EXTRA, D), wide), sems((5,)), sems((2,)), sems((2,))],
+        (0, 8),
+        tuple(range(7)),
+        raw_out=(15, 16, 17, 18, 19),
+        collective_id=6,
+        megabytes=20,
         name="attend",
-    )(patch_rows, *squares, vectors, table_rows, router, ids)
+    )
 
 
 def attend_back_kernel(
-    dafter_in, dhidden, dgate, embed, after, hidden_one, query, keys, values, lse, w1, w2, w3, w4, vec, router,
+    staged, dafter_in, dhidden, dgate, embed, after, query, keys, values, lse, w1, w2, w3, w4, vec, router,
     dafter_low, dquery, dkey, dvalue, dembed_low, sums,
     dafter, dmixed, dkey_own, dvalue_own, dkey_other, dvalue_other, dkey_got, dvalue_got, wide, send, recv,
 ):
@@ -437,6 +753,7 @@
     pairs = D // LANES
     zero = jnp.zeros((1, D), jnp.float32)
     wide[...] = over_last(dgate[...], router[...])
+    staged.need(4)
 
     def second_norm(index, carry):
         part = pl.ds(pl.multiple_of(index * CHUNK, CHUNK), CHUNK)
@@ -451,7 +768,9 @@
     sums[5:6, :] = bias
     sums[6:7, :] = gain
     sums[7:8, :] = shift
+    staged.need(12)
     dmixed[...] = over_last(dafter_low[...], w4[...]).astype(jnp.bfloat16)
+    staged.need(5, 6, 7)
 
     def flights(index):
         return (
@@ -503,6 +822,7 @@
         return carry
 
     lax.fori_loop(0, pairs, gather, 0)
+    staged.need(3, 9, 10, 11)
     wide[...] = (
         over_last(dquery[...], w1[...]) + over_last(dkey[...], w2[...]) + over_last(dvalue[...], w3[...])
     )
@@ -528,20 +848,20 @@
     rows = operands[0].shape[0]
     low, wide = jnp.bfloat16, jnp.float32
     pairs = D // LANES
-    return pl.pallas_call(
+    sems = pltpu.SemaphoreType.DMA
+    return staged_call(
         attend_back_kernel,
-        out_shape=[jax.ShapeDtypeStruct((rows, D), low)] * 5 + [jax.ShapeDtypeStruct((8, D), wide)],
-        in_specs=[pl.BlockSpec(memory_space=pltpu.VMEM)] * 16,
-        out_specs=[pl.BlockSpec(memory_space=pltpu.VMEM)] * 6,
-        scratch_shapes=[pltpu.VMEM((rows, D), wide), pltpu.VMEM((rows, D), low)]
+        operands,
+        [((rows, D), low)] * 5 + [((8, D), wide)],
+        [pltpu.VMEM((rows, D), wide), pltpu.VMEM((rows, D), low)]
         + [pltpu.VMEM((pairs, rows, LANES), wide)] * 6
-        + [pltpu.VMEM((rows, D), wide)]
-        + [pltpu.SemaphoreType.DMA((2 * pairs,)), pltpu.SemaphoreType.DMA((2 * pairs,))],
-        compiler_params=pltpu.CompilerParams(
-            collective_id=7, has_side_effects=True, vmem_limit_bytes=48 * 2**20
-        ),
+        + [pltpu.VMEM((rows, D), wide), sems((2 * pairs,)), sems((2 * pairs,))],
+        (4, 12, 5, 6, 7, 3, 9, 10, 11),
+        (),
+        collective_id=7,
+        megabytes=22,
         name="attend_back",
-    )(*operands)
+    )
 
 
 SLOTS = 16
@@ -600,13 +920,14 @@
         return carry
 
     lax.fori_loop(1, GROUP, greet_one, 0)
-    other = moved(at, "core", 1)
-    pl.semaphore_signal(barrier, inc=1, device_id=device(other), device_id_type=MESH)
-    return other
+    peers = moved(at, "core", 1), moved(at, "y", 2)
+    for peer in peers:
+        pl.semaphore_signal(barrier, inc=1, device_id=device(peer), device_id_type=MESH)
+    return peers
 
 
 def met_experts():
-    pl.semaphore_wait(pltpu.get_barrier_semaphore(), GROUP)
+    pl.semaphore_wait(pltpu.get_barrier_semaphore(), GROUP + 1)
 
 
 def deal(source, target, sems, forth, low, high, act):
@@ -642,8 +963,10 @@
 
 def load_experts(own, across, weights, sems, local, other):
     near = [pltpu.make_async_copy(own, weights.at[0], local.at[0])]
-    near.append(pltpu.make_async_copy(across, weights.at[1], local.at[1]))
-    far = [remote(own, weights.at[2], sems, 0, other), remote(across, weights.at[3], sems, 1, other)]
+    far = [remote(own, weights.at[2], sems, 0, other)]
+    for which, ref in enumerate(across):
+        near.append(pltpu.make_async_copy(ref, weights.at[1, which], local.at[1 + which]))
+        far.append(remote(ref, weights.at[3, which], sems, 1 + which, other))
     return near, far
 
 
@@ -669,15 +992,19 @@
 
 
 def experts_kernel(
-    hidden, target_row, target_column, gates, after, vec, own, across,
-    rows, chosen, total, pool,
+    staged, hidden, target_row, target_column, gates, after, vec, own, across_in,
+    rows, rows_y, chosen, total, pool, across_out,
     weights, sends, lands, backs, returns, act, result, gathered,
-    forth_send, forth_recv, back_send, back_recv, weight_send, weight_recv, local,
+    forth_send, forth_recv, back_send, back_recv, weight_send, weight_recv, row_send, row_recv, local,
 ):
     at = place()
     me = lax.axis_index("exp")
-    other = meet_experts(at)
-    near, far = load_experts(own, across, weights, (weight_send, weight_recv), local, other)
+    other, across_y_peer = meet_experts(at)
+    row_copies = []
+    near, far = load_experts(own, (across_in,), weights, (weight_send, weight_recv), local, other)
+    trade = remote(own.at[1], weights.at[1, 1], (weight_send, weight_recv), 2, across_y_peer)
+    pass_on = remote(weights.at[1, 1], weights.at[3, 1], (weight_send, weight_recv), 3, other)
+    save = pltpu.make_async_copy(weights.at[1, 1], across_out, local.at[3])
     for copy in near:
         copy.start()
     count = hidden.shape[0]
@@ -687,7 +1014,7 @@
     pack(sends, placed[:MAIN], placed[MAIN:])
     met_experts()
     deal(sends, lands, (forth_send, forth_recv), True, 1, GROUP, start_copy)
-    for copy in far:
+    for copy in [*far, trade]:
         copy.start()
     keep = pltpu.make_async_copy(sends.at[me], lands.at[0], local.at[2])
     keep.start()
@@ -701,6 +1028,11 @@
         sources = pl.ds(half * (GROUP // 2), GROUP // 2)
         first, first_tail = half * (MAIN // 2), MAIN + half * (TOTAL - MAIN) // 2
         unpack(lands.at[sources], rows, first, first_tail)
+        for piece, (start, size) in enumerate(((first, MAIN // 2), (first_tail, (TOTAL - MAIN) // 2))):
+            view = pl.ds(start, size)
+            copy = remote(rows.at[view], rows_y.at[view], (row_send, row_recv), half * 2 + piece, across_y_peer)
+            copy.start()
+            row_copies.append(copy)
         if half == 0:
             for copy in far:
                 copy.wait_recv()
@@ -714,6 +1046,11 @@
             return carry
 
         lax.fori_loop(0, 12, hidden_units, 0)
+        if half == 0:
+            trade.wait_recv()
+            pass_on.start()
+            save.start()
+            pass_on.wait_recv()
 
         def outputs(index, carry):
             columns = pl.ds(pl.multiple_of(index * 256, 256), 256)
@@ -735,6 +1072,8 @@
     for k in range(2):
         placing = (slot == target_column[:, k : k + 1]).astype(jnp.bfloat16)
         chosen[k] = plain_dot(placing, gathered[...]).astype(jnp.bfloat16)
+    staged.give(0, 2)
+    staged.need(4)
 
     def final_norm(index, carry):
         part = pl.ds(pl.multiple_of(index * CHUNK, CHUNK), CHUNK)
@@ -747,54 +1086,62 @@
         return carry + jnp.sum(normed * vec[8:9, :] + vec[9:10, :], axis=0, keepdims=True)
 
     summed = lax.fori_loop(0, count // CHUNK, final_norm, jnp.zeros((1, D), jnp.float32)) / PATCHES
+    staged.give(3)
     pool[...] = jnp.zeros_like(pool)
     for tile in range(D // LANES):
         pool[tile : tile + 1, :] = summed[:, tile * LANES : (tile + 1) * LANES]
     deal(sends, lands, (forth_send, forth_recv), True, 1, GROUP, wait_send)
     deal(backs, returns, (back_send, back_recv), False, 1, GROUP, wait_send)
-    for copy in far:
+    for copy in [*far, trade, pass_on]:
         copy.wait_send()
+    save.wait()
+    for copy in row_copies:
+        copy.wait()
+    staged.give(1)
 
 
 def experts_forward(*operands):
     count = operands[0].shape[0]
     low, wide = jnp.bfloat16, jnp.float32
     wire = pltpu.VMEM((GROUP, SLOTS, WIRE), low)
-    shapes = [((TOTAL, D), low), ((2, count, D), low), ((count, D), wide), ((PAD, LANES), wide)]
-    sems = pltpu.SemaphoreType.DMA((GROUP,))
-    return pl.pallas_call(
+    sems = pltpu.SemaphoreType.DMA
+    return staged_call(
         experts_kernel,
-        out_shape=[jax.ShapeDtypeStruct(*shape) for shape in shapes],
-        in_specs=[pl.BlockSpec(memory_space=pltpu.VMEM)] * 6 + [pl.BlockSpec(memory_space=pl.ANY)] * 2,
-        out_specs=[pl.BlockSpec(memory_space=pltpu.VMEM)] * 4,
-        scratch_shapes=[pltpu.VMEM((4, 2, D, D), low)]
+        operands,
+        [((TOTAL, D), low), ((TOTAL, D), low), ((2, count, D), low), ((count, D), wide), ((PAD, LANES), wide), ((D, D), low)],
+        [pltpu.VMEM((4, 2, D, D), low)]
         + [wire] * 4
         + [pltpu.VMEM((4, HALF, D), low), pltpu.VMEM((HALF, D), wide), pltpu.VMEM((TOTAL, D), low)]
-        + [sems] * 4
-        + [pltpu.SemaphoreType.DMA((2,))] * 2
-        + [pltpu.SemaphoreType.DMA((3,))],
-        compiler_params=pltpu.CompilerParams(
-            collective_id=5, has_side_effects=True, vmem_limit_bytes=48 * 2**20
-        ),
+        + [sems((GROUP,))] * 4
+        + [sems((4,))] * 4
+        + [sems((4,))],
+        (4,),
+        (0, 1, 2, 3),
+        raw=(6, 7),
+        raw_out=(5,),
+        collective_id=5,
+        megabytes=25,
         name="experts_forward",
-    )(*operands)
+    )
 
 
 def experts_back_kernel(
-    row_grad, total, chosen, gates, gate_probs, ids, rows, target_row, target_column, vec, own, across,
-    dtotal, dgate, sums, dhidden, to_y, kept,
-    weights, sends, lands, backs, returns, act, slope, dpre, drows, result, dreturned, rows_t, drows_t, outward,
-    forth_send, forth_recv, back_send, back_recv, weight_send, weight_recv, grad_send, grad_recv, local, ready,
+    staged, row_grad, total, chosen, gates, gate_probs, ids, rows, rows_y, target_row, target_column, vec, own, across_in, across_out,
+    dtotal, dgate, sums, dhidden, kept, squared,
+    weights, sends, lands, backs, returns, slope, dpre, act_own, act_set, dpre_set, rows_far, drows, result, dreturned,
+    rows_t, drows_t, outward,
+    forth_send, forth_recv, back_send, back_recv, weight_send, weight_recv, set_send, set_recv, local,
 ):
     at = place()
     me = lax.axis_index("exp")
-    other = meet_experts(at)
-    near, far = load_experts(own, across, weights, (weight_send, weight_recv), local, other)
+    other, across_y_peer = meet_experts(at)
+    near, far = load_experts(own, (across_in, across_out), weights, (weight_send, weight_recv), local, other)
     for copy in near:
         copy.start()
     count = total.shape[0]
     grad = jnp.concatenate([row_grad[tile : tile + 1, :] for tile in range(D // LANES)], axis=1) / PATCHES
     zero = jnp.zeros((1, D), jnp.float32)
+    staged.need(1, 2, 5)
 
     def final_norm(index, carry):
         part = pl.ds(pl.multiple_of(index * CHUNK, CHUNK), CHUNK)
@@ -805,7 +1152,7 @@
         ]
         for k in range(2):
             outward[k, part, :] = (gates[part, k : k + 1] * back).astype(jnp.bfloat16)
-        lane = iota((CHUNK, LANES), 1)
+        lane = iota((CHUNK, LANES), 1) - ROUTER_AT
         probs = gate_probs[part, :]
         dprobs = jnp.where(lane == ids[part, 0:1], dgates[0], 0.0) + jnp.where(
             lane == ids[part, 1:2], dgates[1], 0.0
@@ -815,8 +1162,7 @@
         return carry[0] + gain, carry[1] + shift
 
     gain, shift = lax.fori_loop(0, count // CHUNK, final_norm, (zero, zero))
-    sums[0:1, :] = gain
-    sums[1:2, :] = shift
+    sums[...] = jnp.concatenate([gain, shift, jnp.zeros((PAD - 2, D), jnp.float32)])
     slot = iota((TOTAL, count), 0)
     placed = [
         plain_dot((slot == target_row[k : k + 1, :]).astype(jnp.bfloat16), outward[k]) for k in range(2)
@@ -825,25 +1171,39 @@
     pack(sends, placed[:MAIN], placed[MAIN:])
     met_experts()
     deal(sends, lands, (forth_send, forth_recv), True, 1, GROUP, start_copy)
-    for copy in far:
+    staged.need(6, 7)
+    set_sems = (set_send, set_recv)
+    moves = [remote(rows, rows_far.at[0], set_sems, 0, other), remote(rows_y, rows_far.at[1], set_sems, 1, other)]
+    for copy in far + moves:
         copy.start()
-    keep = pltpu.make_async_copy(sends.at[me], lands.at[0], local.at[2])
+    keep = pltpu.make_async_copy(sends.at[me], lands.at[0], local.at[3])
     keep.start()
     keep.wait()
     for copy in near:
         copy.wait()
 
-    def hidden_units(index, carry):
-        quarter, rest = lax.div(index, 6), lax.rem(index, 6)
-        half, part = lax.div(rest, 3), lax.rem(rest, 3)
+    def tile_of(index):
+        half, part = lax.div(index, 3), lax.rem(index, 3)
         columns = pl.ds(pl.multiple_of(part * 256, 256), 256)
-        lines = pl.ds(pl.multiple_of(half * HALF, HALF), HALF)
-        value = plain_dot(rows[lines, :], weights[quarter, 0, :, columns])
+        return pl.ds(pl.multiple_of(half * HALF, HALF), HALF), columns
+
+    def gelu_both(value):
         tanh = gelu_tanh(value)
-        act[quarter, lines, columns] = (0.5 * value * (1.0 + tanh)).astype(jnp.bfloat16)
-        slope[quarter, lines, columns] = 0.5 * (1.0 + tanh) + 0.5 * value * (1.0 - tanh * tanh) * (
+        grown = (0.5 * value * (1.0 + tanh)).astype(jnp.bfloat16)
+        return grown, 0.5 * (1.0 + tanh) + 0.5 * value * (1.0 - tanh * tanh) * (
             GELU_SCALE * (1.0 + 3 * 0.044715 * (value * value))
         )
+
+    def hidden_units(index, carry):
+        quarter = lax.div(index, 6)
+        lines, columns = tile_of(lax.rem(index, 6))
+        grown, rate = gelu_both(plain_dot(rows[lines, :], weights[quarter, 0, :, columns]))
+
+        @pl.when(quarter == 0)
+        def _():
+            act_own[lines, columns] = grown
+
+        slope[quarter, lines, columns] = rate
         return carry
 
     lax.fori_loop(0, 12, hidden_units, 0)
@@ -852,23 +1212,23 @@
     lax.fori_loop(12, 24, hidden_units, 0)
     rows_t[...] = rows[...].T
     deal(sends, lands, (forth_send, forth_recv), True, 1, GROUP, wait_recv)
-    unpack(lands, drows, 0, MAIN)
+    unpack(lands, drows.at[0], 0, MAIN)
+    moves.append(remote(drows.at[0], drows.at[1], set_sems, 2, across_y_peer))
+    moves.append(remote(drows.at[0], drows.at[2], set_sems, 3, other))
+    for copy in moves[2:]:
+        copy.start()
 
     def hidden_back(index, carry):
-        quarter, rest = lax.div(index, 6), lax.rem(index, 6)
-        half, part = lax.div(rest, 3), lax.rem(rest, 3)
-        columns = pl.ds(pl.multiple_of(part * 256, 256), 256)
-        lines = pl.ds(pl.multiple_of(half * HALF, HALF), HALF)
-        value = plain_dot(drows[lines, :], weights[quarter, 1, :, columns])
+        quarter = lax.div(index, 6)
+        lines, columns = tile_of(lax.rem(index, 6))
+        value = plain_dot(drows[0, lines, :], weights[quarter, 1, :, columns])
         dpre[quarter, lines, columns] = (value * slope[quarter, lines, columns]).astype(jnp.bfloat16)
         return carry
 
     lax.fori_loop(0, 24, hidden_back, 0)
 
     def inputs_back(index, carry):
-        half, part = lax.div(index, 3), lax.rem(index, 3)
-        columns = pl.ds(pl.multiple_of(part * 256, 256), 256)
-        lines = pl.ds(pl.multiple_of(half * HALF, HALF), HALF)
+        lines, columns = tile_of(index)
         value = over_last(dpre[0, lines, :], weights[0, 0, columns, :])
         for quarter in range(1, 4):
             value = value + over_last(dpre[quarter, lines, :], weights[quarter, 0, columns, :])
@@ -876,64 +1236,69 @@
         return carry
 
     lax.fori_loop(0, 6, inputs_back, 0)
-    pl.semaphore_signal(ready, inc=1, device_id=device(other), device_id_type=MESH)
     pack(backs, result[:MAIN, :], result[MAIN:, :])
     deal(backs, returns, (back_send, back_recv), False, 1, GROUP, start_copy)
-    keep = pltpu.make_async_copy(backs.at[0], returns.at[me], local.at[2])
+    keep = pltpu.make_async_copy(backs.at[0], returns.at[me], local.at[3])
     keep.start()
-    drows_t[...] = drows[...].T
-
-    def gradient(quarter, which, columns):
-        if which == 0:
-            return plain_dot(rows_t[...], dpre[quarter, :, columns])
-        return plain_dot(drows_t[...], act[quarter, :, columns])
-
-    def far_grads(index, carry):
-        quarter, part = lax.div(index, 3) + 2, lax.rem(index, 3)
-        columns = pl.ds(pl.multiple_of(part * 256, 256), 256)
-        for which in range(2):
-            weights[quarter, which, :, columns] = gradient(quarter, which, columns).astype(jnp.bfloat16)
-        return carry
-
-    for copy in far:
-        copy.wait_send()
-    lax.fori_loop(0, 6, far_grads, 0)
-    pl.semaphore_wait(ready, 1)
-    swaps = [remote(weights.at[2 + k], weights.at[k], (grad_send, grad_recv), k, other) for k in range(2)]
-    for swap in swaps:
-        swap.start()
-
-    def kept_grads(index, carry):
-        columns = pl.ds(pl.multiple_of(index * 256, 256), 256)
-        for which in range(2):
-            kept[which, :, columns] = gradient(0, which, columns)
-        return carry
-
-    lax.fori_loop(0, 3, kept_grads, 0)
+
+    def add_grads(given, down, act, first):
+        drows_t[...] = drows[down].T
+        if not first:
+            rows_t[...] = given.T
+
+        def step(index, carry):
+            columns = pl.ds(pl.multiple_of(index * 256, 256), 256)
+            inner = plain_dot(rows_t[...], (dpre.at[0] if first else dpre_set)[:, columns])
+            outer = plain_dot(drows_t[...], act[:, columns])
+            if first:
+                kept[0, :, columns] = inner
+                kept[1, :, columns] = outer
+            else:
+                kept[0, :, columns] = kept[0, :, columns] + inner
+                kept[1, :, columns] = kept[1, :, columns] + outer
+            return carry
+
+        lax.fori_loop(0, 3, step, 0)
+
+    def add_set(given, down):
+        def step(index, carry):
+            lines, columns = tile_of(index)
+            grown, rate = gelu_both(plain_dot(given[lines, :], weights[0, 0, :, columns]))
+            act_set[lines, columns] = grown
+            value = plain_dot(drows[down, lines, :], weights[0, 1, :, columns])
+            dpre_set[lines, columns] = (value * rate).astype(jnp.bfloat16)
+            return carry
+
+        lax.fori_loop(0, 6, step, 0)
+        add_grads(given[...], down, act_set, False)
+
+    add_grads(None, 0, act_own, True)
+    for copy in (moves[0], moves[1], moves[3]):
+        copy.wait_recv()
+    add_set(rows_far.at[0], 2)
+    moves[2].wait_recv()
+    moves.append(remote(drows.at[1], drows.at[3], set_sems, 4, other))
+    moves[4].start()
     keep.wait()
     deal(backs, returns, (back_send, back_recv), False, 1, GROUP, wait_recv)
     unpack(returns, dreturned, 0, MAIN)
     slot = iota((count, TOTAL), 1)
     placing = (slot == target_column[:, 0:1]) | (slot == target_column[:, 1:2])
     dhidden[...] = plain_dot(placing.astype(jnp.bfloat16), dreturned[...])
-    for swap in swaps:
-        swap.wait_recv()
-
-    def sent_grads(index, carry):
-        columns = pl.ds(pl.multiple_of(index * 256, 256), 256)
-        for which in range(2):
-            value = gradient(1, which, columns) + weights[1, which, :, columns].astype(jnp.float32)
-            to_y[which, :, columns] = value.astype(jnp.bfloat16)
-            kept[which, :, columns] = kept[which, :, columns] + weights[0, which, :, columns].astype(
-                jnp.float32
-            )
-        return carry
-
-    lax.fori_loop(0, 3, sent_grads, 0)
+    add_set(rows_y, 1)
+    moves[4].wait_recv()
+    add_set(rows_far.at[1], 3)
+    staged.give(4)
+    squared[...] = jnp.zeros_like(squared)
+    for which in range(2):
+        square = kept[which] * kept[which]
+        lines = jnp.broadcast_to(jnp.sum(square, axis=1, keepdims=True), (D, LANES)).T
+        squared[which : which + 1, :] = lines[0:1]
+        squared[2 + which : 3 + which, :] = jnp.sum(square, axis=0, keepdims=True)
     deal(sends, lands, (forth_send, forth_recv), True, 1, GROUP, wait_send)
     deal(backs, returns, (back_send, back_recv), False, 1, GROUP, wait_send)
-    for swap in swaps:
-        swap.wait_send()
+    for copy in far + moves:
+        copy.wait_send()
 
 
 def experts_backward(*operands):
@@ -942,28 +1307,32 @@
     wire = pltpu.VMEM((GROUP, SLOTS, WIRE), low)
     shapes = [
         ((count, D), wide), ((count, LANES), low), ((PAD, D), wide),
-        ((count, D), wide), ((2, D, D), low), ((2, D, D), wide),
+        ((count, D), wide), ((2, D, D), wide), ((PAD, D), wide),
     ]
-    sems = pltpu.SemaphoreType.DMA((GROUP,))
-    return pl.pallas_call(
+    sems = pltpu.SemaphoreType.DMA
+    return staged_call(
         experts_back_kernel,
-        out_shape=[jax.ShapeDtypeStruct(*shape) for shape in shapes],
-        in_specs=[pl.BlockSpec(memory_space=pltpu.VMEM)] * 10 + [pl.BlockSpec(memory_space=pl.ANY)] * 2,
-        out_specs=[pl.BlockSpec(memory_space=pltpu.VMEM)] * 6,
-        scratch_shapes=[pltpu.VMEM((4, 2, D, D), low)]
+        operands,
+        shapes,
+        [pltpu.VMEM((4, 2, D, D), low)]
         + [wire] * 4
-        + [pltpu.VMEM((4, TOTAL, D), low), pltpu.VMEM((4, TOTAL, D), wide), pltpu.VMEM((4, TOTAL, D), low)]
-        + [pltpu.VMEM((TOTAL, D), low), pltpu.VMEM((TOTAL, D), wide), pltpu.VMEM((TOTAL, D), low)]
+        + [pltpu.VMEM((4, TOTAL, D), wide), pltpu.VMEM((4, TOTAL, D), low)]
+        + [pltpu.VMEM((TOTAL, D), low)] * 3
+        + [pltpu.VMEM((2, TOTAL, D), low), pltpu.VMEM((4, TOTAL, D), low)]
+        + [pltpu.VMEM((TOTAL, D), wide), pltpu.VMEM((TOTAL, D), low)]
         + [pltpu.VMEM((D, TOTAL), low)] * 2
         + [pltpu.VMEM((2, count, D), low)]
-        + [sems] * 4
-        + [pltpu.SemaphoreType.DMA((2,))] * 4
-        + [pltpu.SemaphoreType.DMA((3,)), pltpu.SemaphoreType.REGULAR],
-        compiler_params=pltpu.CompilerParams(
-            collective_id=8, has_side_effects=True, vmem_limit_bytes=58 * 2**20
-        ),
+        + [sems((GROUP,))] * 4
+        + [sems((3,))] * 2
+        + [sems((5,))] * 2
+        + [sems((4,))],
+        (1, 2, 5, 6, 7),
+        (4,),
+        raw=(11, 12, 13),
+        collective_id=8,
+        megabytes=53,
         name="experts_backward",
-    )(*operands)
+    )
 
 
 NEAR = tuple((y, core) for y in range(4) for core in range(2) if y or core)
@@ -995,51 +1364,64 @@
     return copies
 
 
-def send_plane(at, source, target, sems, first):
-    copies = []
-    for index, by in enumerate(PLANE):
-        peer = plane_peer(at, by)
-        copies.append(remote(source(peer), target.at[at["x"], at["z"]], sems, first + index, peer))
-        copies[-1].start()
-    return copies
-
-
 def head_kernel(
-    pool, head, targets, valid, count,
+    staged, pool, head, labels, count,
     row_grad, head_grad, loss,
-    near, every, pooled, pulls, got, summed, last, send, recv,
+    near, every, pooled, pulls, got, summed, last, low, send, recv,
 ):
     at = place()
     sems = (send, recv)
     greet_all(at)
     copies = send_near(at, lambda peer: pool, near, sems, 0)
     near[at["y"], at["core"]] = pool[...]
+    classes = head.shape[0]
+    staged.need(1)
+    spare = classes - classes % 16
+    low[spare:, :] = jnp.zeros((low.shape[0] - spare, D), jnp.bfloat16)
+    low[:classes, :] = head[...].astype(jnp.bfloat16)
+    images = pooled.shape[0]
+    number = (lax.axis_index("rep") * GROUP + lax.axis_index("exp")) * classes
+    column = iota((images, low.shape[0]), 1)
+    inside = column < classes
+    column = jnp.where(inside, column + number, -2)
+    hit = labels[:, 0:1] == column
+    for slot in range(1, labels.shape[1]):
+        hit = hit | (labels[:, slot : slot + 1] == column)
+    targets = hit.astype(jnp.float32)
+    valid = (jnp.max(labels[...], axis=1, keepdims=True) >= 0).astype(jnp.float32)
     for copy in copies:
         copy.wait()
     rows = near[:, 0] + near[:, 1]
-    every[at["x"], at["z"]] = rows.astype(jnp.bfloat16).astype(jnp.float32)
-    mine = every.at[at["x"], at["z"]]
-    for copy in send_plane(at, lambda peer: mine, every, sems, 7):
+    mine = every.at[:, at["x"], :, at["z"]]
+    mine[...] = rows.astype(jnp.bfloat16).astype(jnp.float32).reshape(2, 2, PAD, LANES)
+    copies = []
+    for index, by in enumerate(PLANE):
+        copies.append(remote(mine, mine, sems, 7 + index, plane_peer(at, by)))
+        copies[-1].start()
+    for copy in copies:
         copy.wait()
-    images = pooled.shape[0]
     for tile in range(D // LANES):
         lanes = slice(tile * LANES, (tile + 1) * LANES)
-        pooled[:, lanes] = every[:, :, :, tile, :].reshape(images, LANES).astype(jnp.bfloat16)
-    logits = plain_dot(pooled[...], head[...])
+        pooled[:, lanes] = every[:, :, :, :, tile, :].reshape(images, LANES).astype(jnp.bfloat16)
+    logits = over_last(pooled[...], low[...])
     soft = jnp.maximum(logits, 0.0) + jnp.log1p(jnp.exp(-jnp.abs(logits)))
-    inside = iota(logits.shape, 1) < VOCAB_DEV
-    terms = jnp.where(inside, valid[...] * (soft - targets[...] * logits), 0.0)
+    terms = jnp.where(inside, valid * (soft - targets * logits), 0.0)
     loss[...] = jnp.sum(jnp.sum(terms, axis=1, keepdims=True), axis=0, keepdims=True)
     sigmoid = 1.0 / (1.0 + jnp.exp(-logits))
-    down = jnp.where(inside, valid[...] * (sigmoid - targets[...]) / count[...], 0.0).astype(jnp.bfloat16)
-    back = over_last(down, head[...])
+    down = jnp.where(inside, valid * (sigmoid - targets) / count[...], 0.0)
+    back = plain_dot(down.astype(jnp.bfloat16), low[...])
     pulls[...] = jnp.zeros_like(pulls)
     for tile in range(D // LANES):
         lanes = slice(tile * LANES, (tile + 1) * LANES)
-        pulls[:, :, :, tile, :] = back[:, lanes].reshape(4, 4, 4, LANES)
-    copies = send_plane(at, lambda peer: pulls.at[peer["x"], peer["z"]], got, sems, 22)
-    got[at["x"], at["z"]] = pulls[at["x"], at["z"]]
-    head_grad[...] = plain_dot(pooled[...].T, down)
+        pulls[:, :, :, :, tile, :] = back[:, lanes].reshape(2, 4, 2, 4, LANES)
+    copies = []
+    for index, by in enumerate(PLANE):
+        peer = plane_peer(at, by)
+        source = pulls.at[:, peer["x"], :, peer["z"]]
+        copies.append(remote(source, got.at[at["x"], at["z"]], sems, 22 + index, peer))
+        copies[-1].start()
+    got[at["x"], at["z"]] = pulls[:, at["x"], :, at["z"]]
+    head_grad[...] = plain_dot(down.T.astype(jnp.bfloat16), pooled[...])
     for copy in copies:
         copy.wait()
     summed[...] = jnp.sum(got[...].reshape((16,) + summed.shape), axis=0)
@@ -1050,67 +1432,34 @@
     row_grad[...] = jnp.sum(last[...].reshape((8,) + row_grad.shape), axis=0)
 
 
-def head_step(pool, head, targets, valid, count):
-    images, classes = targets.shape
+def head_step(pool, head, labels, count):
+    images = labels.shape[0]
+    classes = -(-head.shape[0] // LANES) * LANES
     wide = jnp.float32
     block = (PAD, LANES)
-    return pl.pallas_call(
+    sems = pltpu.SemaphoreType.DMA
+    return staged_call(
         head_kernel,
-        out_shape=[
-            jax.ShapeDtypeStruct(block, wide),
-            jax.ShapeDtypeStruct((D, classes), wide),
-            jax.ShapeDtypeStruct((1, 1), wide),
-        ],
-        in_specs=[pl.BlockSpec(memory_space=pltpu.VMEM)] * 5,
-        out_specs=[pl.BlockSpec(memory_space=pltpu.VMEM)] * 3,
-        scratch_shapes=[
+        (pool, head, labels, count),
+        [(block, wide), ((classes, D), wide), ((1, 1), wide)],
+        [
             pltpu.VMEM((4, 2) + block, wide),
-            pltpu.VMEM((4, 4, 4) + block, wide),
+            pltpu.VMEM((2, 4, 2, 4) + block, wide),
             pltpu.VMEM((images, D), jnp.bfloat16),
-            pltpu.VMEM((4, 4, 4) + block, wide),
-            pltpu.VMEM((4, 4, 4) + block, wide),
+            pltpu.VMEM((2, 4, 2, 4) + block, wide),
+            pltpu.VMEM((4, 4, 2, 2) + block, wide),
             pltpu.VMEM((4,) + block, wide),
             pltpu.VMEM((4, 2) + block, wide),
-            pltpu.SemaphoreType.DMA((44,)),
-            pltpu.SemaphoreType.DMA((44,)),
+            pltpu.VMEM((classes, D), jnp.bfloat16),
+            sems((44,)),
+            sems((44,)),
         ],
-        compiler_params=pltpu.CompilerParams(collective_id=2, has_side_effects=True),
+        (1,),
+        (),
+        collective_id=2,
+        megabytes=16,
         name="head_step",
-    )(pool, head, targets, valid, count)
-
-
-def total_kernel(x_ref, o_ref, near, every, summed, send, recv):
-    at = place()
-    sems = (send, recv)
-    greet_all(at)
-    copies = send_near(at, lambda peer: x_ref, near, sems, 0)
-    near[at["y"], at["core"]] = x_ref[...]
-    for copy in copies:
-        copy.wait()
-    summed[...] = jnp.sum(near[...].reshape((8,) + summed.shape), axis=0)
-    copies = send_plane(at, lambda peer: summed, every, sems, 7)
-    every[at["x"], at["z"]] = summed[...]
-    for copy in copies:
-        copy.wait()
-    o_ref[...] = jnp.sum(every[...].reshape((16,) + summed.shape), axis=0)
-
-
-def total_all(value):
-    return pl.pallas_call(
-        total_kernel,
-        out_shape=jax.ShapeDtypeStruct(value.shape, value.dtype),
-        in_specs=[pl.BlockSpec(memory_space=pltpu.VMEM)],
-        out_specs=pl.BlockSpec(memory_space=pltpu.VMEM),
-        scratch_shapes=[
-            pltpu.VMEM((4, 2) + value.shape, value.dtype),
-            pltpu.VMEM((4, 4) + value.shape, value.dtype),
-            pltpu.VMEM(value.shape, value.dtype),
-            pltpu.SemaphoreType.DMA((22,)),
-            pltpu.SemaphoreType.DMA((22,)),
-        ],
-        compiler_params=pltpu.CompilerParams(collective_id=4, has_side_effects=True),
-        name="total_all",
-    )(value)
+    )
 
 
 def across_cores(value):
@@ -1161,222 +1510,87 @@
     scale = HEAD ** (-0.5)
     own_rows = square_weights.shape[1]
 
-    def pad_rows(value):
-        return jnp.pad(value, ((0, PAD - own_rows), (0, width - value.shape[1])))
-
-    mine = lax.dynamic_index_in_dim(patches, micro, 0, keepdims=False)[0]
-    theirs = across_y(lax.dynamic_index_in_dim(patches, 1 - micro, 0, keepdims=False)[0])
-    patch_rows = jnp.where(
-        micro == 0, jnp.concatenate([mine, theirs]), jnp.concatenate([theirs, mine])
-    )
-    mine = lax.dynamic_index_in_dim(expert_ids, micro, 0, keepdims=False)[0]
-    theirs = across_y(lax.dynamic_index_in_dim(expert_ids, 1 - micro, 0, keepdims=False)[0])
-    ids = jnp.where(micro == 0, jnp.concatenate([mine, theirs]), jnp.concatenate([theirs, mine]))
-
-    table_t = position_table.T
-    table_high = lax.reduce_precision(table_t, 8, 7)
-    table_low = (table_t - table_high).astype(bfloat)
-    vector_t = vector_params.T
-    vector_high = lax.reduce_precision(vector_t, 8, 7)
-    vector_low = (vector_t - vector_high).astype(bfloat)
+    gap = jnp.zeros((own_rows, 6), jnp.float32)
     extra = jnp.concatenate(
-        [table_high.astype(bfloat), router_weight.astype(bfloat), vector_high.astype(bfloat), vector_low],
-        axis=1,
-    )
-    square_low = square_weights.astype(bfloat)
-    spare = jnp.pad(table_low, ((0, 0), (0, width - PATCHES))).reshape(3, 2, width)
-    payload = jnp.concatenate(
-        [square_low[0], spare[0], square_low[1], spare[1], square_low[2], spare[2]]
-        + [pad_rows(square_low[3]), pad_rows(square_low[4]), pad_rows(extra)],
-        axis=0,
-    ).reshape(3, 16, width)
-    *squares, extra, low = gather_all(payload)
-
-    quarter = lax.optimization_barrier((expert_weights, extra))[0][0].astype(bfloat)
-    quarter_y = across_y(quarter)
-    table = (
-        extra[:, :PATCHES].astype(jnp.float32) + low[:, :PATCHES].astype(jnp.float32)
-    ).T
-    router = extra[:, PATCHES : PATCHES + num_expert]
-    begin = PATCHES + num_expert
-    vectors = (
-        extra[:, begin : begin + 10].astype(jnp.float32)
-        + extra[:, begin + 10 : begin + 20].astype(jnp.float32)
-    ).T
-    table_rows = jnp.concatenate(
-        [
-            lax.dynamic_slice_in_dim(table, core * block, block, 0),
-            lax.dynamic_slice_in_dim(table, (2 + core) * block, block, 0),
-        ]
-    )
-    head_low = head_weight.astype(bfloat)
+        [position_table.T, router_weight, vector_params.T, gap, vector_params.T], axis=1
+    )
+    extra = jnp.pad(extra, ((0, 0), (0, width - extra.shape[1])))
     valid = (label_count > 0).astype(jnp.float32)
     image_count = jnp.sum(valid)
-    expert_range = jnp.arange(num_expert, dtype=jnp.int32)
-    label_range = jnp.arange(labels.shape[2], dtype=jnp.int32)
-
-    flat_hit = ids[:, :, None] == expert_range[None, None, :]
-    flat_hit = flat_hit.reshape(2, block * num_top, num_expert).astype(jnp.int32)
-    before = jnp.cumsum(flat_hit, axis=1) - flat_hit
-    slot = jnp.sum(before * flat_hit, axis=2) + jnp.array([[0], [CAP]], jnp.int32)
-    slot = slot.reshape(rows, num_top)
-    target = jnp.where(slot < SLOTS, ids * SLOTS + slot, MAIN + ids * TAIL + slot - SLOTS)
-    target_t = target.T
-
-    def by_place(value):
-        return value.reshape(2, 4, 2, 4, -1).transpose(1, 3, 0, 2, 4).reshape(2 * num_exp, -1)
-
-    label_rows, count_rows = by_place(labels), by_place(label_count)
-    live = label_range[None, :] < count_rows
-    head_cols_pad = -(-vocab_dev // LANES) * LANES
-    columns = device_index * vocab_dev + jnp.arange(head_cols_pad, dtype=jnp.int32)
-    targets = jnp.any(
-        (label_rows[:, :, None] == columns[None, None, :]) & live[:, :, None], axis=1
-    ).astype(jnp.float32)
-    valid_rows = (count_rows > 0).astype(jnp.float32)
-    head_low = jnp.pad(head_low, ((0, 0), (0, head_cols_pad - vocab_dev)))
-
-    slot_index = jnp.arange(num_exp * 4 * PAD, dtype=jnp.int32)
-
-    def picker(which, offset):
-        first = (slot_index // (num_exp * 2 * PAD)) * (2 * num_exp) + which * num_exp
-        owner = first + (slot_index % (num_exp * 2 * PAD)) // (2 * PAD)
-        inside = slot_index % (2 * PAD) - offset
-        row = jnp.where((inside >= 0) & (inside < own_rows), owner * own_rows + inside, -1)
-        return (jnp.arange(width, dtype=jnp.int32)[:, None] == row[None, :]).astype(bfloat)
-
-    picks = {offset: (picker(core, offset), picker(1 - core, offset)) for offset in (0, PAD)}
-
-    def share_left(value, offset):
-        mine, theirs = (plain_dot(value, pick).astype(bfloat) for pick in picks[offset])
-        return jnp.concatenate([mine, across_cores(theirs)])
-
-    def share_right(value):
-        return jnp.concatenate([value, across_cores(value)])
-
-    left_patches = share_left(patch_rows, 0)
-    vectors = jnp.pad(vectors, ((0, 6), (0, 0)))
-    router = jnp.pad(router, ((0, 0), (0, LANES - num_expert)))
-    embed, hidden_one, query, keys, values, mixed, after_attn, hidden_two, gate_probs, gates, lse = attend(
-        patch_rows, squares, vectors, table_rows, router, ids
-    )
-    quarter_y, hidden_two = lax.optimization_barrier((quarter_y, hidden_two))
-    received, chosen, after_moe, pool = experts_forward(
-        hidden_two, target_t, target, gates, after_attn, vectors, quarter, quarter_y
+    live = jnp.arange(labels.shape[2], dtype=jnp.int32) < label_count[:, :, None]
+    live_labels = jnp.where(live, labels, -1).reshape(2 * num_exp, -1)
+
+    wide_ids = jnp.pad(expert_ids.reshape(2, block, num_top), ((0, 0), (0, 0), (0, LANES - num_top)))
+    *squares, extra, low, patch_rows, ids, quarter = gather_all(
+        square_weights, extra, patches.reshape(2, block, width), wide_ids, expert_weights[0]
+    )
+    patch_rows, ids = patch_rows.reshape(rows, width), ids.reshape(rows, LANES)
+
+    across_in = across_y(quarter[0])
+    (
+        embed, hidden_one, query, keys, values, mixed, after_attn, hidden_two,
+        gate_probs, gates, lse, vectors, router, target, target_t, hidden_kept, *squares,
+    ) = attend(patch_rows, squares, extra, low, ids)
+    across_in, hidden_two = lax.optimization_barrier((across_in, hidden_two))
+    received, received_y, chosen, after_moe, pool, across_out = experts_forward(
+        hidden_two, target_t, target, gates, after_attn, vectors, quarter, across_in
     )
     row_grad, head_g, loss_part = head_step(
-        pool, head_low, targets, valid_rows, image_count.reshape(1, 1)
-    )
-    head_g = head_g[:, :vocab_dev]
-    loss_part = loss_part[0, 0]
-    dmoe_in, dgate_logits, final_sums, dhidden, to_y, expert_g = experts_backward(
-        row_grad, after_moe, chosen, gates, gate_probs, ids, received, target_t, target, vectors, quarter, quarter_y
-    )
-    from_y = across_y(to_y)
-    left_one = [share_left(hidden_one, offset) for offset in (0, PAD)]
-    left_mixed = share_left(mixed, 0)
-    router_grad = over_rows(hidden_two, dgate_logits)[:, :num_expert]
+        pool, head_weight.T, live_labels, image_count.reshape(1, 1)
+    )
+    dmoe_in, dgate_logits, final_sums, dhidden, expert_g, expert_squared = experts_backward(
+        row_grad, after_moe, chosen, gates, gate_probs, ids, received, received_y,
+        target_t, target, vectors, quarter, across_in, across_out,
+    )
     dafter_low, dquery_low, dkey_low, dvalue_low, dembed_low, sums = attend_back(
         dmoe_in,
         dhidden,
         dgate_logits,
         embed,
         after_attn,
-        hidden_one,
         query,
         keys,
         values,
         lse,
-        *squares[1:],
+        *squares,
         vectors,
         router,
     )
-    right_after = share_right(dafter_low)
-    right_query, right_key, right_value = (
-        share_right(value) for value in (dquery_low, dkey_low, dvalue_low)
-    )
-    right_embed = share_right(dembed_low)
-
-    vector_grad = jnp.concatenate([sums, final_sums[:2]])
-    few = jnp.concatenate([vector_grad, router_grad.T], axis=0)
-    few = few + across_cores(few)
-    count = few.shape[0]
-    few_high = lax.reduce_precision(few, 8, 7)
-    embed_all = jnp.where(
-        core == 0, right_embed, jnp.concatenate([right_embed[rows:], right_embed[:rows]])
-    )
-    extra_right = jnp.concatenate(
-        [embed_all, few_high.astype(bfloat), (few - few_high).astype(bfloat)]
-        + [jnp.zeros((width - PATCHES - 2 * count, width), bfloat)],
-        axis=0,
-    ).T
-    def pair(lefts, rights):
-        total = over_rows(jnp.concatenate(lefts), jnp.concatenate(rights))
-        return total.astype(bfloat).reshape(2, 4, 2, 4, 2 * PAD, width)
-
-    owned = scatter_all(
-        [
-            pair([left_patches, left_one[1]], [right_embed, right_query]),
-            pair([left_one[0], left_one[1]], [right_key, right_value]),
-            pair([left_mixed, picks[PAD][0]], [right_after, extra_right]),
-        ]
-    )
+    *owned, totals = shared_gradients(
+        patch_rows, hidden_one, mixed, dembed_low, dquery_low, dkey_low, dvalue_low, dafter_low,
+        hidden_kept, dgate_logits, sums, final_sums, head_g, expert_squared, loss_part, square_rows, router_rows[None],
+    )
+    head_g = head_g[:vocab_dev].T
+    expert_g = expert_g[None]
     owned = [half for part in owned for half in (part[:own_rows], part[PAD : PAD + own_rows])]
-    owned, from_y = lax.optimization_barrier((owned, from_y))
-    expert_g = (expert_g + from_y.astype(jnp.float32))[None]
     square_g = jnp.stack(owned[:5])
     extra_g = owned[5]
-    table_g = extra_g[:, :PATCHES].reshape(own_rows, 2, 2, block)
-    table_g = table_g.transpose(0, 2, 1, 3).reshape(own_rows, PATCHES).T
-    few_g = extra_g[:, PATCHES : PATCHES + count] + extra_g[:, PATCHES + count : PATCHES + 2 * count]
-    vector_g = few_g[:, :10].T
-    router_g = few_g[:, 10:]
-    norm_part = (
-        jnp.sum(square_g * square_g)
-        + jnp.sum(router_g * router_g)
-        + jnp.sum(table_g * table_g)
-        + jnp.sum(vector_g * vector_g)
-        + jnp.sum(head_g * head_g)
-        + jnp.sum(expert_g * expert_g)
-    )
+    second = 3 * LANES
+    few_at = EXTRA + num_expert
+    vector_at = EXTRA + 96
+
+    def positions(value):
+        return jnp.concatenate(
+            [value[:, start : start + block] for start in (0, second, block, second + block)], axis=1
+        )
+
+    table_g = positions(extra_g).T
+    router_g = extra_g[:, few_at : few_at + num_expert]
+    vector_g = extra_g[:, vector_at : vector_at + 10].T
     square_rowmean = jnp.mean(square_g * square_g, axis=2)
     router_rowmean = jnp.mean(router_g * router_g, axis=1)
-    expert_rowsq = jnp.sum(expert_g * expert_g, axis=-1)
-    expert_rowsq = expert_rowsq + across_cores(expert_rowsq)
-    expert_mine = expert_rowsq + across_y(expert_rowsq)
-    terms = (
-        loss_part,
-        norm_part,
-        jnp.sum(square_g * square_g, axis=1),
-        jnp.sum(square_rows, axis=1),
-        jnp.sum(square_rowmean, axis=1),
-        jnp.sum(router_g * router_g, axis=0),
-        jnp.sum(router_rows),
-        jnp.sum(router_rowmean),
-        jnp.sum(table_g * table_g, axis=1),
-        jnp.sum(head_g * head_g, axis=1),
-    )
-    flat = jnp.concatenate([term.reshape(-1) for term in terms])
-    length = flat.shape[0]
-    padded = -(-length // (8 * LANES)) * 8 * LANES
-    flat = total_all(jnp.pad(flat, (0, padded - length)).reshape(-1, LANES)).reshape(-1)
-    totals = []
-    begin = 0
-    for term in terms:
-        totals.append(flat[begin : begin + term.size].reshape(term.shape))
-        begin += term.size
-    (
-        loss_total,
-        norm_total,
-        square_colsq,
-        square_rows_sum,
-        square_mean_sum,
-        router_colsq,
-        router_rows_sum,
-        router_mean_sum,
-        table_rowsq,
-        head_rowsq,
-    ) = totals
+    loss_total = totals[7, 0]
+    norm_total = jnp.sum(totals[:7]) + totals[7, 1]
+    square_colsq = totals[:5]
+    square_rows_sum = totals[7, 2:7]
+    square_mean_sum = jnp.mean(square_colsq, axis=1)
+    router_colsq = totals[6, few_at : few_at + num_expert]
+    router_rows_sum = totals[7, 7]
+    router_mean_sum = jnp.sum(router_colsq) / num_expert
+    table_rowsq = positions(totals[6:7])[0]
+    head_rowsq = totals[5]
+    expert_mine = totals[8:10][None]
+    expert_colmean = (expert_squared[2:4] / width)[None]
     grad_norm = jnp.sqrt(norm_total)
     clip = jnp.minimum(1.0, CLIP_NORM / grad_norm)
     clip_sq = clip * clip
@@ -1445,7 +1659,7 @@
         clip_sq * expert_mine / (ff_dev * num_rep) + EPS_SQ
     )
     expert_cols_next = DECAY * expert_cols + keep * (
-        clip_sq * jnp.mean(expert_g * expert_g, axis=2) + EPS_SQ
+        clip_sq * expert_colmean + EPS_SQ
     )
     expert_rate = jnp.array([0.3 / math.sqrt(D), 4.8 / math.sqrt(FF)], jnp.float32)[
         None, :, None, None

time: 466 us -> 379 us (0.81)
  other arithmetic: 54.4 us -> 16.3 us
  matrix products: 26.5 us -> 0 us
  local copies, waits for them, and re-layouts: 34 us -> 8.88 us
  starting transfers between devices: 25.4 us -> 1.08 us
  Pallas kernels: 312 us -> 335 us
  waiting for transfers between devices: 0.04 us -> 5.82 us
    dot_general x12 -> x0, matrix products: 26.5 us -> none  [the longest x4 13.8 us: over_rows(): lax.dot_general(left, right, (((0,), (0,)), ((), ())), preferred_element_...]
    pallas_call x8 -> x7, Pallas kernels: 312 us -> 335 us  [the longest x6 286 us: staged_call(): pl.pallas_call(kernel, out_shape=[pltpu.HBM(*shape) if index in far_out +...]
    ppermute x11 -> x0, starting transfers between devices: 16.1 us -> none  [across_cores(): return lax.ppermute(value, 'rep', CORE_SWAP)]
    convert_element_type x10 -> x0, other arithmetic: 11.5 us -> none  [the longest x1 6.04 us: shards(): lax.optimization_barrier((expert_weights, extra))[0][0].astype(bfloat)]
    ppermute x5 -> x1, starting transfers between devices: 9.31 us -> 1.08 us  [across_y(): return lax.ppermute(value, 'rep', Y_SWAP)]
    concatenate x6 -> x1, local copies, waits for them, and re-layouts: 7.41 us -> 0.85 us  [shards(): jnp.concatenate([position_table.T, router_weight, vector_params.T, gap, v...]
    reduce_sum x7 -> x2, other arithmetic: 7.32 us -> 1.27 us  [the longest x1 0.67 us: shards(): router_mean_sum = jnp.sum(router_colsq) / num_expert]
    unnamed x163 -> x79, local copies, waits for them, and re-layouts: 11.3 us -> 5.26 us
  transfers between devices with their start and end apart: 16 -> 1, of which waited for: 0 -> 1; matrix products, arithmetic and copies ran while one was open for 17% -> 0% of each run, Pallas kernels for 63% -> 5%
where the time goes in v3:
time: 379 us; the launch traced here: 374 us
  Pallas kernels  335 us (88%)
  other arithmetic  16.3 us (4%)
  local copies, waits for them, and re-layouts  8.88 us (2%)
  between operations  6.74 us (2%)
  waiting for transfers between devices  5.82 us (2%)
    pallas_call x6, Pallas kernels, staged_call(): pl.pallas_call(kernel, out_shape=[pltpu.HBM(*shape) if index in far_out +...  286 us
    pallas_call x1, Pallas kernels, gather_all(): pl.pallas_call(gather_kernel, out_shape=[jax.ShapeDtypeStruct((D, D), jnp...  49.1 us
  transfers between devices with their start and end apart: 1, of which 1 were waited for; matrix products, arithmetic and copies ran while one was open for 0% of the time, Pallas kernels for 5%

profile of v3, /device:TPU:1, one launch (start us, length us, event | category | flops | bytes accessed | tf_op | source)
XLA Modules:
  0.0 374.1 jit_solution(8184253671774271042)
XLA Ops:
  0.7 0.8 concatenate.9
  1.5 0.8 copy.49
  2.4 0.7 pad.9.ids
  3.0 0.9 copy-done.2
  3.9 49.1 %gather_weights.1 = (bf16[768,768]{1,0:T(8,128)(2,1)S(1)}, bf16[768,768]{1,0:T(8,128)(2,1)S(1)}, bf16[768,768]{1,0:T(8,128)(2,1)S(1)}, bf16[768,768]{1,0:T(8,128...) custom-call(f32[5,6,768]{2,1,0:T(8,128)S(1)} %copy-done.2, ...), custom_call_target="tpu_custom_call" | custom-call | tf_op jit(solution)/shard_map/gather_weights/pallas_call | solution.py:323
  53.1 1.3 slice_bitcast_fusion
  54.4 0.0 copy-start.29
  54.4 0.0 copy-start.12
  54.4 1.1 collective-permute-start
  55.5 20.3 %attend.1 = (f32[288,768]{1,0:T(8,128)}, bf16[288,768]{1,0:T(8,128)(2,1)}, bf16[288,768]{1,0:T(8,128)(2,1)}, bf16[2,288,768]{2,1,0:T(8,128)(2,1)}, bf16[2,288,76...) custom-call(bf16[288,768]{1,0:T(8,128)(2,1)} %bitcast.58, ...), custom_call_target="tpu_custom_call" | custom-call | tf_op jit(solution)/shard_map/attend/pallas_call | solution.py:151
  75.8 0.6 fusion.2
  76.4 0.1 fusion
  76.5 5.8 %collective-permute-done.refs_7_.refs_12_ = bf16[768,768]{1,0:T(8,128)(2,1)S(1)} collective-permute-done((bf16[768,768]{1,0:T(8,128)(2,1)S(1)}, bf16[768,768]{1,0:T(8,128)(2,1)S(1)}, u32[]{:S(2)}, u32[]{:S(2)}) %collective-permute-start) | collective-permute-done | bytes 1179680 | tf_op jit(solution)/shard_map/ppermute | solution.py:1470
  82.3 1.0 copy-done.7
  83.3 76.9 %experts_forward.1 = (bf16[640,768]{1,0:T(8,128)(2,1)}, bf16[640,768]{1,0:T(8,128)(2,1)}, bf16[2,288,768]{2,1,0:T(8,128)(2,1)}, f32[288,768]{1,0:T(8,128)}, f32[...) custom-call(bf16[288,768]{1,0:T(8,128)(2,1)S(1)} %get-tuple-element.96.refs_0_, ...), custom_call_target="tpu_custom_call" | custom-call | tf_op jit(solution)/shard_map/experts_forward/pallas_call | solution.py:151
  160.3 29.6 %head_step.1 = (f32[8,128]{1,0:T(8,128)S(1)}, f32[256,768]{1,0:T(8,128)S(1)}, f32[1,1]{1,0:T(1,128)}) custom-call(f32[8,128]{1,0:T(8,128)S(1)} %get-tuple-element.103.refs_0_, f32[171,768]{1,0:T(8,128)} %bitcast.57, s32[64,64]{1,0:T(8,128)S(1)} %bitcast.52, f32[1,1]{1,0:T(1,128)} %bitcast.10.refs_3_), custom_call_target="tpu_custom_call" | custom-call | tf_op jit(solution)/shard_map/head_step/pallas_call | solution.py:151
  189.8 76.6 %experts_backward.1 = (f32[288,768]{1,0:T(8,128)}, bf16[288,128]{1,0:T(8,128)(2,1)S(1)}, f32[8,768]{1,0:T(8,128)S(1)}, f32[288,768]{1,0:T(8,128)}, f32[2,768,768]{2,1,0:T(8,128)}, /*index=5*/f32[8,768]{1,0:T(8,128)S(1)}) custom-call(f32[8,128]{1,0:T(8,128)S(1)} %get-tuple-element.104.refs_0_, f32[288,768]{1,0:T(8,128)} %get-tuple-element.105.refs_1_, ...), custom_call_target="tpu_custom_call" | custom-call | tf_op jit(solution)/shard_map/experts_backward/pallas_call | solution.py:151
  266.4 1.2 copy-done
  267.6 1.2 copy-done.1
  268.8 19.6 %attend_back.1 = (bf16[288,768]{1,0:T(8,128)(2,1)S(1)}, bf16[288,768]{1,0:T(8,128)(2,1)S(1)}, bf16[288,768]{1,0:T(8,128)(2,1)S(1)}, bf16[288,768]{1,0:T(8,128)(2...) custom-call(f32[288,768]{1,0:T(8,128)S(1)} %copy-done, f32[288,768]{1,0:T(8,128)S(1)} %copy-done.1, ...), custom_call_target="tpu_custom_call" | custom-call | tf_op jit(solution)/shard_map/attend_back/pallas_call | solution.py:151
  288.5 63.2 %shared_gradients.1 = (f32[16,768]{1,0:T(8,128)S(1)}, f32[16,768]{1,0:T(8,128)S(1)}, f32[16,768]{1,0:T(8,128)S(1)}, f32[16,768]{1,0:T(8,128)S(1)}) custom-call(bf16[288,768]{1,0:T(8,128)(2,1)} %bitcast.59, bf16[288,768]{1,0:T(8,128)(2,1)} %get-tuple-element.92.refs_1_, bf16[288,768]{1,0:T(8,128)(2,1)} %get-tuple-element.93.refs_2_, ...), custom_call_target="tpu_custom_call" | custom-call | tf_op jit(solution)/shard_map/shared_gradients/pallas_call | solution.py:151
  351.7 0.7 slice_reduce_fusion.2
  352.4 0.6 slice_reduce_fusion
  353.0 0.1 multiply_reduce_fusion
  353.1 0.6 fusion.9
  353.7 0.1 fusion.8
  353.8 0.2 multiply_reduce_fusion.3
  354.0 0.1 fusion.7
  356.8 0.1 fusion.4
  356.9 0.0 copy-start.14
  357.0 0.1 bitcast_add_fusion.2
  357.1 0.6 fusion.5
  358.3 0.1 multiply_reduce_fusion.5
  358.4 0.6 fusion.6
  359.7 0.7 multiply_subtract_fusion.3
  360.4 0.1 multiply_add_fusion
  360.5 0.1 fusion.3
  360.6 0.1 multiply_reduce_fusion.1
  360.8 0.0 slice-start
  360.8 0.0 copy-start.32
  360.8 0.0 copy-start.31
  360.8 5.2 %multiply_bitcast_fusion = f32[1,2,768,768]{3,2,1,0:T(8,128)} fusion(f32[2,768,768]{2,1,0:T(8,128)} %get-tuple-element.139, f32[]{:T(128)S(6)} %min_shard_map.3), kind=kLoop, calls=%fused_computation.1 | loop fusion | flops 1179648 | bytes 9437188 | tf_op jit(solution)/shard_map/mul | solution.py:1657
  366.1 0.2 multiply_reduce_fusion.2
  366.3 0.7 multiply_subtract_fusion.2
  367.0 0.7 multiply_subtract_fusion.4
  367.7 1.2 multiply_subtract_fusion
  368.9 0.8 multiply_subtract_fusion.1
  369.7 2.8 bitcast_subtract_fusion
  (77 shorter events, 0.2 us)
Async XLA Ops:
  3.0 0.9 copy-start.2
  54.4 21.4 %copy-start.29 = (s32[2,32]{1,0:T(2,128)S(1)}, s32[2,32]{1,0:T(2,128)}, u32[]{:S(2)}) copy-start(s32[2,32]{1,0:T(2,128)} %param.26) | copy-start | bytes 772
  54.4 22.0 %copy-start.12 = (s32[2,32,64]{2,1,0:T(8,128)S(1)}, s32[2,32,64]{2,1,0:T(8,128)}, u32[]{:S(2)}) copy-start(s32[2,32,64]{2,1,0:T(8,128)} %param.25) | copy-start | bytes 49156
  54.4 27.9 %collective-permute-start = (bf16[768,768]{1,0:T(8,128)(2,1)S(1)}, bf16[768,768]{1,0:T(8,128)(2,1)S(1)}, u32[]{:S(2)}, u32[]{:S(2)}) collective-permute-start(bf16[768,768]{1,0:T(8,128)(2,1)S(1)} %slice_bitcast_fusion), channel_id=1, source_target_pairs={{0,64},{32,96},{64,0},{96,32},{1,65},{33,97},{65,1},{97,33},{2,66}... | collective-permute-start | bytes 3538952 | tf_op jit(solution)/shard_map/ppermute | solution.py:1470
  82.3 1.0 copy-start.7
  266.4 1.2 copy-start
  267.6 1.2 copy-start.1
  268.8 19.7 %copy-start.4 = (f32[5,6]{1,0:T(8,128)S(1)}, f32[5,6]{1,0:T(8,128)}, u32[]{:S(2)}) copy-start(f32[5,6]{1,0:T(8,128)} %refs_15_.1) | copy-start | bytes 364
  268.8 19.7 %copy-start.5 = (f32[6]{0:T(128)S(1)}, f32[6]{0:T(128)}, u32[]{:S(2)}) copy-start(f32[6]{0:T(128)} %param.35) | copy-start | bytes 76
  288.4 68.4 %copy-start.20 = (f32[1,2,768]{2,1,0:T(2,128)S(1)}, f32[1,2,768]{2,1,0:T(2,128)}, u32[]{:S(2)}) copy-start(f32[1,2,768]{2,1,0:T(2,128)} %param.41) | copy-start | bytes 18436
  288.4 68.4 %copy-start.21 = (f32[1,2,768]{2,1,0:T(2,128)S(1)}, f32[1,2,768]{2,1,0:T(2,128)}, u32[]{:S(2)}) copy-start(f32[1,2,768]{2,1,0:T(2,128)} %param.42) | copy-start | bytes 18436
  288.4 68.6 %copy-start.33 = (f32[32]{0:T(128)S(1)}, f32[32]{0:T(128)}, u32[]{:S(2)}) copy-start(f32[32]{0:T(128)} %param.36) | copy-start | bytes 388
  288.4 68.7 %copy-start.23 = (f32[768]{0:T(1024)S(1)}, f32[768]{0:T(1024)}, u32[]{:S(2)}) copy-start(f32[768]{0:T(1024)} %param.39) | copy-start | bytes 9220
  288.4 70.0 %copy-start.24 = (f32[576]{0:T(1024)S(1)}, f32[576]{0:T(1024)}, u32[]{:S(2)}) copy-start(f32[576]{0:T(1024)} %param.37) | copy-start | bytes 6916
  288.4 71.3 %copy-start.11 = (f32[10,6]{0,1:T(8,128)S(1)}, f32[10,6]{0,1:T(8,128)}, u32[]{:S(2)}) copy-start(f32[10,6]{0,1:T(8,128)} %param.32) | copy-start | bytes 724
  288.4 71.3 %copy-start.25 = (f32[10,6]{0,1:T(8,128)S(1)}, f32[10,6]{0,1:T(8,128)}, u32[]{:S(2)}) copy-start(f32[10,6]{0,1:T(8,128)} %param.43) | copy-start | bytes 724
  288.4 72.0 %copy-start.15 = (f32[5,768]{1,0:T(8,128)S(1)}, f32[5,768]{1,0:T(8,128)}, u32[]{:S(2)}) copy-start(f32[5,768]{1,0:T(8,128)} %param.34) | copy-start | bytes 46084
  356.7 11.0 %copy-start.8 = (f32[768,171]{0,1:T(8,128)S(1)}, f32[768,171]{0,1:T(8,128)}, u32[]{:S(2)}) copy-start(f32[768,171]{0,1:T(8,128)} %param.30) | copy-start | bytes 1575940
  356.8 9.3 %copy-start.30 = (f32[171]{0:T(256)S(1)}, f32[171]{0:T(256)}, u32[]{:S(2)}) copy-start(f32[171]{0:T(256)} %param.40) | copy-start | bytes 2056
  356.8 9.5 %copy-start.34 = (f32[6]{0:T(128)S(1)}, f32[6]{0:T(128)}, u32[]{:S(2)}) copy-start(f32[6]{0:T(128)} %param.38) | copy-start | bytes 76
  356.8 9.5 %copy-start.10 = (f32[576,6]{0,1:T(8,128)S(1)}, f32[576,6]{0,1:T(8,128)}, u32[]{:S(2)}) copy-start(f32[576,6]{0,1:T(8,128)} %param.29) | copy-start | bytes 41476
  356.9 12.7 %copy-start.13 = (f32[1,2,768]{2,1,0:T(2,128)}, f32[1,2,768]{2,1,0:T(2,128)S(1)}, u32[]{:S(2)}) copy-start(f32[1,2,768]{2,1,0:T(2,128)S(1)} %get-tuple-element.144) | copy-start | bytes 18436
  356.9 12.7 %copy-start.14 = (f32[1,2,768]{2,1,0:T(2,128)}, f32[1,2,768]{2,1,0:T(2,128)S(1)}, u32[]{:S(2)}) copy-start(f32[1,2,768]{2,1,0:T(2,128)S(1)} %get-tuple-element.170) | copy-start | bytes 18436
  357.1 10.0 %copy-start.27 = (f32[32]{0:T(128)}, f32[32]{0:T(128)S(1)}, u32[]{:S(2)}) copy-start(f32[32]{0:T(128)S(1)} %bitcast_add_fusion.2) | copy-start | bytes 388
  357.7 10.0 %copy-start.16 = (f32[768]{0:T(1024)}, f32[768]{0:T(1024)S(1)}, u32[]{:S(2)}) copy-start(f32[768]{0:T(1024)S(1)} %get-tuple-element.148) | copy-start | bytes 9220
  359.0 7.3 %copy-start.19 = (f32[576]{0:T(1024)}, f32[576]{0:T(1024)S(1)}, u32[]{:S(2)}) copy-start(f32[576]{0:T(1024)S(1)} %get-tuple-element.152) | copy-start | bytes 6916
  360.5 8.3 %copy-start.9 = (f32[5,768]{1,0:T(8,128)}, f32[5,768]{1,0:T(8,128)S(1)}, u32[]{:S(2)}) copy-start(f32[5,768]{1,0:T(8,128)S(1)} %get-tuple-element.168) | copy-start | bytes 46084
  360.7 8.1 %copy-start.17 = (f32[5,6]{1,0:T(8,128)}, f32[5,6]{1,0:T(8,128)S(1)}, u32[]{:S(2)}) copy-start(f32[5,6]{1,0:T(8,128)S(1)} %multiply_add_fusion.4) | copy-start | bytes 364
  360.8 8.9 %slice-start = ((s8[4718592]{0:T(1024)(128)(4,1)}), s8[4194304]{0:T(1024)(128)(4,1)S(1)}, s32[]{:S(2)}) async-start(s8[4718592]{0:T(1024)(128)(4,1)} %bitcast.55), calls=%async_computation | async-start | bytes 8388608
  360.8 6.3 %copy-start.18 = (f32[6,32]{1,0:T(8,128)S(1)}, f32[6,32]{1,0:T(8,128)}, u32[]{:S(2)}) copy-start(f32[6,32]{1,0:T(8,128)} %param.28) | copy-start | bytes 2308
  360.8 8.1 %copy-start.3 = (f32[5,6,768]{2,1,0:T(8,128)S(1)}, f32[5,6,768]{2,1,0:T(8,128)}, u32[]{:S(2)}) copy-start(f32[5,6,768]{2,1,0:T(8,128)} %own_squares.1) | copy-start | bytes 276484
  360.8 8.1 %copy-start.32 = (f32[5]{0:T(128)S(1)}, f32[5]{0:T(128)}, u32[]{:S(2)}) copy-start(f32[5]{0:T(128)} %constant.124) | copy-start | bytes 64
  360.8 8.8 %slice-start.1 = ((s8[4718592]{0:T(1024)(128)(4,1)}), s8[524288]{0:T(1024)(128)(4,1)S(1)}, s32[]{:S(2)}) async-start(s8[4718592]{0:T(1024)(128)(4,1)} %bitcast.55), calls=%async_computation.1 | async-start | bytes 1048576
  360.8 8.8 %copy-start.6 = (f32[2,768,768]{2,1,0:T(8,128)S(1)}, f32[2,768,768]{2,1,0:T(8,128)}, u32[]{:S(2)}) copy-start(f32[2,768,768]{2,1,0:T(8,128)} %get-tuple-element.139) | copy-start | bytes 14155780
  360.8 8.8 %copy-start.31 = (f32[2]{0:T(128)S(1)}, f32[2]{0:T(128)}, u32[]{:S(2)}) copy-start(f32[2]{0:T(128)} %constant.43.clone) | copy-start | bytes 28
  366.0 6.4 %copy-start.22 = (f32[171]{0:T(256)}, f32[171]{0:T(256)S(1)}, u32[]{:S(2)}) copy-start(f32[171]{0:T(256)S(1)} %multiply_add_fusion.5) | copy-start | bytes 2056
  366.3 6.2 %copy-start.26 = (f32[6]{0:T(128)}, f32[6]{0:T(128)S(1)}, u32[]{:S(2)}) copy-start(f32[6]{0:T(128)S(1)} %get-tuple-element.171) | copy-start | bytes 76
  366.3 6.2 %copy-start.28 = (f32[6]{0:T(128)}, f32[6]{0:T(128)S(1)}, u32[]{:S(2)}) copy-start(f32[6]{0:T(128)S(1)} %get-tuple-element.172) | copy-start | bytes 76

commit v4 on v3

--- a/solution.py
+++ b/solution.py
@@ -14,6 +14,7 @@
 PATCHES = 576
 CAP = 10
 VOCAB_DEV = 171
+EARLY = 256
 EXTRA = 640
 VECTOR_AT = 608
 ROUTER_AT = 64
@@ -31,12 +32,6 @@
 CORE_SWAP = ((0, 1), (1, 0), (2, 3), (3, 2))
 
 
-def layer_norm(value, gain, shift):
-    centred = value - jnp.mean(value, axis=-1, keepdims=True)
-    spread = jnp.mean(centred * centred, axis=-1, keepdims=True)
-    return centred * lax.rsqrt(spread + 1e-06) * gain + shift
-
-
 def plain_dot(left, right):
     return jnp.dot(left, right, preferred_element_type=jnp.float32)
 
@@ -51,11 +46,6 @@
     return lax.dot_general(
         left, right, (((1,), (1,)), ((), ())), preferred_element_type=jnp.float32
     )
-
-
-def factored_step(weight, clipped, rows_next, cols_next, rows_mean, rate):
-    estimate = rows_next[..., :, None] * cols_next[..., None, :] / rows_mean
-    return weight - rate * clipped * lax.rsqrt(estimate)
 
 
 def place():
@@ -87,10 +77,18 @@
     return ref.at[hi, x, low, z]
 
 
-def greet(at):
+NEAR = tuple((y, core) for y in range(4) for core in range(2) if y or core)
+PLANE = tuple((x, z) for x in range(4) for z in range(4) if x or z)
+
+
+def near_peer(at, by):
+    return moved(moved(at, "y", by[0]), "core", by[1])
+
+
+def greet(at, near=False):
     barrier = pltpu.get_barrier_semaphore()
-    peers = [moved(at, axis, by) for axis in ("x", "y", "z") for by in (1, 2, 3)]
-    peers.append(moved(at, "core", 1))
+    peers = [moved(at, axis, by) for axis in ("x", "z") for by in (1, 2, 3)]
+    peers += [near_peer(at, by) for by in NEAR if near or not (by[0] and by[1])]
     for peer in peers:
         pl.semaphore_signal(barrier, inc=1, device_id=device(peer), device_id_type=MESH)
     pl.semaphore_wait(barrier, len(peers))
@@ -173,8 +171,8 @@
 
 
 def gather_kernel(own_squares, own_extra, patches, ids, experts, *refs):
-    squares, extra, spare, image, image_ids, experts_low = refs[:5], *refs[5:10]
-    outs, (x_ref, wide, narrow, send, recv, local, local_in, local_out) = refs[10:13], refs[13:]
+    squares, extra, spare, image, image_ids, experts_low, experts_in, across_part = refs[:5], *refs[5:12]
+    outs, (x_ref, wide, narrow, send, recv, local, local_in, local_out) = refs[12:15], refs[15:]
     at = place()
     sems = (send, recv)
     value = own_extra[...]
@@ -216,14 +214,22 @@
     def store(step):
         return pltpu.make_async_copy(narrow.at[step % 2], lines(experts_low, step), local_out.at[step % 2])
 
+    def store_in(step):
+        lines_in = experts_in.at[pl.ds(step % 3 * 256, 256)]
+        return pltpu.make_async_copy(narrow.at[step % 2], lines_in, local_out.at[2 + step % 2])
+
     def round_experts(step):
         if step < 5:
             fetch(step + 1).start()
         fetch(step).wait()
         if step >= 2:
             store(step - 2).wait()
+            if step < 5:
+                store_in(step - 2).wait()
         narrow[step % 2] = wide[step % 2].astype(jnp.bfloat16)
         store(step).start()
+        if step < 3:
+            store_in(step).start()
 
     fetch(0).start()
     greet(at)
@@ -272,6 +278,8 @@
         for part in range(3):
             flights[part, 2, by].wait_recv()
             forward(part, by)
+    early = remote(experts_low.at[1, pl.ds(0, EARLY)], across_part, sems, 41, moved(at, "y", 2))
+    early.start()
 
     row = lax.broadcasted_iota(jnp.int32, (96, 256), 0)
     column = lax.broadcasted_iota(jnp.int32, (96, 256), 1)
@@ -312,7 +320,7 @@
         if key[1] == 3:
             copy.wait_recv()
     pack(1 - at["core"])
-    for copy in kept + trades:
+    for copy in [*kept, *trades, early]:
         copy.wait()
     for copy in flights.values():
         copy.wait_send()
@@ -324,19 +332,20 @@
         gather_kernel,
         out_shape=[jax.ShapeDtypeStruct((D, D), jnp.bfloat16)] * 7
         + [pltpu.HBM(value.shape, value.dtype) for value in (patches, ids)]
-        + [pltpu.HBM(experts.shape, jnp.bfloat16)],
+        + [pltpu.HBM(experts.shape, jnp.bfloat16), pltpu.HBM(experts.shape[1:], jnp.bfloat16)]
+        + [pltpu.HBM((EARLY, D), jnp.bfloat16)],
         in_specs=[pl.BlockSpec(memory_space=pltpu.VMEM)] * 2 + [pl.BlockSpec(memory_space=pl.ANY)] * 3,
-        out_specs=[pl.BlockSpec(memory_space=pltpu.VMEM)] * 7 + [pl.BlockSpec(memory_space=pl.ANY)] * 3,
+        out_specs=[pl.BlockSpec(memory_space=pltpu.VMEM)] * 7 + [pl.BlockSpec(memory_space=pl.ANY)] * 5,
         scratch_shapes=[pltpu.VMEM(shape, jnp.bfloat16)] * 3
         + [
             pltpu.VMEM((3, 16, D), jnp.bfloat16),
             pltpu.VMEM((2, 256, D), jnp.float32),
             pltpu.VMEM((2, 256, D), jnp.bfloat16),
-            pltpu.SemaphoreType.DMA((41,)),
-            pltpu.SemaphoreType.DMA((41,)),
+            pltpu.SemaphoreType.DMA((42,)),
+            pltpu.SemaphoreType.DMA((42,)),
             pltpu.SemaphoreType.DMA((5,)),
             pltpu.SemaphoreType.DMA((2,)),
-            pltpu.SemaphoreType.DMA((2,)),
+            pltpu.SemaphoreType.DMA((4,)),
         ],
         compiler_params=pltpu.CompilerParams(
             collective_id=0, has_side_effects=True, vmem_limit_bytes=24 * 2**20
@@ -347,20 +356,21 @@
 
 def gradients_kernel(
     staged, patches, hidden_one, mixed, dembed, dquery, dkey, dvalue, dafter, hidden_two, dgate, sums, final_sums,
-    head_grad, expert_squared, loss, square_rows, router_rows, *refs,
+    head_grad, loss, square_rows, router_rows, part_grads, own, rows_y, rows_last, drows_y, drows_last, *refs,
 ):
-    outs, totals, refs = refs[:3], refs[3], refs[1:]
+    outs, totals, kept, expert_cols, refs = refs[:3], refs[3], refs[4], refs[5], refs[3:]
     lefts, tables, rights, left_got, table_got, right_got, few_mine, few_got, few_t, partial, grads = refs[3:14]
     first, total_one, second, total_two, third = (refs[14 + 3 * i : 17 + 3 * i] for i in range(5))
     core_sems, sems = refs[29:31], refs[31:33]
-    parts, total_sems = refs[33], refs[34:36]
+    parts, total_sems, (act_set, dpre_set, rows_t, drows_t) = refs[33], refs[34:36], refs[36:40]
     at = place()
     other = moved(at, "core", 1)
     count = patches.shape[0]
     part_rows = D // 4
+    staged.need(3, 4, 5, 6, 7)
     for index, ref in enumerate((dembed, dquery, dkey, dvalue, dafter)):
         rights[index] = ref[...]
-    greet(at)
+    greet(at, near=True)
     copies = [remote(rights, right_got, core_sems, 0, other)]
     copies[0].start()
     staged.need(0, 1, 2, 8)
@@ -463,20 +473,35 @@
             copy.start()
             flights[part, stage].append(copy)
 
-    for part in range(3):
+    for part in (2, 0, 1):
         for half in range(2):
             finish(part, half)
         launch(part, 0)
     head_squared = jnp.sum(head_grad[...] * head_grad[...], axis=0, keepdims=True)
-    expert_norm = jnp.sum(jnp.sum(expert_squared[0:2, :], axis=1, keepdims=True), axis=0, keepdims=True)
+
+    staged.need(16, 17, 18, 19, 20, 21)
+    for which in range(2):
+        kept[which] = part_grads[which]
+    quarter_set(kept, own, rows_y, drows_y, act_set, dpre_set, rows_t, drows_t)
     for stage in range(3):
-        for part in range(3):
+        if stage == 1:
+            quarter_set(kept, own, rows_last, drows_last, act_set, dpre_set, rows_t, drows_t)
+            staged.give(4)
+            expert_rows = []
+            for which in range(2):
+                square = kept[which] * kept[which]
+                expert_rows.append(jnp.broadcast_to(jnp.sum(square, axis=1, keepdims=True), (D, LANES)).T[0:1])
+                expert_cols[which : which + 1, :] = jnp.sum(square, axis=0, keepdims=True)
+            expert_rows = jnp.concatenate(expert_rows)
+            expert_norm = jnp.sum(jnp.sum(expert_rows, axis=1, keepdims=True), axis=0, keepdims=True)
+        for part in (2, 0, 1):
             for copy in flights[part, stage]:
                 copy.wait_recv()
             landing = landings[stage][part]
             terms = [part_of(sources[stage][part], at, ORDERS[part], stage)[...]]
             terms = [term.astype(jnp.float32) for term in terms + [landing[i] for i in range(3)]]
-            targets[stage][part][...] = (terms[0] + terms[1]) + (terms[2] + terms[3])
+            target = targets[stage][part]
+            target[...] = ((terms[0] + terms[1]) + (terms[2] + terms[3])).astype(target.dtype)
             if stage < 2:
                 launch(part, stage + 1)
 
@@ -494,34 +519,40 @@
         last = last + jnp.where(spot == 2 + k, jnp.sum(square_rows[k : k + 1, :], axis=1, keepdims=True), 0.0)
     last = last + jnp.where(spot == 7, jnp.sum(router_rows[...], axis=1, keepdims=True), 0.0)
     parts[0, 0] = jnp.concatenate(squared[:5] + [head_squared, squared[5], last])
-    parts[0, 1] = expert_squared[...]
-    total = parts.at[0]
-    number = 0
-    for stage, axis in enumerate(("core", "y", "z", "x")):
-        size = 2 if axis == "core" else 4
-        base = 1 + 5 * stage
+    parts[0, 1] = jnp.concatenate([expert_rows, jnp.zeros((PAD - 2, D), jnp.float32)])
+    mine = parts.at[0]
+    trips = []
+    for number, by in enumerate(NEAR):
+        whole = by[0] in (0, 2)
+        slot = parts.at[1 + at["y"] * 2 + at["core"]]
+        source, target = (mine, slot) if whole else (mine.at[0], slot.at[0])
+        trips.append(remote(source, target, total_sems, number, near_peer(at, by)))
+        trips[-1].start()
+    parts[1 + at["y"] * 2 + at["core"]] = mine[...]
+    for trip in trips:
+        trip.wait()
+    value = parts[1, 0]
+    for index in range(1, 8):
+        value = value + parts[1 + index, 0]
+    parts[9, 0] = value
+    low = lax.rem(at["y"], 2) * 2
+    totals[PAD:, :] = (parts[1 + low, 1] + parts[2 + low, 1]) + (parts[5 + low, 1] + parts[6 + low, 1])
+    total = parts.at[9]
+    for stage, axis in enumerate(("z", "x")):
+        base = 10 + 5 * stage
         trips = []
-        for by in range(1, size):
-            whole = axis == "core" or (axis == "y" and by == 2)
-            view = total if whole else total.at[0]
-            slot = parts.at[base + at[axis]]
-            trips.append(remote(view, slot if whole else slot.at[0], total_sems, number, moved(at, axis, by)))
+        for by in (1, 2, 3):
+            number = 7 + 3 * stage + by - 1
+            slot = parts.at[base + at[axis], 0]
+            trips.append(remote(total.at[0], slot, total_sems, number, moved(at, axis, by)))
             trips[-1].start()
-            number += 1
-        parts[base + at[axis]] = total[...]
+        parts[base + at[axis], 0] = total[0]
         for trip in trips:
             trip.wait()
         value = parts[base, 0]
-        for index in range(1, size):
+        for index in range(1, 4):
             value = value + parts[base + index, 0]
         parts[base + 4, 0] = value
-        if axis == "core":
-            parts[base + 4, 1] = parts[base, 1] + parts[base + 1, 1]
-        elif axis == "y":
-            parts[base + 4, 1] = parts[base + at["y"], 1] + parts[base + lax.rem(at["y"] + 2, 4), 1]
-            totals[PAD:, :] = parts[base + 4, 1]
-        else:
-            parts[base + 4, 1] = jnp.zeros((PAD, D), jnp.float32)
         total = parts.at[base + 4]
     totals[:PAD, :] = total[0]
     for copy in copies:
@@ -552,21 +583,22 @@
         pltpu.VMEM((3, 2, 4, 2, 4) + block, low),
     ]
     scratch += [pltpu.VMEM((3,) + one + block, low) for one in ones]
-    scratch += [pltpu.VMEM(one + block, wide) for one in ones]
-    scratch += [pltpu.VMEM((3,) + two + block, wide) for two in twos]
+    scratch += [pltpu.VMEM(one + block, kind) for one, kind in zip(ones, (low, low, wide))]
+    scratch += [pltpu.VMEM((3,) + two + block, kind) for two, kind in zip(twos, (low, low, wide))]
     scratch += [pltpu.VMEM(two + block, wide) for two in twos]
     scratch += [pltpu.VMEM((3,) + block, wide)] * 3
     scratch += [pltpu.SemaphoreType.DMA((6,))] * 2 + [pltpu.SemaphoreType.DMA((27,))] * 2
-    scratch += [pltpu.VMEM((21, 2, PAD, D), wide)] + [pltpu.SemaphoreType.DMA((10,))] * 2
+    scratch += [pltpu.VMEM((20, 2, PAD, D), wide)] + [pltpu.SemaphoreType.DMA((13,))] * 2
+    scratch += [pltpu.VMEM((TOTAL, D), low)] * 2 + [pltpu.VMEM((D, TOTAL), low)] * 2
     return staged_call(
         gradients_kernel,
         operands,
-        [(block, wide)] * 4,
+        [(block, wide)] * 4 + [((2, D, D), wide), ((2, D), wide)],
         scratch,
-        (0, 1, 2, 8),
-        (),
+        (3, 4, 5, 6, 7, 0, 1, 2, 8, 16, 17, 18, 19, 20, 21),
+        (4,),
         collective_id=1,
-        megabytes=36,
+        megabytes=57,
         name="shared_gradients",
     )
 
@@ -753,7 +785,7 @@
     pairs = D // LANES
     zero = jnp.zeros((1, D), jnp.float32)
     wide[...] = over_last(dgate[...], router[...])
-    staged.need(4)
+    staged.need(0, 1, 4)
 
     def second_norm(index, carry):
         part = pl.ds(pl.multiple_of(index * CHUNK, CHUNK), CHUNK)
@@ -768,6 +800,7 @@
     sums[5:6, :] = bias
     sums[6:7, :] = gain
     sums[7:8, :] = shift
+    staged.give(0)
     staged.need(12)
     dmixed[...] = over_last(dafter_low[...], w4[...]).astype(jnp.bfloat16)
     staged.need(5, 6, 7)
@@ -822,6 +855,7 @@
         return carry
 
     lax.fori_loop(0, pairs, gather, 0)
+    staged.give(1, 2, 3)
     staged.need(3, 9, 10, 11)
     wide[...] = (
         over_last(dquery[...], w1[...]) + over_last(dkey[...], w2[...]) + over_last(dvalue[...], w3[...])
@@ -842,6 +876,7 @@
 
     for index, total in enumerate(lax.fori_loop(0, rows // CHUNK, first_norm, (zero,) * 5)):
         sums[index : index + 1, :] = total
+    staged.give(4)
 
 
 def attend_back(*operands):
@@ -856,10 +891,10 @@
         [pltpu.VMEM((rows, D), wide), pltpu.VMEM((rows, D), low)]
         + [pltpu.VMEM((pairs, rows, LANES), wide)] * 6
         + [pltpu.VMEM((rows, D), wide), sems((2 * pairs,)), sems((2 * pairs,))],
-        (4, 12, 5, 6, 7, 3, 9, 10, 11),
-        (),
+        (0, 1, 4, 12, 5, 6, 7, 3, 9, 10, 11),
+        (0, 1, 2, 3, 4),
         collective_id=7,
-        megabytes=22,
+        megabytes=28,
         name="attend_back",
     )
 
@@ -992,7 +1027,7 @@
 
 
 def experts_kernel(
-    staged, hidden, target_row, target_column, gates, after, vec, own, across_in,
+    staged, hidden, target_row, target_column, gates, after, vec, own, across_in, across_part,
     rows, rows_y, chosen, total, pool, across_out,
     weights, sends, lands, backs, returns, act, result, gathered,
     forth_send, forth_recv, back_send, back_recv, weight_send, weight_recv, row_send, row_recv, local,
@@ -1002,9 +1037,11 @@
     other, across_y_peer = meet_experts(at)
     row_copies = []
     near, far = load_experts(own, (across_in,), weights, (weight_send, weight_recv), local, other)
-    trade = remote(own.at[1], weights.at[1, 1], (weight_send, weight_recv), 2, across_y_peer)
+    late = pl.ds(EARLY, D - EARLY)
+    trade = remote(own.at[1, late], weights.at[1, 1, late], (weight_send, weight_recv), 2, across_y_peer)
     pass_on = remote(weights.at[1, 1], weights.at[3, 1], (weight_send, weight_recv), 3, other)
     save = pltpu.make_async_copy(weights.at[1, 1], across_out, local.at[3])
+    near.append(pltpu.make_async_copy(across_part, weights.at[1, 1, pl.ds(0, EARLY)], local.at[4]))
     for copy in near:
         copy.start()
     count = hidden.shape[0]
@@ -1114,10 +1151,10 @@
         + [pltpu.VMEM((4, HALF, D), low), pltpu.VMEM((HALF, D), wide), pltpu.VMEM((TOTAL, D), low)]
         + [sems((GROUP,))] * 4
         + [sems((4,))] * 4
-        + [sems((4,))],
+        + [sems((5,))],
         (4,),
         (0, 1, 2, 3),
-        raw=(6, 7),
+        raw=(6, 7, 8),
         raw_out=(5,),
         collective_id=5,
         megabytes=25,
@@ -1125,10 +1162,50 @@
     )
 
 
+def tile_of(index):
+    half, part = lax.div(index, 3), lax.rem(index, 3)
+    columns = pl.ds(pl.multiple_of(part * 256, 256), 256)
+    return pl.ds(pl.multiple_of(half * HALF, HALF), HALF), columns
+
+
+def gelu_both(value):
+    tanh = gelu_tanh(value)
+    grown = (0.5 * value * (1.0 + tanh)).astype(jnp.bfloat16)
+    return grown, 0.5 * (1.0 + tanh) + 0.5 * value * (1.0 - tanh * tanh) * (
+        GELU_SCALE * (1.0 + 3 * 0.044715 * (value * value))
+    )
+
+
+def quarter_grads(kept, rows_t, drows_t, dpre, act, first):
+    def step(index, carry):
+        columns = pl.ds(pl.multiple_of(index * 256, 256), 256)
+        for which, (left, right) in enumerate(((rows_t, dpre), (drows_t, act))):
+            value = plain_dot(left[...], right[:, columns])
+            kept[which, :, columns] = value if first else kept[which, :, columns] + value
+        return carry
+
+    lax.fori_loop(0, 3, step, 0)
+
+
+def quarter_set(kept, weights, rows, drows, act, dpre, rows_t, drows_t):
+    def step(index, carry):
+        lines, columns = tile_of(index)
+        grown, rate = gelu_both(plain_dot(rows[lines, :], weights[0, :, columns]))
+        act[lines, columns] = grown
+        value = plain_dot(drows[lines, :], weights[1, :, columns])
+        dpre[lines, columns] = (value * rate).astype(jnp.bfloat16)
+        return carry
+
+    lax.fori_loop(0, 6, step, 0)
+    rows_t[...] = rows[...].T
+    drows_t[...] = drows[...].T
+    quarter_grads(kept, rows_t, drows_t, dpre, act, False)
+
+
 def experts_back_kernel(
     staged, row_grad, total, chosen, gates, gate_probs, ids, rows, rows_y, target_row, target_column, vec, own, across_in, across_out,
-    dtotal, dgate, sums, dhidden, kept, squared,
-    weights, sends, lands, backs, returns, slope, dpre, act_own, act_set, dpre_set, rows_far, drows, result, dreturned,
+    dtotal, dgate, sums, dhidden, kept, rows_last, drows_y, drows_last,
+    weights, sends, lands, backs, returns, slope, dpre, act_own, act_set, dpre_set, rows_far, drows, drows_far, result, dreturned,
     rows_t, drows_t, outward,
     forth_send, forth_recv, back_send, back_recv, weight_send, weight_recv, set_send, set_recv, local,
 ):
@@ -1163,6 +1240,7 @@
 
     gain, shift = lax.fori_loop(0, count // CHUNK, final_norm, (zero, zero))
     sums[...] = jnp.concatenate([gain, shift, jnp.zeros((PAD - 2, D), jnp.float32)])
+    staged.give(0)
     slot = iota((TOTAL, count), 0)
     placed = [
         plain_dot((slot == target_row[k : k + 1, :]).astype(jnp.bfloat16), outward[k]) for k in range(2)
@@ -1173,7 +1251,7 @@
     deal(sends, lands, (forth_send, forth_recv), True, 1, GROUP, start_copy)
     staged.need(6, 7)
     set_sems = (set_send, set_recv)
-    moves = [remote(rows, rows_far.at[0], set_sems, 0, other), remote(rows_y, rows_far.at[1], set_sems, 1, other)]
+    moves = [remote(rows, rows_far, set_sems, 0, other), remote(rows_y, rows_last, set_sems, 1, other)]
     for copy in far + moves:
         copy.start()
     keep = pltpu.make_async_copy(sends.at[me], lands.at[0], local.at[3])
@@ -1182,18 +1260,6 @@
     for copy in near:
         copy.wait()
 
-    def tile_of(index):
-        half, part = lax.div(index, 3), lax.rem(index, 3)
-        columns = pl.ds(pl.multiple_of(part * 256, 256), 256)
-        return pl.ds(pl.multiple_of(half * HALF, HALF), HALF), columns
-
-    def gelu_both(value):
-        tanh = gelu_tanh(value)
-        grown = (0.5 * value * (1.0 + tanh)).astype(jnp.bfloat16)
-        return grown, 0.5 * (1.0 + tanh) + 0.5 * value * (1.0 - tanh * tanh) * (
-            GELU_SCALE * (1.0 + 3 * 0.044715 * (value * value))
-        )
-
     def hidden_units(index, carry):
         quarter = lax.div(index, 6)
         lines, columns = tile_of(lax.rem(index, 6))
@@ -1210,18 +1276,17 @@
     for copy in far:
         copy.wait_recv()
     lax.fori_loop(12, 24, hidden_units, 0)
-    rows_t[...] = rows[...].T
     deal(sends, lands, (forth_send, forth_recv), True, 1, GROUP, wait_recv)
-    unpack(lands, drows.at[0], 0, MAIN)
-    moves.append(remote(drows.at[0], drows.at[1], set_sems, 2, across_y_peer))
-    moves.append(remote(drows.at[0], drows.at[2], set_sems, 3, other))
+    unpack(lands, drows, 0, MAIN)
+    moves.append(remote(drows, drows_y, set_sems, 2, across_y_peer))
+    moves.append(remote(drows, drows_far, set_sems, 3, other))
     for copy in moves[2:]:
         copy.start()
 
     def hidden_back(index, carry):
         quarter = lax.div(index, 6)
         lines, columns = tile_of(lax.rem(index, 6))
-        value = plain_dot(drows[0, lines, :], weights[quarter, 1, :, columns])
+        value = plain_dot(drows[lines, :], weights[quarter, 1, :, columns])
         dpre[quarter, lines, columns] = (value * slope[quarter, lines, columns]).astype(jnp.bfloat16)
         return carry
 
@@ -1241,43 +1306,15 @@
     keep = pltpu.make_async_copy(backs.at[0], returns.at[me], local.at[3])
     keep.start()
 
-    def add_grads(given, down, act, first):
-        drows_t[...] = drows[down].T
-        if not first:
-            rows_t[...] = given.T
-
-        def step(index, carry):
-            columns = pl.ds(pl.multiple_of(index * 256, 256), 256)
-            inner = plain_dot(rows_t[...], (dpre.at[0] if first else dpre_set)[:, columns])
-            outer = plain_dot(drows_t[...], act[:, columns])
-            if first:
-                kept[0, :, columns] = inner
-                kept[1, :, columns] = outer
-            else:
-                kept[0, :, columns] = kept[0, :, columns] + inner
-                kept[1, :, columns] = kept[1, :, columns] + outer
-            return carry
-
-        lax.fori_loop(0, 3, step, 0)
-
-    def add_set(given, down):
-        def step(index, carry):
-            lines, columns = tile_of(index)
-            grown, rate = gelu_both(plain_dot(given[lines, :], weights[0, 0, :, columns]))
-            act_set[lines, columns] = grown
-            value = plain_dot(drows[down, lines, :], weights[0, 1, :, columns])
-            dpre_set[lines, columns] = (value * rate).astype(jnp.bfloat16)
-            return carry
-
-        lax.fori_loop(0, 6, step, 0)
-        add_grads(given[...], down, act_set, False)
-
-    add_grads(None, 0, act_own, True)
-    for copy in (moves[0], moves[1], moves[3]):
+    rows_t[...] = rows[...].T
+    drows_t[...] = drows[...].T
+    quarter_grads(kept, rows_t, drows_t, dpre.at[0], act_own, True)
+    for copy in (moves[0], moves[3]):
         copy.wait_recv()
-    add_set(rows_far.at[0], 2)
+    quarter_set(kept, weights.at[0], rows_far, drows_far, act_set, dpre_set, rows_t, drows_t)
+    staged.give(4)
     moves[2].wait_recv()
-    moves.append(remote(drows.at[1], drows.at[3], set_sems, 4, other))
+    moves.append(remote(drows_y, drows_last, set_sems, 4, other))
     moves[4].start()
     keep.wait()
     deal(backs, returns, (back_send, back_recv), False, 1, GROUP, wait_recv)
@@ -1285,16 +1322,10 @@
     slot = iota((count, TOTAL), 1)
     placing = (slot == target_column[:, 0:1]) | (slot == target_column[:, 1:2])
     dhidden[...] = plain_dot(placing.astype(jnp.bfloat16), dreturned[...])
-    add_set(rows_y, 1)
+    staged.give(3)
+    moves[1].wait_recv()
     moves[4].wait_recv()
-    add_set(rows_far.at[1], 3)
-    staged.give(4)
-    squared[...] = jnp.zeros_like(squared)
-    for which in range(2):
-        square = kept[which] * kept[which]
-        lines = jnp.broadcast_to(jnp.sum(square, axis=1, keepdims=True), (D, LANES)).T
-        squared[which : which + 1, :] = lines[0:1]
-        squared[2 + which : 3 + which, :] = jnp.sum(square, axis=0, keepdims=True)
+    staged.give(5, 6, 7)
     deal(sends, lands, (forth_send, forth_recv), True, 1, GROUP, wait_send)
     deal(backs, returns, (back_send, back_recv), False, 1, GROUP, wait_send)
     for copy in far + moves:
@@ -1307,7 +1338,7 @@
     wire = pltpu.VMEM((GROUP, SLOTS, WIRE), low)
     shapes = [
         ((count, D), wide), ((count, LANES), low), ((PAD, D), wide),
-        ((count, D), wide), ((2, D, D), wide), ((PAD, D), wide),
+        ((count, D), wide), ((2, D, D), wide), ((TOTAL, D), low), ((TOTAL, D), low), ((TOTAL, D), low),
     ]
     sems = pltpu.SemaphoreType.DMA
     return staged_call(
@@ -1317,8 +1348,7 @@
         [pltpu.VMEM((4, 2, D, D), low)]
         + [wire] * 4
         + [pltpu.VMEM((4, TOTAL, D), wide), pltpu.VMEM((4, TOTAL, D), low)]
-        + [pltpu.VMEM((TOTAL, D), low)] * 3
-        + [pltpu.VMEM((2, TOTAL, D), low), pltpu.VMEM((4, TOTAL, D), low)]
+        + [pltpu.VMEM((TOTAL, D), low)] * 6
         + [pltpu.VMEM((TOTAL, D), wide), pltpu.VMEM((TOTAL, D), low)]
         + [pltpu.VMEM((D, TOTAL), low)] * 2
         + [pltpu.VMEM((2, count, D), low)]
@@ -1327,20 +1357,12 @@
         + [sems((5,))] * 2
         + [sems((4,))],
         (1, 2, 5, 6, 7),
-        (4,),
+        (0, 3, 4, 5, 6, 7),
         raw=(11, 12, 13),
         collective_id=8,
-        megabytes=53,
+        megabytes=57,
         name="experts_backward",
     )
-
-
-NEAR = tuple((y, core) for y in range(4) for core in range(2) if y or core)
-PLANE = tuple((x, z) for x in range(4) for z in range(4) if x or z)
-
-
-def near_peer(at, by):
-    return moved(moved(at, "y", by[0]), "core", by[1])
 
 
 def plane_peer(at, by):
@@ -1462,6 +1484,146 @@
     )
 
 
+def follow(old, square):
+    return DECAY * old + (1.0 - DECAY) * (square + EPS_SQ)
+
+
+def update_kernel(
+    part_one, part_two, part_three, totals, head_grad, table_grad, table_squared, expert_cols_squared, expert_grad,
+    squares, router, table, head, vectors, experts,
+    square_rows, square_cols, router_rows, router_cols, table_rows, table_cols, head_rows, head_cols,
+    expert_rows, expert_cols, moment,
+    loss, norm, square_clip, square_rows_next, square_cols_next, square_next,
+    router_clip, router_rows_next, router_cols_next, router_next,
+    table_clip, table_rows_next, table_cols_next, table_next,
+    head_clip, head_rows_next, head_cols_next, head_next,
+    expert_clip, expert_rows_next, expert_cols_next, expert_next,
+    vector_clip, moment_next, vector_next,
+    turned, scale_ref, column_ref, line_ref,
+):
+    step = pl.program_id(0)
+
+    def stand(line):
+        count = line.shape[1]
+        column_ref[...] = jnp.zeros_like(column_ref)
+        column_ref[0:1, :count] = line
+        return column_ref[...].T[:count, 0:1]
+
+    def lie(column):
+        count = column.shape[0]
+        line_ref[...] = jnp.zeros_like(line_ref)
+        line_ref[:count, :] = jnp.broadcast_to(column, (count, LANES))
+        return line_ref[...].T[0:1, :count]
+
+    expert_rates = (0.3 / math.sqrt(D), 4.8 / math.sqrt(FF))
+
+    def total(value):
+        return jnp.sum(jnp.sum(value, axis=1, keepdims=True), axis=0, keepdims=True)
+
+    @pl.when(step == 0)
+    def _():
+        size = jnp.sqrt(total(totals[:7, :]) + totals[7:8, 1:2])
+        clip = jnp.minimum(1.0, CLIP_NORM / size)
+        clip_sq = clip * clip
+        loss[...] = totals[7:8, 0:1]
+        norm[...] = size
+        scale_ref[...] = jnp.broadcast_to(clip, scale_ref.shape)
+        rows = squares.shape[1]
+        parts = (part_one, part_two, part_three)
+        for k in range(5):
+            grad = parts[k // 2][PAD * (k % 2) : PAD * (k % 2) + rows, :]
+            near = follow(stand(square_rows[k : k + 1, :]), clip_sq * jnp.mean(grad * grad, axis=1, keepdims=True))
+            far = follow(square_cols[k : k + 1, :], clip_sq * totals[k : k + 1, :] / D)
+            middle = jnp.mean(totals[k : k + 1, :], axis=1, keepdims=True)
+            middle = follow(totals[7:8, 2 + k : 3 + k] / D, clip_sq * middle / D)
+            square_rows_next[k : k + 1, :] = lie(near)
+            square_cols_next[k : k + 1, :] = far
+            square_clip[k] = clip * grad
+            rate = (4.0 if k == 4 else 1.0) * (0.3 / math.sqrt(D))
+            square_next[k] = squares[k] - rate * (clip * grad) * lax.rsqrt(near * far / middle)
+        tail = part_three[PAD : PAD + rows, EXTRA:]
+        grad = tail[:, 32:64]
+        near = follow(stand(router_rows[...][None]), clip_sq * jnp.mean(grad * grad, axis=1, keepdims=True))
+        squared = totals[6:7, EXTRA + 32 : EXTRA + 64]
+        far = follow(router_cols[...][None], clip_sq * squared / D)
+        middle = jnp.sum(squared, axis=1, keepdims=True) / GROUP
+        middle = follow(totals[7:8, 7:8] / D, clip_sq * middle / D)
+        router_rows_next[...] = lie(near)[0]
+        router_cols_next[...] = far[0]
+        router_clip[...] = clip * grad
+        router_next[...] = router[...] - (0.2 / math.sqrt(D)) * (clip * grad) * lax.rsqrt(near * far / middle)
+        grad = table_grad[...]
+        near = follow(table_rows[...][None], clip_sq * table_squared[...] / D)
+        far = follow(stand(table_cols[...][None]), clip_sq * jnp.mean(grad * grad, axis=1, keepdims=True))
+        middle = jnp.mean(near, axis=1, keepdims=True)
+        table_rows_next[...] = near[0]
+        table_cols_next[...] = lie(far)[0]
+        table_clip[...] = clip * grad
+        table_next[...] = table[...] - 0.15 * (clip * grad) * lax.rsqrt(near * far / middle)
+        classes = head.shape[0]
+        grad = head_grad[:classes, :]
+        near = follow(head_rows[...][None], clip_sq * totals[5:6, :] / (classes * 4 * GROUP))
+        far = follow(stand(head_cols[...][None]), clip_sq * jnp.mean(grad * grad, axis=1, keepdims=True))
+        middle = jnp.mean(near, axis=1, keepdims=True)
+        head_rows_next[...] = near[0]
+        head_cols_next[...] = lie(far)[0]
+        head_clip[...] = clip * grad
+        head_next[...] = head[...] - (0.5 / math.sqrt(D)) * (clip * grad) * lax.rsqrt(near * far / middle)
+        grad = clip * tail[:, 96:106]
+        state = follow(moment[...], grad * grad)
+        vector_clip[...] = grad
+        moment_next[...] = state
+        vector_next[...] = vectors[...] - 0.3 * grad * lax.rsqrt(state)
+        near = follow(expert_rows[...], clip_sq * totals[PAD : PAD + 2, :] / FF)
+        far = follow(expert_cols[...], clip_sq * expert_cols_squared[...] / D)
+        middle = jnp.mean(near, axis=1, keepdims=True)
+        expert_rows_next[...] = near
+        expert_cols_next[...] = far
+        for which in range(2):
+            ratio = near[which : which + 1, :] / middle[which : which + 1, :]
+            turned[which] = jnp.broadcast_to(ratio, (LANES, D)).T
+
+    lines = expert_grad.shape[1]
+    steps = D // lines
+    which = lax.div(step, steps)
+    column = turned[which, pl.ds(pl.multiple_of(lax.rem(step, steps) * lines, lines), lines), 0:1]
+    row = expert_cols_next[pl.ds(which, 1), :]
+    clipped = scale_ref[0:1, 0:1] * expert_grad[0]
+    rate = jnp.where(which == 0, expert_rates[0], expert_rates[1])
+    expert_clip[0] = clipped
+    expert_next[0] = experts[0] - rate * clipped * lax.rsqrt(column * row)
+
+
+def update_all(*operands):
+    lines = 256
+    wide = jnp.float32
+    squares, router, table, head, vectors = (operands[index].shape for index in range(9, 14))
+    rows = squares[1]
+    expert = operands[14].shape
+    shapes = [
+        (1, 1), (1, 1), squares, (5, rows), (5, D), squares, router, (rows,), (GROUP,), router,
+        table, (PATCHES,), (rows,), table, head, (D,), (head[0],), head,
+        expert, (2, D), (2, D), expert, vectors, vectors, vectors,
+    ]
+
+    def spec(shape, streamed):
+        if streamed:
+            return pl.BlockSpec((1, lines, D), lambda step: (step // (D // lines), step % (D // lines), 0))
+        return pl.BlockSpec(shape, lambda step: (0,) * len(shape))
+
+    return pl.pallas_call(
+        update_kernel,
+        grid=(2 * D // lines,),
+        out_shape=[jax.ShapeDtypeStruct(shape, wide) for shape in shapes],
+        in_specs=[spec(value.shape, index in (8, 14)) for index, value in enumerate(operands)],
+        out_specs=[spec(shape, index in (18, 21)) for index, shape in enumerate(shapes)],
+        scratch_shapes=[pltpu.VMEM((2, D, LANES), wide), pltpu.VMEM((PAD, LANES), wide)]
+        + [pltpu.VMEM((LANES, 2 * LANES), wide), pltpu.VMEM((2 * LANES, LANES), wide)],
+        compiler_params=pltpu.CompilerParams(vmem_limit_bytes=32 * 2**20),
+        name="update_all",
+    )(*(pin(value) for value in operands))
+
+
 def across_cores(value):
     return lax.ppermute(value, "rep", CORE_SWAP)
 
@@ -1520,25 +1682,28 @@
     live = jnp.arange(labels.shape[2], dtype=jnp.int32) < label_count[:, :, None]
     live_labels = jnp.where(live, labels, -1).reshape(2 * num_exp, -1)
 
+    counted = image_count.reshape(1, 1)
+    extra, live_labels, counted = lax.optimization_barrier((extra, live_labels, counted))
+
     wide_ids = jnp.pad(expert_ids.reshape(2, block, num_top), ((0, 0), (0, 0), (0, LANES - num_top)))
-    *squares, extra, low, patch_rows, ids, quarter = gather_all(
+    *squares, extra, low, patch_rows, ids, quarter, quarter_in, across_part = gather_all(
         square_weights, extra, patches.reshape(2, block, width), wide_ids, expert_weights[0]
     )
     patch_rows, ids = patch_rows.reshape(rows, width), ids.reshape(rows, LANES)
 
-    across_in = across_y(quarter[0])
+    across_in = across_y(quarter_in)
     (
         embed, hidden_one, query, keys, values, mixed, after_attn, hidden_two,
         gate_probs, gates, lse, vectors, router, target, target_t, hidden_kept, *squares,
     ) = attend(patch_rows, squares, extra, low, ids)
     across_in, hidden_two = lax.optimization_barrier((across_in, hidden_two))
     received, received_y, chosen, after_moe, pool, across_out = experts_forward(
-        hidden_two, target_t, target, gates, after_attn, vectors, quarter, across_in
+        hidden_two, target_t, target, gates, after_attn, vectors, quarter, across_in, across_part
     )
     row_grad, head_g, loss_part = head_step(
-        pool, head_weight.T, live_labels, image_count.reshape(1, 1)
-    )
-    dmoe_in, dgate_logits, final_sums, dhidden, expert_g, expert_squared = experts_backward(
+        pool, head_weight.T, live_labels, counted
+    )
+    dmoe_in, dgate_logits, final_sums, dhidden, part_g, received_last, down_y, down_last = experts_backward(
         row_grad, after_moe, chosen, gates, gate_probs, ids, received, received_y,
         target_t, target, vectors, quarter, across_in, across_out,
     )
@@ -1556,129 +1721,37 @@
         vectors,
         router,
     )
-    *owned, totals = shared_gradients(
+    *owned, totals, expert_g, expert_colsq = shared_gradients(
         patch_rows, hidden_one, mixed, dembed_low, dquery_low, dkey_low, dvalue_low, dafter_low,
-        hidden_kept, dgate_logits, sums, final_sums, head_g, expert_squared, loss_part, square_rows, router_rows[None],
-    )
-    head_g = head_g[:vocab_dev].T
-    expert_g = expert_g[None]
-    owned = [half for part in owned for half in (part[:own_rows], part[PAD : PAD + own_rows])]
-    square_g = jnp.stack(owned[:5])
-    extra_g = owned[5]
+        hidden_kept, dgate_logits, sums, final_sums, head_g, loss_part, square_rows, router_rows[None],
+        part_g, quarter, received_y, received_last, down_y, down_last,
+    )
     second = 3 * LANES
-    few_at = EXTRA + num_expert
-    vector_at = EXTRA + 96
 
     def positions(value):
         return jnp.concatenate(
             [value[:, start : start + block] for start in (0, second, block, second + block)], axis=1
         )
 
-    table_g = positions(extra_g).T
-    router_g = extra_g[:, few_at : few_at + num_expert]
-    vector_g = extra_g[:, vector_at : vector_at + 10].T
-    square_rowmean = jnp.mean(square_g * square_g, axis=2)
-    router_rowmean = jnp.mean(router_g * router_g, axis=1)
-    loss_total = totals[7, 0]
-    norm_total = jnp.sum(totals[:7]) + totals[7, 1]
-    square_colsq = totals[:5]
-    square_rows_sum = totals[7, 2:7]
-    square_mean_sum = jnp.mean(square_colsq, axis=1)
-    router_colsq = totals[6, few_at : few_at + num_expert]
-    router_rows_sum = totals[7, 7]
-    router_mean_sum = jnp.sum(router_colsq) / num_expert
-    table_rowsq = positions(totals[6:7])[0]
-    head_rowsq = totals[5]
-    expert_mine = totals[8:10][None]
-    expert_colmean = (expert_squared[2:4] / width)[None]
-    grad_norm = jnp.sqrt(norm_total)
-    clip = jnp.minimum(1.0, CLIP_NORM / grad_norm)
-    clip_sq = clip * clip
-    keep = 1.0 - DECAY
-    square_clip = clip * square_g
-    square_rows_next = DECAY * square_rows + keep * (clip_sq * square_rowmean + EPS_SQ)
-    square_cols_next = DECAY * square_cols + keep * (clip_sq * square_colsq / width + EPS_SQ)
-    square_mean = (
-        DECAY * square_rows_sum + keep * (clip_sq * square_mean_sum + width * EPS_SQ)
-    ) / width
-    square_rate = jnp.array([1.0, 1.0, 1.0, 1.0, 4.0], jnp.float32)[:, None, None] * (
-        0.3 / math.sqrt(D)
-    )
-    square_next = factored_step(
-        square_weights,
-        square_clip,
-        square_rows_next,
-        square_cols_next,
-        square_mean[:, None, None],
-        square_rate,
-    )
-    router_clip = clip * router_g
-    router_rows_next = DECAY * router_rows + keep * (clip_sq * router_rowmean + EPS_SQ)
-    router_cols_next = DECAY * router_cols + keep * (clip_sq * router_colsq / width + EPS_SQ)
-    router_mean = (
-        DECAY * router_rows_sum + keep * (clip_sq * router_mean_sum + width * EPS_SQ)
-    ) / width
-    router_next = factored_step(
-        router_weight,
-        router_clip,
-        router_rows_next,
-        router_cols_next,
-        router_mean,
-        0.2 / math.sqrt(D),
-    )
-    table_clip = clip * table_g
-    table_rows_next = DECAY * position_rows + keep * (clip_sq * table_rowsq / width + EPS_SQ)
-    table_cols_next = DECAY * position_cols + keep * (
-        clip_sq * jnp.mean(table_g * table_g, axis=0) + EPS_SQ
-    )
-    table_next = factored_step(
-        position_table,
-        table_clip,
-        table_rows_next,
-        table_cols_next,
-        jnp.mean(table_rows_next),
-        0.15,
-    )
-    head_clip = clip * head_g
-    head_rows_next = DECAY * head_rows + keep * (
-        clip_sq * head_rowsq / (vocab_dev * num_rep * num_exp) + EPS_SQ
-    )
-    head_cols_next = DECAY * head_cols + keep * (
-        clip_sq * jnp.mean(head_g * head_g, axis=0) + EPS_SQ
-    )
-    head_next = factored_step(
-        head_weight,
-        head_clip,
-        head_rows_next,
-        head_cols_next,
-        jnp.mean(head_rows_next),
-        0.5 / math.sqrt(D),
-    )
-    expert_clip = clip * expert_g
-    expert_rows_next = DECAY * expert_rows + keep * (
-        clip_sq * expert_mine / (ff_dev * num_rep) + EPS_SQ
-    )
-    expert_cols_next = DECAY * expert_cols + keep * (
-        clip_sq * expert_colmean + EPS_SQ
-    )
-    expert_rate = jnp.array([0.3 / math.sqrt(D), 4.8 / math.sqrt(FF)], jnp.float32)[
-        None, :, None, None
-    ]
-    expert_next = factored_step(
-        expert_weights,
-        expert_clip,
-        expert_rows_next,
-        expert_cols_next,
-        jnp.mean(expert_rows_next, axis=-1)[..., None, None],
-        expert_rate,
-    )
-    vector_clip = clip * vector_g
-    moment_next = DECAY * vector_moment + keep * (vector_clip * vector_clip + EPS_SQ)
-    vector_next = vector_params - 0.3 * vector_clip * lax.rsqrt(moment_next)
+    (
+        loss_total, grad_norm, square_clip, square_rows_next, square_cols_next, square_next,
+        router_clip, router_rows_next, router_cols_next, router_next,
+        table_clip, table_rows_next, table_cols_next, table_next,
+        head_clip, head_rows_next, head_cols_next, head_next,
+        expert_clip, expert_rows_next, expert_cols_next, expert_next,
+        vector_clip, moment_next, vector_next,
+    ) = update_all(
+        *owned, totals, head_g, positions(owned[2][PAD : PAD + own_rows]), positions(totals[6:7]),
+        expert_colsq, expert_g,
+        square_weights, router_weight, position_table.T, head_weight.T, vector_params.T, expert_weights[0],
+        square_rows, square_cols, router_rows, router_cols, position_rows,
+        position_cols, head_rows, head_cols, expert_rows[0], expert_cols[0],
+        vector_moment.T,
+    )
     return (
-        loss_total,
+        loss_total[0, 0],
         image_count,
-        grad_norm,
+        grad_norm[0, 0],
         square_clip,
         square_rows_next,
         square_cols_next,
@@ -1687,21 +1760,21 @@
         router_rows_next,
         router_cols_next,
         router_next,
-        table_clip,
+        table_clip.T,
         table_rows_next,
         table_cols_next,
-        table_next,
-        head_clip,
+        table_next.T,
+        head_clip.T,
         head_rows_next,
         head_cols_next,
-        head_next,
-        expert_clip,
-        expert_rows_next,
-        expert_cols_next,
-        expert_next,
-        vector_clip,
-        moment_next,
-        vector_next,
+        head_next.T,
+        expert_clip[None],
+        expert_rows_next[None],
+        expert_cols_next[None],
+        expert_next[None],
+        vector_clip.T,
+        moment_next.T,
+        vector_next.T,
     )
 
 

time: 379 us -> 357 us (0.942)
  other arithmetic: 16.3 us -> 3.46 us
  between operations: 6.74 us -> 1.31 us
    pallas_call x6, Pallas kernels: 286 us -> 274 us  [staged_call(): pl.pallas_call(kernel, out_shape=[pltpu.HBM(*shape) if index in far_out +...]
    pallas_call x0 -> x1, Pallas kernels: none -> 12 us  [update_all(): pl.pallas_call(update_kernel, grid=(2 * D // lines,), out_shape=[jax.Shap...]
    sub x6 -> x0, other arithmetic: 6.77 us -> none  [the longest x5 6.09 us: factored_step(): return weight - rate * clipped * lax.rsqrt(estimate)]
    mul x3 -> x0, other arithmetic: 5.32 us -> none  [the longest x1 5.2 us: shards(): expert_clip = clip * expert_g]
  transfers between devices with their start and end apart: 1 -> 1, of which waited for: 1 -> 1; matrix products, arithmetic and copies ran while one was open for 0% -> 0% of each run, Pallas kernels for 5% -> 6%
where the time goes in v4:
time: 357 us; the launch traced here: 353 us
  Pallas kernels  335 us (94%)
  local copies, waits for them, and re-layouts  9.03 us (3%)
    pallas_call x6, Pallas kernels, staged_call(): pl.pallas_call(kernel, out_shape=[pltpu.HBM(*shape) if index in far_out +...  274 us
    pallas_call x1, Pallas kernels, gather_all(): pl.pallas_call(gather_kernel, out_shape=[jax.ShapeDtypeStruct((D, D), jnp...  49.2 us
    pallas_call x1, Pallas kernels, update_all(): pl.pallas_call(update_kernel, grid=(2 * D // lines,), out_shape=[jax.Shap...  12 us
  transfers between devices with their start and end apart: 1, of which 1 were waited for; matrix products, arithmetic and copies ran while one was open for 0% of the time, Pallas kernels for 6%

profile of v4, /device:TPU:1, one launch (start us, length us, event | category | flops | bytes accessed | tf_op | source)
XLA Modules:
  0.0 352.7 jit_solution(379985609742646192)
XLA Ops:
  0.7 1.3 fusion.1
  2.0 0.8 concatenate.9
  2.8 0.8 fusion
  3.6 0.8 copy.47
  4.5 0.7 pad.9.ids
  5.1 0.0 copy-start.3
  5.2 0.9 copy-done.3
  6.1 49.2 %gather_weights.1 = (bf16[768,768]{1,0:T(8,128)(2,1)S(1)}, bf16[768,768]{1,0:T(8,128)(2,1)S(1)}, bf16[768,768]{1,0:T(8,128)(2,1)S(1)}, bf16[768,768]{1,0:T(8,128...) custom-call(f32[5,6,768]{2,1,0:T(8,128)S(1)} %copy-done.3, ...), custom_call_target="tpu_custom_call" | custom-call | tf_op jit(solution)/shard_map/gather_weights/pallas_call | solution.py:331
  55.2 1.5 collective-permute-start
  56.7 22.9 %attend.1 = (f32[288,768]{1,0:T(8,128)}, bf16[288,768]{1,0:T(8,128)(2,1)}, bf16[288,768]{1,0:T(8,128)(2,1)}, bf16[2,288,768]{2,1,0:T(8,128)(2,1)}, bf16[2,288,76...) custom-call(bf16[288,768]{1,0:T(8,128)(2,1)} %bitcast.32, ...), custom_call_target="tpu_custom_call" | custom-call | tf_op jit(solution)/shard_map/attend/pallas_call | solution.py:149
  79.6 0.0 copy-start.1
  79.6 0.0 copy-start.2
  79.6 0.0 copy-start.4
  79.6 0.0 copy-start.7
  79.6 0.0 copy-start.8
  79.6 2.7 collective-permute-done.refs_7_.refs_12_
  82.3 0.0 copy-start.11
  82.3 1.0 copy-done.11
  83.3 69.4 %experts_forward.1 = (bf16[640,768]{1,0:T(8,128)(2,1)}, bf16[640,768]{1,0:T(8,128)(2,1)}, bf16[2,288,768]{2,1,0:T(8,128)(2,1)}, f32[288,768]{1,0:T(8,128)}, f32[...) custom-call(bf16[288,768]{1,0:T(8,128)(2,1)S(1)} %get-tuple-element.131.refs_0_, ...), custom_call_target="tpu_custom_call" | custom-call | tf_op jit(solution)/shard_map/experts_forward/pallas_call | solution.py:149
  152.7 0.0 copy-done.1
  152.7 0.0 copy-done.2
  152.7 0.0 copy-done.4
  152.7 0.0 copy-done.7
  152.7 0.0 copy-done.8
  152.8 31.4 %head_step.1 = (f32[8,128]{1,0:T(8,128)S(1)}, f32[256,768]{1,0:T(8,128)S(1)}, f32[1,1]{1,0:T(1,128)}) custom-call(f32[8,128]{1,0:T(8,128)S(1)} %get-tuple-element.140.refs_0_, f32[171,768]{1,0:T(8,128)} %bitcast.30, s32[64,64]{1,0:T(8,128)S(1)} %bitcast.27, f32[1,1]{1,0:T(1,128)} %bitcast.3.refs_3_), custom_call_target="tpu_custom_call" | custom-call | tf_op jit(solution)/shard_map/head_step/pallas_call | solution.py:149
  184.1 0.0 copy-start
  184.1 0.9 copy-done
  185.1 0.0 copy-start.10
  185.1 0.6 copy-done.10
  185.7 0.0 copy-start.5
  185.7 63.7 %experts_backward.1 = (f32[288,768]{1,0:T(8,128)}, bf16[288,128]{1,0:T(8,128)(2,1)}, f32[8,768]{1,0:T(8,128)}, f32[288,768]{1,0:T(8,128)}, f32[2,768,768]{2,1,0:...) custom-call(f32[8,128]{1,0:T(8,128)} %copy-done.10, ...), custom_call_target="tpu_custom_call" | custom-call | tf_op jit(solution)/shard_map/experts_backward/pallas_call | solution.py:149
  249.4 0.0 copy-done.5
  249.4 0.0 copy-start.6
  249.4 0.9 copy-done.6
  250.3 20.7 %attend_back.1 = (bf16[288,768]{1,0:T(8,128)(2,1)}, bf16[288,768]{1,0:T(8,128)(2,1)}, bf16[288,768]{1,0:T(8,128)(2,1)}, bf16[288,768]{1,0:T(8,128)(2,1)}, bf16[2...) custom-call(f32[288,768]{1,0:T(8,128)} %get-tuple-element.150.refs_0_, f32[288,768]{1,0:T(8,128)} %get-tuple-element.151.refs_1_, ...), custom_call_target="tpu_custom_call" | custom-call | tf_op jit(solution)/shard_map/attend_back/pallas_call | solution.py:149
  271.0 0.0 copy-start.9
  271.0 0.6 copy-done.9
  271.6 65.6 %shared_gradients.1 = (f32[16,768]{1,0:T(8,128)}, f32[16,768]{1,0:T(8,128)}, f32[16,768]{1,0:T(8,128)}, f32[16,768]{1,0:T(8,128)}, f32[2,768,768]{2,1,0:T(8,128)}, /*index=5*/f32[2,768]{1,0:T(2,128)}) custom-call(bf16[288,768]{1,0:T(8,128)(2,1)} %bitcast.33, bf16[288,768]{1,0:T(8,128)(2,1)} %get-tuple-element.127.refs_1_, ...), custom_call_target="tpu_custom_call" | custom-call | tf_op jit(solution)/shard_map/shared_gradients/pallas_call | solution.py:149
  337.2 0.9 fusion.2
  338.0 0.9 fusion.3
  338.9 0.7 pad_maximum_fusion.1.table_squared
  339.6 0.7 pad_maximum_fusion.table_grad
  340.2 12.0 %update_all.1 = (f32[1,1]{1,0:T(1,128)}, f32[1,1]{1,0:T(1,128)}, f32[5,6,768]{2,1,0:T(8,128)}, f32[5,6]{1,0:T(8,128)}, f32[5,768]{1,0:T(8,128)}, /*index=5*/f32[...) custom-call(f32[16,768]{1,0:T(8,128)} %get-tuple-element.177.part_on, ...), custom_call_target="tpu_custom_call" | custom-call | tf_op jit(solution)/shard_map/update_all/pallas_call | solution.py:1614
  (2 shorter events, 0.0 us)
Async XLA Ops:
  5.1 0.9 copy-start.3
  55.2 27.1 %collective-permute-start = (bf16[768,768]{1,0:T(8,128)(2,1)}, bf16[768,768]{1,0:T(8,128)(2,1)S(1)}, u32[]{:S(2)}, u32[]{:S(2)}) collective-permute-start(bf16[768,768]{1,0:T(8,128)(2,1)} %get-tuple-element.129), channel_id=1, source_target_pairs={{0,64},{32,96},{64,0},{96,32},{1,65},{33,97},{65,1},{97,33},{2,66}... | collective-permute-start | bytes 3538952 | tf_op jit(solution)/shard_map/ppermute | solution.py:1632
  79.6 73.1 %copy-start.1 = (f32[288,128]{1,0:T(8,128)}, f32[288,128]{1,0:T(8,128)S(1)}, u32[]{:S(2)}) copy-start(f32[288,128]{1,0:T(8,128)S(1)} %get-tuple-element.134.refs_3_) | copy-start | bytes 442372
  79.6 73.1 %copy-start.2 = (s32[288,128]{1,0:T(8,128)}, s32[288,128]{1,0:T(8,128)S(1)}, u32[]{:S(2)}) copy-start(s32[288,128]{1,0:T(8,128)S(1)} %get-tuple-element.133.refs_2_.refs_9_) | copy-start | bytes 442372
  79.6 73.1 %copy-start.4 = (f32[16,768]{1,0:T(8,128)}, f32[16,768]{1,0:T(8,128)S(1)}, u32[]{:S(2)}) copy-start(f32[16,768]{1,0:T(8,128)S(1)} %get-tuple-element.136.refs_5_.refs_10_.refs_13_) | copy-start | bytes 147460
  79.6 73.1 %copy-start.7 = (f32[288,128]{1,0:T(8,128)}, f32[288,128]{1,0:T(8,128)S(1)}, u32[]{:S(2)}) copy-start(f32[288,128]{1,0:T(8,128)S(1)} %get-tuple-element.146.refs_4_) | copy-start | bytes 442372
  79.6 73.1 %copy-start.8 = (s32[8,288]{1,0:T(8,128)}, s32[8,288]{1,0:T(8,128)S(1)}, u32[]{:S(2)}) copy-start(s32[8,288]{1,0:T(8,128)S(1)} %get-tuple-element.132.refs_1_.refs_8_) | copy-start | bytes 27652
  82.3 1.0 copy-start.11
  184.1 1.0 copy-start
  185.1 0.6 copy-start.10
  185.7 63.7 %copy-start.5 = (f32[16,768]{1,0:T(8,128)S(1)}, f32[16,768]{1,0:T(8,128)}, u32[]{:S(2)}) copy-start(f32[16,768]{1,0:T(8,128)} %copy-done.4) | copy-start | bytes 147460
  249.4 0.9 copy-start.6
  271.0 0.6 copy-start.9

commit v5 on v4

--- a/solution.py
+++ b/solution.py
@@ -1074,32 +1074,36 @@
             for copy in far:
                 copy.wait_recv()
         given = halves(rows, half)
+        lines = pl.ds(half * HALF, HALF)
 
         def hidden_units(index, carry):
             quarter, part = lax.div(index, 3), lax.rem(index, 3)
             columns = pl.ds(pl.multiple_of(part * 256, 256), 256)
             value = plain_dot(given, weights[quarter, 0, :, columns])
-            act[quarter, :, columns] = (0.5 * value * (1.0 + gelu_tanh(value))).astype(jnp.bfloat16)
+            act[quarter, lines, columns] = (0.5 * value * (1.0 + gelu_tanh(value))).astype(jnp.bfloat16)
             return carry
 
         lax.fori_loop(0, 12, hidden_units, 0)
-        if half == 0:
-            trade.wait_recv()
-            pass_on.start()
-            save.start()
-            pass_on.wait_recv()
+    trade.wait_recv()
+    pass_on.start()
+    save.start()
+    pass_on.wait_recv()
+    for half in range(2):
+        sources = pl.ds(half * (GROUP // 2), GROUP // 2)
+        lines = pl.ds(half * HALF, HALF)
 
         def outputs(index, carry):
             columns = pl.ds(pl.multiple_of(index * 256, 256), 256)
-            value = over_last(act[0], weights[0, 1, columns, :])
+            value = over_last(act[0, lines, :], weights[0, 1, columns, :])
             for quarter in range(1, 4):
-                value = value + over_last(act[quarter], weights[quarter, 1, columns, :])
+                value = value + over_last(act[quarter, lines, :], weights[quarter, 1, columns, :])
             result[:, columns] = value
             return carry
 
         lax.fori_loop(0, 3, outputs, 0)
         pack(backs.at[sources], result[: MAIN // 2, :], result[MAIN // 2 :, :])
-        deal(backs, returns, (back_send, back_recv), False, max(1, half * (GROUP // 2)), (half + 1) * (GROUP // 2), start_copy)
+        low, high = max(1, half * (GROUP // 2)), (half + 1) * (GROUP // 2)
+        deal(backs, returns, (back_send, back_recv), False, low, high, start_copy)
     keep = pltpu.make_async_copy(backs.at[0], returns.at[me], local.at[2])
     keep.start()
     keep.wait()
@@ -1148,7 +1152,7 @@
         [((TOTAL, D), low), ((TOTAL, D), low), ((2, count, D), low), ((count, D), wide), ((PAD, LANES), wide), ((D, D), low)],
         [pltpu.VMEM((4, 2, D, D), low)]
         + [wire] * 4
-        + [pltpu.VMEM((4, HALF, D), low), pltpu.VMEM((HALF, D), wide), pltpu.VMEM((TOTAL, D), low)]
+        + [pltpu.VMEM((4, TOTAL, D), low), pltpu.VMEM((HALF, D), wide), pltpu.VMEM((TOTAL, D), low)]
         + [sems((GROUP,))] * 4
         + [sems((4,))] * 4
         + [sems((5,))],
@@ -1157,7 +1161,7 @@
         raw=(6, 7, 8),
         raw_out=(5,),
         collective_id=5,
-        megabytes=25,
+        megabytes=28,
         name="experts_forward",
     )
 
@@ -1595,7 +1599,7 @@
 
 
 def update_all(*operands):
-    lines = 256
+    lines = 384
     wide = jnp.float32
     squares, router, table, head, vectors = (operands[index].shape for index in range(9, 14))
     rows = squares[1]

time: 357 us -> 357 us (level)
  no operation moved by 1% of the time
where the time goes in v5:
time: 357 us; the launch traced here: 353 us
  Pallas kernels  335 us (94%)
  local copies, waits for them, and re-layouts  9.03 us (3%)
    pallas_call x6, Pallas kernels, staged_call(): pl.pallas_call(kernel, out_shape=[pltpu.HBM(*shape) if index in far_out +...  275 us
    pallas_call x1, Pallas kernels, gather_all(): pl.pallas_call(gather_kernel, out_shape=[jax.ShapeDtypeStruct((D, D), jnp...  49.2 us
    pallas_call x1, Pallas kernels, update_all(): pl.pallas_call(update_kernel, grid=(2 * D // lines,), out_shape=[jax.Shap...  11.2 us
  transfers between devices with their start and end apart: 1, of which 1 were waited for; matrix products, arithmetic and copies ran while one was open for 0% of the time, Pallas kernels for 6%

profile of v5, /device:TPU:1, one launch (start us, length us, event | category | flops | bytes accessed | tf_op | source)
XLA Modules:
  0.0 352.9 jit_solution(10992489817442937653)
XLA Ops:
  0.7 1.3 fusion.1
  2.0 0.8 concatenate.9
  2.8 0.8 fusion
  3.6 0.8 copy.47
  4.5 0.7 pad.9.ids
  5.1 0.0 copy-start.3
  5.2 0.9 copy-done.3
  6.1 49.2 %gather_weights.1 = (bf16[768,768]{1,0:T(8,128)(2,1)S(1)}, bf16[768,768]{1,0:T(8,128)(2,1)S(1)}, bf16[768,768]{1,0:T(8,128)(2,1)S(1)}, bf16[768,768]{1,0:T(8,128...) custom-call(f32[5,6,768]{2,1,0:T(8,128)S(1)} %copy-done.3, ...), custom_call_target="tpu_custom_call" | custom-call | tf_op jit(solution)/shard_map/gather_weights/pallas_call | solution.py:331
  55.2 1.5 collective-permute-start
  56.7 22.9 %attend.1 = (f32[288,768]{1,0:T(8,128)}, bf16[288,768]{1,0:T(8,128)(2,1)}, bf16[288,768]{1,0:T(8,128)(2,1)}, bf16[2,288,768]{2,1,0:T(8,128)(2,1)}, bf16[2,288,76...) custom-call(bf16[288,768]{1,0:T(8,128)(2,1)} %bitcast.32, ...), custom_call_target="tpu_custom_call" | custom-call | tf_op jit(solution)/shard_map/attend/pallas_call | solution.py:149
  79.6 0.0 copy-start.1
  79.6 0.0 copy-start.2
  79.6 0.0 copy-start.4
  79.6 0.0 copy-start.7
  79.6 0.0 copy-start.8
  79.6 2.7 collective-permute-done.refs_7_.refs_12_
  82.3 0.0 copy-start.11
  82.3 1.0 copy-done.11
  83.3 73.7 %experts_forward.1 = (bf16[640,768]{1,0:T(8,128)(2,1)}, bf16[640,768]{1,0:T(8,128)(2,1)}, bf16[2,288,768]{2,1,0:T(8,128)(2,1)}, f32[288,768]{1,0:T(8,128)}, f32[...) custom-call(bf16[288,768]{1,0:T(8,128)(2,1)S(1)} %get-tuple-element.131.refs_0_, ...), custom_call_target="tpu_custom_call" | custom-call | tf_op jit(solution)/shard_map/experts_forward/pallas_call | solution.py:149
  157.0 0.0 copy-done.1
  157.1 0.0 copy-done.2
  157.1 0.0 copy-done.4
  157.1 0.0 copy-done.7
  157.1 0.0 copy-done.8
  157.1 27.9 %head_step.1 = (f32[8,128]{1,0:T(8,128)S(1)}, f32[256,768]{1,0:T(8,128)S(1)}, f32[1,1]{1,0:T(1,128)}) custom-call(f32[8,128]{1,0:T(8,128)S(1)} %get-tuple-element.140.refs_0_, f32[171,768]{1,0:T(8,128)} %bitcast.30, s32[64,64]{1,0:T(8,128)S(1)} %bitcast.27, f32[1,1]{1,0:T(1,128)} %bitcast.3.refs_3_), custom_call_target="tpu_custom_call" | custom-call | tf_op jit(solution)/shard_map/head_step/pallas_call | solution.py:149
  185.1 0.0 copy-start
  185.1 0.9 copy-done
  186.0 0.0 copy-start.10
  186.0 0.6 copy-done.10
  186.6 0.0 copy-start.5
  186.6 63.8 %experts_backward.1 = (f32[288,768]{1,0:T(8,128)}, bf16[288,128]{1,0:T(8,128)(2,1)}, f32[8,768]{1,0:T(8,128)}, f32[288,768]{1,0:T(8,128)}, f32[2,768,768]{2,1,0:...) custom-call(f32[8,128]{1,0:T(8,128)} %copy-done.10, ...), custom_call_target="tpu_custom_call" | custom-call | tf_op jit(solution)/shard_map/experts_backward/pallas_call | solution.py:149
  250.5 0.0 copy-done.5
  250.5 0.0 copy-start.6
  250.5 0.9 copy-done.6
  251.3 20.6 %attend_back.1 = (bf16[288,768]{1,0:T(8,128)(2,1)}, bf16[288,768]{1,0:T(8,128)(2,1)}, bf16[288,768]{1,0:T(8,128)(2,1)}, bf16[288,768]{1,0:T(8,128)(2,1)}, bf16[2...) custom-call(f32[288,768]{1,0:T(8,128)} %get-tuple-element.150.refs_0_, f32[288,768]{1,0:T(8,128)} %get-tuple-element.151.refs_1_, ...), custom_call_target="tpu_custom_call" | custom-call | tf_op jit(solution)/shard_map/attend_back/pallas_call | solution.py:149
  272.0 0.0 copy-start.9
  272.0 0.6 copy-done.9
  272.6 65.6 %shared_gradients.1 = (f32[16,768]{1,0:T(8,128)}, f32[16,768]{1,0:T(8,128)}, f32[16,768]{1,0:T(8,128)}, f32[16,768]{1,0:T(8,128)}, f32[2,768,768]{2,1,0:T(8,128)}, /*index=5*/f32[2,768]{1,0:T(2,128)}) custom-call(bf16[288,768]{1,0:T(8,128)(2,1)} %bitcast.33, bf16[288,768]{1,0:T(8,128)(2,1)} %get-tuple-element.127.refs_1_, ...), custom_call_target="tpu_custom_call" | custom-call | tf_op jit(solution)/shard_map/shared_gradients/pallas_call | solution.py:149
  338.2 0.9 fusion.2
  339.0 0.9 fusion.3
  339.9 0.7 pad_maximum_fusion.1.table_squared
  340.6 0.7 pad_maximum_fusion.table_grad
  341.2 11.2 %update_all.1 = (f32[1,1]{1,0:T(1,128)}, f32[1,1]{1,0:T(1,128)}, f32[5,6,768]{2,1,0:T(8,128)}, f32[5,6]{1,0:T(8,128)}, f32[5,768]{1,0:T(8,128)}, /*index=5*/f32[...) custom-call(f32[16,768]{1,0:T(8,128)} %get-tuple-element.177.part_on, ...), custom_call_target="tpu_custom_call" | custom-call | tf_op jit(solution)/shard_map/update_all/pallas_call | solution.py:1618
  (2 shorter events, 0.0 us)
Async XLA Ops:
  5.1 0.9 copy-start.3
  55.2 27.1 %collective-permute-start = (bf16[768,768]{1,0:T(8,128)(2,1)}, bf16[768,768]{1,0:T(8,128)(2,1)S(1)}, u32[]{:S(2)}, u32[]{:S(2)}) collective-permute-start(bf16[768,768]{1,0:T(8,128)(2,1)} %get-tuple-element.129), channel_id=1, source_target_pairs={{0,64},{32,96},{64,0},{96,32},{1,65},{33,97},{65,1},{97,33},{2,66}... | collective-permute-start | bytes 3538952 | tf_op jit(solution)/shard_map/ppermute | solution.py:1636
  79.6 77.5 %copy-start.1 = (f32[288,128]{1,0:T(8,128)}, f32[288,128]{1,0:T(8,128)S(1)}, u32[]{:S(2)}) copy-start(f32[288,128]{1,0:T(8,128)S(1)} %get-tuple-element.134.refs_3_) | copy-start | bytes 442372
  79.6 77.5 %copy-start.2 = (s32[288,128]{1,0:T(8,128)}, s32[288,128]{1,0:T(8,128)S(1)}, u32[]{:S(2)}) copy-start(s32[288,128]{1,0:T(8,128)S(1)} %get-tuple-element.133.refs_2_.refs_9_) | copy-start | bytes 442372
  79.6 77.5 %copy-start.4 = (f32[16,768]{1,0:T(8,128)}, f32[16,768]{1,0:T(8,128)S(1)}, u32[]{:S(2)}) copy-start(f32[16,768]{1,0:T(8,128)S(1)} %get-tuple-element.136.refs_5_.refs_10_.refs_13_) | copy-start | bytes 147460
  79.6 77.5 %copy-start.7 = (f32[288,128]{1,0:T(8,128)}, f32[288,128]{1,0:T(8,128)S(1)}, u32[]{:S(2)}) copy-start(f32[288,128]{1,0:T(8,128)S(1)} %get-tuple-element.146.refs_4_) | copy-start | bytes 442372
  79.6 77.5 %copy-start.8 = (s32[8,288]{1,0:T(8,128)}, s32[8,288]{1,0:T(8,128)S(1)}, u32[]{:S(2)}) copy-start(s32[8,288]{1,0:T(8,128)S(1)} %get-tuple-element.132.refs_1_.refs_8_) | copy-start | bytes 27652
  82.3 1.0 copy-start.11
  185.1 1.0 copy-start
  186.0 0.6 copy-start.10
  186.6 63.9 %copy-start.5 = (f32[16,768]{1,0:T(8,128)S(1)}, f32[16,768]{1,0:T(8,128)}, u32[]{:S(2)}) copy-start(f32[16,768]{1,0:T(8,128)} %copy-done.4) | copy-start | bytes 147460
  250.5 0.9 copy-start.6
  272.0 0.6 copy-start.9
